TPU v7x, 32 devices: a whole 2x2x4 slice. The times are simulated.
32 devices in a mesh: node: 4 (over z), space: 8 (over y, x, core).
Axes of the slice: x: 2, y: 2, z: 4, core: 2. Of those that a mesh axis runs over, the one named last changes fastest.
Arguments:
- start_state: float32 [5, 4, 4, 4, 8, 1280], P(None, None, None, None, 'space'), may hold values from -1.5 to 14, as said below
- node_offset: float32 [4, 5, 4, 4, 4, 8, 1280], P('node', None, None, None, None, 'space'), may hold values from -0.6 to 0.6
Outputs:
- increments: float32 [4, 5, 4, 4, 4, 8, 1280], P('node', None, None, None, None, 'space')
Inputs may be any that keep to these rules, and one draw needn't show every extreme that they name: `start_state`: conserved variables of a gas with gamma 1.4, density and pressure between 2 and 5 and every velocity component within 0.3 in magnitude, drawn independently at each node.
All inputs are finite; a program needn't handle non-finite values.
Results may differ from a plain program's by a relative error of at most 0.0001.
Values sent between devices are 32-bit elements; how exact they have to be, the bound alone decides.
No kernel may reach another device: no remote copies, remote signals or barrier semaphores. Data moves between devices by JAX's collectives and lax.ppermute only.
A program may use at most 64 MiB of HBM per device.

v0:
```python
import functools
import math

import jax
import jax.numpy as jnp
import numpy as np
from jax import lax
from jax.experimental import pallas as pl
from jax.experimental.pallas import tpu as pltpu
from jax.sharding import PartitionSpec as P

EZ = 80
QUARTER = 320
TILES = 10
ITERS = 2
gamma_gas = 1.4
step_length = 0.01
VMEM_LIMIT = 48 * 1024 * 1024


def lobatto_derivative():
    points = np.array([-1.0, -math.sqrt(0.2), math.sqrt(0.2), 1.0])
    barycentric = np.ones(4)
    for i in range(4):
        for k in range(4):
            if k != i:
                barycentric[i] = barycentric[i] / (points[i] - points[k])
    derivative = np.zeros((4, 4))
    for i in range(4):
        for j in range(4):
            if i != j:
                derivative[i, j] = barycentric[j] / barycentric[i] / (points[i] - points[j])
        derivative[i, i] = -np.sum(derivative[i])
    return derivative


def collocation_matrix():
    near_root = math.sqrt(3.0 / 7 - 2.0 / 7 * math.sqrt(1.2))
    far_root = math.sqrt(3.0 / 7 + 2.0 / 7 * math.sqrt(1.2))
    time_nodes = [(1.0 + value) / 2 for value in (-far_root, -near_root, near_root, far_root)]
    quad_table = np.zeros((4, 4))
    for j in range(4):
        coeffs = [1.0]
        for k in range(4):
            if k != j:
                scale = 1.0 / (time_nodes[j] - time_nodes[k])
                widened = [0.0] * (len(coeffs) + 1)
                for power in range(len(coeffs)):
                    widened[power + 1] = widened[power + 1] + coeffs[power] * scale
                    widened[power] = widened[power] - time_nodes[k] * coeffs[power] * scale
                coeffs = widened
        for m in range(4):
            total = 0.0
            for power in range(len(coeffs)):
                total = total + coeffs[power] * time_nodes[m] ** (power + 1) / (power + 1)
            quad_table[m, j] = total
    return quad_table


DERIV = np.float32(lobatto_derivative())
QUAD = np.float32(step_length * collocation_matrix())
VREG = (8, 128)


def lanes():
    return lax.broadcasted_iota(jnp.int32, VREG, 1)


def sublanes():
    return lax.broadcasted_iota(jnp.int32, VREG, 0)


def lane_roll(tiles, shift):
    count = len(tiles)
    whole, rest = divmod(shift % (128 * count), 128)
    if rest == 0:
        return [tiles[(t - whole) % count] for t in range(count)]
    rotated = [pltpu.roll(tile, rest, 1) for tile in tiles]
    lane = lanes()
    return [
        jnp.where(lane < rest, rotated[(t - whole - 1) % count], rotated[(t - whole) % count])
        for t in range(count)
    ]


def primitive(state):
    rho, m1, m2, m3, energy = state
    inverse = 1.0 / rho
    v1, v2, v3 = m1 * inverse, m2 * inverse, m3 * inverse
    pressure = (gamma_gas - 1.0) * (energy - 0.5 * (m1 * v1 + m2 * v2 + m3 * v3))
    return inverse, (v1, v2, v3), pressure


def flux_entry(state, velocity, pressure, variable, direction):
    speed = velocity[direction]
    if variable == 0:
        return state[1 + direction]
    if variable == 4:
        return (state[4] + pressure) * speed
    entry = state[variable] * speed
    if variable - 1 == direction:
        entry = entry + pressure
    return entry


def wave(inverse, velocity, pressure, direction):
    square = gamma_gas * pressure * inverse
    return jnp.abs(velocity[direction]) + square * lax.rsqrt(square)


def face_terms(own, other, direction, sign):
    own_inv, own_v, own_p = primitive(own)
    oth_inv, oth_v, oth_p = primitive(other)
    speed = 3.0 * jnp.maximum(
        wave(own_inv, own_v, own_p, direction), wave(oth_inv, oth_v, oth_p, direction)
    )
    weight = 3.0 * sign
    terms = []
    for variable in range(5):
        jump = other[variable] - own[variable]
        flux_jump = flux_entry(own, own_v, own_p, variable, direction) - flux_entry(
            other, oth_v, oth_p, variable, direction
        )
        terms.append(speed * jump + weight * flux_jump)
    return terms


def z_partners(pair, pz_ref):
    lane = lanes()
    slot = sublanes() % 4
    even_ref, odd_ref = pair

    def one_variable(v, carry):
        for r in range(2):
            rows = slice(8 * r, 8 * r + 8)
            mixed = []
            for t in range(TILES):
                even = even_ref[t, v, rows, :]
                odd = odd_ref[t, v, rows, :]
                low = jnp.where(slot == 0, pltpu.roll(even, 5, 0), pltpu.roll(odd, 6, 0))
                high = jnp.where(slot == 3, pltpu.roll(even, 3, 0), pltpu.roll(odd, 2, 0))
                mixed.append(jnp.where(slot < 2, low, high))
            before = lane_roll(mixed, 1)
            before_wrap = lane_roll(mixed, -(EZ - 1))
            after = lane_roll(mixed, -1)
            after_wrap = lane_roll(mixed, EZ - 1)
            for t in range(TILES):
                column = (lane + 128 * t) % EZ
                low = jnp.where(column == 0, before_wrap[t], before[t])
                high = jnp.where(column == EZ - 1, after_wrap[t], after[t])
                pz_ref[t, v, rows, :] = jnp.where(slot < 2, low, high)
        return carry

    lax.fori_loop(0, 5, one_variable, 0)


def y_partners(u_ref, py_ref, halo_ref=None):
    lane = lanes()
    lower = sublanes() < 4

    def one_variable(v, carry):
        swapped = []
        for t in range(TILES):
            trace = jnp.where(lower, u_ref[t, v, 0:8, :], u_ref[t, v, 8:16, :])
            swapped.append(pltpu.roll(trace, 4, 0))
        before = lane_roll(swapped, EZ)
        after = lane_roll(swapped, -EZ)
        if halo_ref is not None:
            for m in range(4):
                base = 5 * (m // 2)
                got = pltpu.roll(halo_ref[m, v], 4, 0)
                if m % 2 == 0:
                    before[base] = jnp.where(lane < 80, got, before[base])
                    moved = pltpu.roll(got, 112, 1)
                    after[base + 1] = jnp.where(lane >= 112, moved, after[base + 1])
                    after[base + 2] = jnp.where(lane < 64, moved, after[base + 2])
                else:
                    moved = pltpu.roll(got, 64, 1)
                    before[base + 2] = jnp.where(lane >= 64, moved, before[base + 2])
                    before[base + 3] = jnp.where(lane < 16, moved, before[base + 3])
                    moved = pltpu.roll(got, 48, 1)
                    after[base + 4] = jnp.where(lane >= 48, moved, after[base + 4])
        for t in range(TILES):
            py_ref[t, v] = jnp.where(lower, before[t], after[t])
        return carry

    lax.fori_loop(0, 5, one_variable, 0)


def load_state(u_ref, t, rows):
    return [u_ref[t, v, rows, :] for v in range(5)]


def z_face_terms(pair, pz_ref, t):
    slot = sublanes() % 4
    outer = (slot == 0) | (slot == 3)
    sign = jnp.where(slot < 2, -1.0, 1.0).astype(jnp.float32)
    result = [[[None, None] for _ in range(2)] for _ in range(5)]
    for r in range(2):
        rows = slice(8 * r, 8 * r + 8)
        own, other = [], []
        for v in range(5):
            even = pair[0][t, v, rows, :]
            odd = pair[1][t, v, rows, :]
            inner = jnp.where(slot == 1, pltpu.roll(odd, 1, 0), pltpu.roll(odd, 7, 0))
            own.append(jnp.where(outer, even, inner))
            other.append(pz_ref[t, v, rows, :])
        terms = face_terms(own, other, 2, sign)
        for v in range(5):
            term = terms[v]
            result[v][0][r] = jnp.where(outer, term, 0.0)
            moved = jnp.where(slot == 0, pltpu.roll(term, 7, 0), pltpu.roll(term, 1, 0))
            result[v][1][r] = jnp.where(outer, moved, 0.0)
    return result


def volume_tile(t, states, targets, coef_ref, start, emit):
    slot = sublanes() % 4
    state, prim = {}, {}
    for a, ref in states.items():
        for r in range(2):
            state[a, r] = load_state(ref, t, slice(8 * r, 8 * r + 8))
            prim[a, r] = primitive(state[a, r])

    def flux(a, r, v, direction):
        return flux_entry(state[a, r], prim[a, r][1], prim[a, r][2], v, direction)

    for v in range(5):
        total = {}
        for r in range(2):
            column = {a: flux(a, r, v, 0) for a in states}
            for a in targets:
                value = start(v, a, r)
                for other in states:
                    term = float(-DERIV[a, other]) * column[other]
                    value = term if value is None else value + term
                total[a, r] = value
        for a, whole in targets.items():
            if whole:
                first, second = flux(a, 0, v, 1), flux(a, 1, v, 1)
                parts = [first, pltpu.roll(first, 4, 0), second, pltpu.roll(second, 4, 0)]
                for r in range(2):
                    for k in range(4):
                        total[a, r] = total[a, r] - coef_ref[4 * r + k] * parts[k]
            for r in range(2):
                acc = total[a, r]
                if whole:
                    along = flux(a, r, v, 2)
                    across = pltpu.roll(along, 4, 0)
                    acc = acc - coef_ref[8] * along
                    for shift in range(1, 4):
                        mixed = pltpu.roll(jnp.where(slot < 4 - shift, along, across), shift, 0)
                        acc = acc - coef_ref[8 + shift] * mixed
                emit(v, a, r, acc)


def coefficient_table():
    table = np.zeros((12, 8, 128), np.float32)
    for s in range(8):
        group, c = divmod(s, 4)
        for r in range(2):
            b = 2 * r + group
            for k in range(4):
                source = 2 * (k // 2) + (group if k % 2 == 0 else 1 - group)
                table[4 * r + k, s, :] = DERIV[b, source]
        for shift in range(4):
            table[8 + shift, s, :] = DERIV[c, (c - shift) % 4]
    return table


def y_face_tile(u_ref, py_ref, r_ref, which, t):
    lower = sublanes() < 4
    sign = jnp.where(lower, -1.0, 1.0).astype(jnp.float32)
    own = [jnp.where(lower, u_ref[t, v, 0:8, :], u_ref[t, v, 8:16, :]) for v in range(5)]
    terms = face_terms(own, [py_ref[t, v] for v in range(5)], 1, sign)
    for v in range(5):
        r_ref[t, v * 2 + which, 0:8, :] += jnp.where(lower, terms[v], 0.0)
        r_ref[t, v * 2 + which, 8:16, :] += jnp.where(lower, 0.0, terms[v])


def x_face_tile(u_ref, other_ref, r_ref, which, t):
    sign = -1.0 if which == 0 else 1.0
    for r in range(2):
        rows = slice(8 * r, 8 * r + 8)
        terms = face_terms(load_state(u_ref, t, rows), load_state(other_ref, t, rows), 0, sign)
        for v in range(5):
            r_ref[t, v * 2 + which, rows, :] += terms[v]


def rates_tile(t, states, pair, sources, pz_ref, py_refs, r_ref, coef_ref, added=None, extra=None):
    targets = {a: True for a in pair}
    refs = [states[a] for a in pair]
    face = z_face_terms(refs, pz_ref, t)

    def start(v, a, r):
        if a not in pair:
            return None
        which = pair.index(a)
        value = face[v][which][r]
        if added is not None:
            value = value + added[t, v * 2 + which, 8 * r : 8 * r + 8, :]
        return value

    def emit(v, a, r, value):
        if a in pair:
            r_ref[t, v * 2 + pair.index(a), 8 * r : 8 * r + 8, :] = value
        else:
            extra[1][t, v * 2 + extra[0].index(a), 8 * r : 8 * r + 8, :] = value

    if extra is not None:
        targets.update({a: False for a in extra[0]})
    volume_tile(t, {a: states[a] for a in sources}, targets, coef_ref, start, emit)
    for which in range(2):
        y_face_tile(refs[which], py_refs[which], r_ref, which, t)


def pack_pair(tiles):
    lane = lanes()
    low = lane < 64
    flip = [[pltpu.roll(half, 64, 1) for half in tile] for tile in tiles]
    first = [
        tiles[0][0],
        tiles[1][0],
        tiles[0][1],
        tiles[1][1],
        jnp.where(low, tiles[2][0], flip[2][1]),
    ]
    second = [
        jnp.where(low, flip[2][0], flip[3][0]),
        jnp.where(low, flip[3][0], flip[4][0]),
        jnp.where(low, flip[2][1], flip[3][1]),
        jnp.where(low, flip[3][1], flip[4][1]),
        jnp.where(low, flip[4][0], tiles[4][1]),
    ]
    return first, second


def unpack_pair(first, second):
    low = lanes() < 64
    flip_first = pltpu.roll(first[4], 64, 1)
    flip = [pltpu.roll(block, 64, 1) for block in second]
    return [
        [first[0], first[2]],
        [first[1], first[3]],
        [jnp.where(low, first[4], flip[0]), jnp.where(low, flip_first, flip[2])],
        [jnp.where(low, flip[0], flip[1]), jnp.where(low, flip[2], flip[3])],
        [jnp.where(low, flip[1], flip[4]), jnp.where(low, flip[3], second[4])],
    ]


PACK_ROWS = 50
HALO_ROWS = 57


def pack_halo_parts(halos):
    lane = lanes()
    packed = [
        jnp.where(lane < 64, halos[2 * v], pltpu.roll(halos[2 * v + 1], 64, 1)) for v in range(5)
    ]
    for first in (0, 8):
        block = None
        for n in range(first, min(first + 8, 10)):
            moved = pltpu.roll(halos[n], (16 * (n - first) + 64) % 128, 1)
            block = moved if block is None else jnp.where(lane < 16 * (n - first), block, moved)
        packed.append(block)
    return packed


def unpack_halo_parts(packed):
    lane = lanes()
    halos = []
    for n in range(10):
        low = packed[n // 2] if n % 2 == 0 else pltpu.roll(packed[n // 2], 64, 1)
        rest = pltpu.roll(packed[5 + n // 8], (64 - 16 * (n % 8)) % 128, 1)
        halos.append(jnp.where(lane < 64, low, rest))
    return halos


def pack_message(load, quarter, out_ref):
    lane = lanes()
    low = lane < 64
    lower = sublanes() < 4
    odd = quarter % 2
    base = (5 * quarter) // 2
    shift = 64 * odd
    keep = lane < 128 - shift
    under = lax.rem(base + 9, 10)
    over = lax.rem(base + 3, 10)
    below_shift = 80 - 64 * odd
    above_shift = 64 - 64 * odd
    halos = []
    for n in range(10):
        top = [load(n, 0, base + i) for i in range(3)]
        bottom = [load(n, 1, base + i) for i in range(3)]
        turned = [[pltpu.roll(x, shift, 1) for x in half] for half in (top, bottom)]
        for r in range(2):
            out_ref[5 * n + 2 * r] = jnp.where(keep, turned[r][0], turned[r][1])
            out_ref[5 * n + 2 * r + 1] = jnp.where(keep, turned[r][1], turned[r][2])
        out_ref[5 * n + 4] = jnp.where(low, turned[0][2], pltpu.roll(bottom[2], above_shift, 1))
        below = jnp.where(
            lane < below_shift,
            pltpu.roll(load(n, 1, under), below_shift, 1),
            pltpu.roll(bottom[0], below_shift, 1),
        )
        above = jnp.where(
            lane < above_shift,
            pltpu.roll(top[2], above_shift, 1),
            pltpu.roll(load(n, 0, over), above_shift, 1),
        )
        halos.append(jnp.where(lower, above, below))
    for i, block in enumerate(pack_halo_parts(halos)):
        out_ref[PACK_ROWS + i] = block


def rate_loader(r_ref):
    return lambda n, r, t: r_ref[t, n, 8 * r : 8 * r + 8, :]


def start_rows(v, a, r, t):
    return pl.ds(((v * 4 + a) * 16 + 8 * r) * 10 + t, 8, stride=10)


def front_kernel(rank_ref, coef_ref, start_hbm, offset_hbm, u0, u1, u2, u3, r_ref, m1, m2, m3, start_ref, offset_ref, pz_ref, py1, py2, sems):
    copies = []
    for v in range(5):
        rows = pl.ds(640 * v, 640)
        pair = [
            pltpu.make_async_copy(start_hbm.at[rows], start_ref.at[rows], sems.at[2 * v]),
            pltpu.make_async_copy(offset_hbm.at[rows], offset_ref.at[rows], sems.at[2 * v + 1]),
        ]
        for copy in pair:
            copy.start()
        copies.append(pair)
    states = {0: u0, 1: u1, 2: u2, 3: u3}
    for v in range(5):
        for copy in copies[v]:
            copy.wait()
        for a in range(4):

            def one_tile(t, carry):
                for r in range(2):
                    rows = start_rows(v, a, r, t)
                    states[a][t, v, 8 * r : 8 * r + 8, :] = start_ref[rows, :] + offset_ref[rows, :]
                return carry

            lax.fori_loop(0, TILES, one_tile, 0, unroll=True)
    z_partners((u1, u2), pz_ref)
    y_partners(u1, py1)
    y_partners(u2, py2)

    def one_tile(t, carry):
        rates_tile(t, states, (1, 2), (0, 1, 2, 3), pz_ref, (py1, py2), r_ref, coef_ref)
        return carry

    lax.fori_loop(0, TILES, one_tile, 0)
    for d, out in ((1, m1), (2, m2), (3, m3)):
        pack_message(rate_loader(r_ref), lax.rem(rank_ref[0] + d, 4), out)


def edge_kernel(rank_ref, coef_ref, u0, u1, u2, u3, left_ref, right_ref, m1, m2, m3, r_ref, pz_ref, py0, py3):
    z_partners((u0, u3), pz_ref)
    y_partners(u0, py0)
    y_partners(u3, py3)
    states = {0: u0, 1: u1, 2: u2, 3: u3}

    def one_tile(t, carry):
        rates_tile(t, states, (0, 3), (0, 1, 2, 3), pz_ref, (py0, py3), r_ref, coef_ref)
        x_face_tile(u0, left_ref, r_ref, 0, t)
        x_face_tile(u3, right_ref, r_ref, 1, t)
        return carry

    lax.fori_loop(0, TILES, one_tile, 0)
    for d, out in ((1, m1), (2, m2), (3, m3)):
        pack_message(rate_loader(r_ref), lax.rem(rank_ref[0] + d, 4), out)


def own_kernel(rank_ref, start_ref, mid_ref, edge_ref, start_mid, start_edge, own_mid, own_edge):
    rank = rank_ref[0]
    for pair, rates, start_out, own_out in (((1, 2), mid_ref, start_mid, own_mid), ((0, 3), edge_ref, start_edge, own_edge)):

        def load(n, r, t):
            return start_ref[start_rows(n // 2, pair[n % 2], r, t), :]

        pack_message(load, rank, start_out)
        pack_message(rate_loader(rates), rank, own_out)


def assemble(rank_ref, table_ref, start_ref, rates, states, halos):
    rank = rank_ref[0]
    weight = [
        [table_ref[m * 4 + lax.rem(rank + 4 - d, 4)] for d in range(4)] for m in range(4)
    ]

    def node_state(m, row):
        total = start_ref[row]
        for d in range(4):
            total = total + weight[m][d] * rates[d][row]
        return total

    def one_variable(v, carry):
        for which in range(2):
            first = 10 * v + 5 * which
            for pair in range(2):
                pieces = [[node_state(2 * pair + half, first + i) for i in range(5)] for half in range(2)]
                tiles = unpack_pair(*pieces)
                for i in range(5):
                    for r in range(2):
                        states[which][5 * pair + i, v, 8 * r : 8 * r + 8, :] = tiles[i][r]
        return carry

    lax.fori_loop(0, 5, one_variable, 0)
    for m in range(4):
        blocks = unpack_halo_parts([node_state(m, PACK_ROWS + i) for i in range(7)])
        for n in range(10):
            halos[n % 2][m, n // 2] = blocks[n]


def send_increments(rank_ref, table_ref, r_ref, outs):
    rank = rank_ref[0]
    weight = [[table_ref[lax.rem(rank + d, 4) * 4 + j] for j in range(4)] for d in range(4)]

    def one_block(n, carry):
        pieces = []
        for pair in range(2):
            tiles = [[r_ref[5 * pair + i, n, 8 * r : 8 * r + 8, :] for r in range(2)] for i in range(5)]
            pieces.extend(pack_pair(tiles))
        for d in range(4):
            for i in range(5):
                total = weight[d][0] * pieces[0][i]
                for j in range(1, 4):
                    total = total + weight[d][j] * pieces[j][i]
                outs[d][5 * n + i] = total
        return carry

    lax.fori_loop(0, 10, one_block, 0)


def middle_kernel(rank_ref, table_ref, coef_ref, start_ref, q0, q1, q2, q3, mid_ref, edge_ref, u1, u2, h1, h2, pz_ref, py1, py2):
    assemble(rank_ref, table_ref, start_ref, (q0, q1, q2, q3), (u1, u2), (h1, h2))
    z_partners((u1, u2), pz_ref)
    y_partners(u1, py1, h1)
    y_partners(u2, py2, h2)
    states = {1: u1, 2: u2}

    def one_tile(t, carry):
        rates_tile(t, states, (1, 2), (1, 2), pz_ref, (py1, py2), mid_ref, coef_ref, extra=((0, 3), edge_ref))
        return carry

    lax.fori_loop(0, TILES, one_tile, 0)


def join_kernel(rank_ref, table_ref, start_ref, q0, q1, q2, q3, mid_ref, u0, u3, h0, h3, o0, o1, o2, o3, r_ref):
    assemble(rank_ref, table_ref, start_ref, (q0, q1, q2, q3), (u0, u3), (h0, h3))

    def one_tile(t, carry):
        def start(v, a, r):
            return mid_ref[t, v * 2 + a - 1, 8 * r : 8 * r + 8, :]

        def emit(v, a, r, value):
            r_ref[t, v * 2 + a - 1, 8 * r : 8 * r + 8, :] = value

        volume_tile(t, {0: u0, 3: u3}, {1: False, 2: False}, None, start, emit)
        return carry

    lax.fori_loop(0, TILES, one_tile, 0)
    send_increments(rank_ref, table_ref, r_ref, (o0, o1, o2, o3))


def last_kernel(rank_ref, table_ref, coef_ref, u0, u3, h0, h3, partial_ref, left_ref, right_ref, o0, o1, o2, o3, r_ref, pz_ref, py0, py3):
    z_partners((u0, u3), pz_ref)
    y_partners(u0, py0, h0)
    y_partners(u3, py3, h3)
    states = {0: u0, 3: u3}

    def one_tile(t, carry):
        rates_tile(t, states, (0, 3), (0, 3), pz_ref, (py0, py3), r_ref, coef_ref, added=partial_ref)
        x_face_tile(u0, left_ref, r_ref, 0, t)
        x_face_tile(u3, right_ref, r_ref, 1, t)
        return carry

    lax.fori_loop(0, TILES, one_tile, 0)
    send_increments(rank_ref, table_ref, r_ref, (o0, o1, o2, o3))


def finish(rank_ref, pieces, out_hbm, order_ref, stage_ref, sems, pair):
    rank = rank_ref[0]
    for d in range(4):
        slot = lax.rem(rank + 4 - d, 4)
        order_ref[slot] = pieces[d][...]
    copies = []
    for v in range(5):
        for which in range(2):
            n = v * 2 + which
            for half in range(2):
                blocks = [[order_ref[2 * half + k, 5 * n + i] for i in range(5)] for k in range(2)]
                tiles = unpack_pair(*blocks)
                for i in range(5):
                    for r in range(2):
                        stage_ref[pl.ds(n * 160 + 80 * r + 5 * half + i, 8, stride=10), :] = tiles[i][r]
            copy = pltpu.make_async_copy(
                stage_ref.at[pl.ds(n * 160, 160)],
                out_hbm.at[pl.ds((v * 4 + pair[which]) * 160, 160)],
                sems.at[n],
            )
            copy.start()
            copies.append(copy)
    for copy in copies:
        copy.wait()


def finish_middle(rank_ref, q0, q1, q2, q3, out_hbm, order_ref, stage_ref, sems):
    finish(rank_ref, (q0, q1, q2, q3), out_hbm, order_ref, stage_ref, sems, (1, 2))


def finish_edge(rank_ref, q0, q1, q2, q3, before_hbm, out_hbm, order_ref, stage_ref, sems):
    finish(rank_ref, (q0, q1, q2, q3), out_hbm, order_ref, stage_ref, sems, (0, 3))


def f32(*shape):
    return jax.ShapeDtypeStruct(shape, jnp.float32)


TRACE = (TILES, 5, 16, 128)
SIDE = (TILES, 5, 8, 128)
RATE = (TILES, 10, 16, 128)
HALO = (4, 5, 8, 128)
FLAT = (3200, 128)
MESSAGE = (HALO_ROWS, 8, 128)
PIECE = (PACK_ROWS, 8, 128)


def call(kernel, outs, args, scratch=(), flops=0, aliases=None):
    place = {
        "s": pl.BlockSpec(memory_space=pltpu.SMEM),
        "v": pl.BlockSpec(memory_space=pltpu.VMEM),
        "h": pl.BlockSpec(memory_space=pl.ANY),
    }
    moved = sum(4 * math.prod(a.shape) for _, a in args)
    moved += sum(4 * math.prod(shape) for _, shape in outs)
    result = pl.pallas_call(
        kernel,
        out_shape=[f32(*shape) for _, shape in outs],
        in_specs=[place[where] for where, _ in args],
        out_specs=[place[where] for where, _ in outs],
        scratch_shapes=[
            pltpu.SemaphoreType.DMA(shape) if len(shape) == 1 else pltpu.VMEM(shape, jnp.float32)
            for shape in scratch
        ],
        input_output_aliases=aliases or {},
        compiler_params=pltpu.CompilerParams(vmem_limit_bytes=VMEM_LIMIT),
        cost_estimate=pl.CostEstimate(flops=flops, bytes_accessed=moved, transcendentals=0),
    )(*[a for _, a in args])
    return result


def shifted(block, axis, distance):
    count = lax.axis_size(axis)
    return lax.ppermute(block, axis, [((i - distance) % count, i) for i in range(count)])


def v(*arrays):
    return [("v", a) for a in arrays]


def exchange(messages):
    return [shifted(messages[d - 1], "node", d) for d in (1, 2, 3)]


def body(start_state, node_offset):
    start_flat = start_state.reshape(FLAT)
    offset_flat = node_offset.reshape(FLAT)
    rank = ("s", lax.axis_index("node").astype(jnp.int32).reshape(1))
    table = ("s", jnp.asarray(QUAD.reshape(16)))
    coef = ("v", jnp.asarray(coefficient_table()))

    u0, u1, u2, u3, mid, *sent = call(
        front_kernel,
        v(TRACE, TRACE, TRACE, TRACE, RATE, MESSAGE, MESSAGE, MESSAGE),
        [rank, coef, ("h", start_flat), ("h", offset_flat)],
        scratch=[FLAT, FLAT, TRACE, SIDE, SIDE, (10,)],
    )
    got_mid = exchange(sent)
    left = shifted(u3, "space", 1)
    right = shifted(u0, "space", -1)
    *sent, edge = call(
        edge_kernel,
        v(MESSAGE, MESSAGE, MESSAGE, RATE),
        [rank, coef] + v(u0, u1, u2, u3, left, right),
        scratch=[TRACE, SIDE, SIDE],
    )
    got_edge = exchange(sent)
    start_mid, start_edge, own_mid, own_edge = call(
        own_kernel,
        v(MESSAGE, MESSAGE, MESSAGE, MESSAGE),
        [rank] + v(start_flat, mid, edge),
    )
    mid, edge = call(
        middle_kernel,
        v(RATE, RATE),
        [rank, table, coef] + v(start_mid, own_mid, *got_mid),
        scratch=[TRACE, TRACE, HALO, HALO, TRACE, SIDE, SIDE],
    )
    u0, u3, h0, h3, own_mid, *sent = call(
        join_kernel,
        v(TRACE, TRACE, HALO, HALO, PIECE, PIECE, PIECE, PIECE),
        [rank, table] + v(start_edge, own_edge, *got_edge, mid),
        scratch=[RATE],
    )
    got_mid = exchange(sent)
    left = shifted(u3, "space", 1)
    right = shifted(u0, "space", -1)
    own_edge, *sent = call(
        last_kernel,
        v(PIECE, PIECE, PIECE, PIECE),
        [rank, table, coef] + v(u0, u3, h0, h3, edge, left, right),
        scratch=[RATE, TRACE, SIDE, SIDE],
    )
    got_edge = exchange(sent)
    finishing = [(4,) + PIECE, (1600, 128), (10,)]
    (result,) = call(
        finish_middle,
        [("h", FLAT)],
        [rank] + v(own_mid, *got_mid),
        scratch=finishing,
    )
    (result,) = call(
        finish_edge,
        [("h", FLAT)],
        [rank] + v(own_edge, *got_edge) + [("h", result)],
        scratch=finishing,
        aliases={5: 0},
    )
    return result.reshape(node_offset.shape)


def solution(mesh):
    return jax.shard_map(
        body,
        mesh=mesh,
        in_specs=(
            P(None, None, None, None, "space", None),
            P("node", None, None, None, None, "space", None),
        ),
        out_specs=P("node", None, None, None, None, "space", None),
        check_vma=False,
    )
```

profile of v0, /device:TPU:13, one launch (start us, length us, event | category | flops | bytes accessed | tf_op | source)
XLA Modules:
  0.0 96.2 jit_solution(15670360502151470660)
XLA Ops:
  0.0 1.4 %copy-done = f32[5,4,4,4,1,1280]{5,4,3,2,1,0:T(1,128)S(1)} copy-done((f32[5,4,4,4,1,1280]{5,4,3,2,1,0:T(1,128)S(1)}, f32[5,4,4,4,1,1280]{5,4,3,2,1,0:T(1,128)}, u32[]{:S(2)}) %copy-start) | copy-done | bytes 1638424
  2.2 5.8 %shard_map.46 = (f32[10,5,16,128]{3,2,1,0:T(8,128)S(1)}, f32[10,5,16,128]{3,2,1,0:T(8,128)S(1)}, f32[10,5,16,128]{3,2,1,0:T(8,128)S(1)}, f32[10,5,16,128]{3,2,1,...) custom-call(s32[1]{0:T(128)} %bitcast.rank_ref, ...), custom_call_target="tpu_custom_call" | custom-call | bytes 6483972 | tf_op jit(solution)/shard_map/pallas_call | solution.py:640
  8.8 1.2 %collective-permute-start = (f32[10,5,16,128]{3,2,1,0:T(8,128)S(1)}, f32[10,5,16,128]{3,2,1,0:T(8,128)S(1)}, u32[]{:S(2)}, u32[]{:S(2)}) collective-permute-start(f32[10,5,16,128]{3,2,1,0:T(8,128)S(1)} %get-tuple-element.39.u3), channel_id=1, source_target_pairs={{7,0},{0,1},{1,2},{2,3},{3,4},{4,5},{5,6},{6,7},{15,8},{8,9},{9,10... | collective-permute-start | bytes 1228808 | tf_op jit(solution)/shard_map/ppermute | solution.py:658
  10.0 1.3 %collective-permute-start.5 = (f32[57,8,128]{2,1,0:T(8,128)S(1)}, f32[57,8,128]{2,1,0:T(8,128)S(1)}, u32[]{:S(2)}, u32[]{:S(2)}) collective-permute-start(f32[57,8,128]{2,1,0:T(8,128)S(1)} %get-tuple-element.48), channel_id=1, source_target_pairs={{24,0},{0,8},{8,16},{16,24},{25,1},{1,9},{9,17},{17,25},{26,2},{2,... | collective-permute-start | bytes 700424 | tf_op jit(solution)/shard_map/ppermute | solution.py:658
  11.3 1.0 %collective-permute-start.6 = (f32[57,8,128]{2,1,0:T(8,128)S(1)}, f32[57,8,128]{2,1,0:T(8,128)S(1)}, u32[]{:S(2)}, u32[]{:S(2)}) collective-permute-start(f32[57,8,128]{2,1,0:T(8,128)S(1)} %get-tuple-element.49), channel_id=1, source_target_pairs={{16,0},{24,8},{0,16},{8,24},{17,1},{25,9},{1,17},{9,25},{18,2},{26... | collective-permute-start | bytes 700424 | tf_op jit(solution)/shard_map/ppermute | solution.py:658
  12.3 1.5 %collective-permute-start.7 = (f32[57,8,128]{2,1,0:T(8,128)S(1)}, f32[57,8,128]{2,1,0:T(8,128)S(1)}, u32[]{:S(2)}, u32[]{:S(2)}) collective-permute-start(f32[57,8,128]{2,1,0:T(8,128)S(1)} %get-tuple-element.50), channel_id=1, source_target_pairs={{8,0},{16,8},{24,16},{0,24},{9,1},{17,9},{25,17},{1,25},{10,2},{18... | collective-permute-start | bytes 700424 | tf_op jit(solution)/shard_map/ppermute | solution.py:658
  13.7 4.6 %collective-permute-done.1.right_ref = f32[10,5,16,128]{3,2,1,0:T(8,128)S(1)} collective-permute-done((f32[10,5,16,128]{3,2,1,0:T(8,128)S(1)}, f32[10,5,16,128]{3,2,1,0:T(8,128)S(1)}, u32[]{:S(2)}, u32[]{:S(2)}) %collective-permute-start.1) | collective-permute-done | bytes 409632 | tf_op jit(solution)/shard_map/ppermute | solution.py:658
  18.4 0.8 collective-permute-done.left_ref
  19.2 4.6 %shard_map.47 = (f32[57,8,128]{2,1,0:T(8,128)S(1)}, f32[57,8,128]{2,1,0:T(8,128)S(1)}, f32[57,8,128]{2,1,0:T(8,128)S(1)}, f32[10,10,16,128]{3,2,1,0:T(8,128)S(1)}) custom-call(s32[1]{0:T(128)} %bitcast.rank_ref, f32[12,8,128]{2,1,0:T(8,128)S(1)} %copy-done.2, f32[10,5,16,128]{3,2,1,0:T(8,128)S(1)} %get-tuple-element.36.u0, ...), custom_call_target="tpu_custom_call" | custom-call | bytes 4026372 | tf_op jit(solution)/shard_map/pallas_call | solution.py:640
  23.8 1.3 %collective-permute-start.2 = (f32[57,8,128]{2,1,0:T(8,128)S(1)}, f32[57,8,128]{2,1,0:T(8,128)S(1)}, u32[]{:S(2)}, u32[]{:S(2)}) collective-permute-start(f32[57,8,128]{2,1,0:T(8,128)S(1)} %get-tuple-element.43), channel_id=1, source_target_pairs={{24,0},{0,8},{8,16},{16,24},{25,1},{1,9},{9,17},{17,25},{26,2},{2,... | collective-permute-start | bytes 700424 | tf_op jit(solution)/shard_map/ppermute | solution.py:658
  25.2 1.1 %collective-permute-start.3 = (f32[57,8,128]{2,1,0:T(8,128)S(1)}, f32[57,8,128]{2,1,0:T(8,128)S(1)}, u32[]{:S(2)}, u32[]{:S(2)}) collective-permute-start(f32[57,8,128]{2,1,0:T(8,128)S(1)} %get-tuple-element.44), channel_id=1, source_target_pairs={{16,0},{24,8},{0,16},{8,24},{17,1},{25,9},{1,17},{9,25},{18,2},{26... | collective-permute-start | bytes 700424 | tf_op jit(solution)/shard_map/ppermute | solution.py:658
  26.3 1.4 %collective-permute-start.4 = (f32[57,8,128]{2,1,0:T(8,128)S(1)}, f32[57,8,128]{2,1,0:T(8,128)S(1)}, u32[]{:S(2)}, u32[]{:S(2)}) collective-permute-start(f32[57,8,128]{2,1,0:T(8,128)S(1)} %get-tuple-element.45), channel_id=1, source_target_pairs={{8,0},{16,8},{24,16},{0,24},{9,1},{17,9},{25,17},{1,25},{10,2},{18... | collective-permute-start | bytes 700424 | tf_op jit(solution)/shard_map/ppermute | solution.py:658
  28.5 3.2 %collective-permute-done.6.q2 = f32[57,8,128]{2,1,0:T(8,128)S(1)} collective-permute-done((f32[57,8,128]{2,1,0:T(8,128)S(1)}, f32[57,8,128]{2,1,0:T(8,128)S(1)}, u32[]{:S(2)}, u32[]{:S(2)}) %collective-permute-start.6) | collective-permute-done | bytes 233504 | tf_op jit(solution)/shard_map/ppermute | solution.py:658
  31.7 11.8 %collective-permute-done.7.q3 = f32[57,8,128]{2,1,0:T(8,128)S(1)} collective-permute-done((f32[57,8,128]{2,1,0:T(8,128)S(1)}, f32[57,8,128]{2,1,0:T(8,128)S(1)}, u32[]{:S(2)}, u32[]{:S(2)}) %collective-permute-start.7) | collective-permute-done | bytes 233504 | tf_op jit(solution)/shard_map/ppermute | solution.py:658
  43.5 4.7 %shard_map.49 = (f32[10,10,16,128]{3,2,1,0:T(8,128)S(1)}, f32[10,10,16,128]{3,2,1,0:T(8,128)S(1)}) custom-call(s32[1]{0:T(128)} %bitcast.rank_ref, f32[16]{0:T(128)S(1)} %copy-done.4, f32[12,8,128]{2,1,0:T(8,128)S(1)} %copy-done.2, f32[57,8,128]{2,1,0:T(8,128)S(1)} %get-tuple-element.46.start_ref, f32[57,8,128]{2,1,0:T(8,128)S(1)} %get-tuple-element.47.q0, ...), custom_call_target="tpu_custom_call" | custom-call | bytes 2854980 | tf_op jit(solution)/shard_map/pallas_call | solution.py:640
  48.2 3.4 %collective-permute-done.3.q2 = f32[57,8,128]{2,1,0:T(8,128)S(1)} collective-permute-done((f32[57,8,128]{2,1,0:T(8,128)S(1)}, f32[57,8,128]{2,1,0:T(8,128)S(1)}, u32[]{:S(2)}, u32[]{:S(2)}) %collective-permute-start.3) | collective-permute-done | bytes 233504 | tf_op jit(solution)/shard_map/ppermute | solution.py:658
  51.6 1.9 %collective-permute-done.4.q3 = f32[57,8,128]{2,1,0:T(8,128)S(1)} collective-permute-done((f32[57,8,128]{2,1,0:T(8,128)S(1)}, f32[57,8,128]{2,1,0:T(8,128)S(1)}, u32[]{:S(2)}, u32[]{:S(2)}) %collective-permute-start.4) | collective-permute-done | bytes 233504 | tf_op jit(solution)/shard_map/ppermute | solution.py:658
  53.5 2.5 %shard_map.50 = (f32[10,5,16,128]{3,2,1,0:T(8,128)S(1)}, f32[10,5,16,128]{3,2,1,0:T(8,128)S(1)}, f32[4,5,8,128]{3,2,1,0:T(8,128)S(1)}, f32[4,5,8,128]{3,2,1,0:T(...) custom-call(s32[1]{0:T(128)} %bitcast.rank_ref, ...), custom_call_target="tpu_custom_call" | custom-call | bytes 3788868 | tf_op jit(solution)/shard_map/pallas_call | solution.py:640
  56.5 1.3 %collective-permute-start.8 = (f32[10,5,16,128]{3,2,1,0:T(8,128)S(1)}, f32[10,5,16,128]{3,2,1,0:T(8,128)S(1)}, u32[]{:S(2)}, u32[]{:S(2)}) collective-permute-start(f32[10,5,16,128]{3,2,1,0:T(8,128)S(1)} %get-tuple-element.53.u3), channel_id=1, source_target_pairs={{7,0},{0,1},{1,2},{2,3},{3,4},{4,5},{5,6},{6,7},{15,8},{8,9},{9,10... | collective-permute-start | bytes 1228808 | tf_op jit(solution)/shard_map/ppermute | solution.py:658
  57.8 1.2 %collective-permute-start.14 = (f32[50,8,128]{2,1,0:T(8,128)S(1)}, f32[50,8,128]{2,1,0:T(8,128)S(1)}, u32[]{:S(2)}, u32[]{:S(2)}) collective-permute-start(f32[50,8,128]{2,1,0:T(8,128)S(1)} %get-tuple-element.63), channel_id=1, source_target_pairs={{16,0},{24,8},{0,16},{8,24},{17,1},{25,9},{1,17},{9,25},{18,2},{26... | collective-permute-start | bytes 614408 | tf_op jit(solution)/shard_map/ppermute | solution.py:658
  59.0 1.5 %collective-permute-start.15 = (f32[50,8,128]{2,1,0:T(8,128)S(1)}, f32[50,8,128]{2,1,0:T(8,128)S(1)}, u32[]{:S(2)}, u32[]{:S(2)}) collective-permute-start(f32[50,8,128]{2,1,0:T(8,128)S(1)} %get-tuple-element.64), channel_id=1, source_target_pairs={{8,0},{16,8},{24,16},{0,24},{9,1},{17,9},{25,17},{1,25},{10,2},{18... | collective-permute-start | bytes 614408 | tf_op jit(solution)/shard_map/ppermute | solution.py:658
  60.5 6.1 %collective-permute-done.9.right_ref = f32[10,5,16,128]{3,2,1,0:T(8,128)S(1)} collective-permute-done((f32[10,5,16,128]{3,2,1,0:T(8,128)S(1)}, f32[10,5,16,128]{3,2,1,0:T(8,128)S(1)}, u32[]{:S(2)}, u32[]{:S(2)}) %collective-permute-start.9) | collective-permute-done | bytes 409632 | tf_op jit(solution)/shard_map/ppermute | solution.py:658
  66.8 5.3 %shard_map.51 = (f32[50,8,128]{2,1,0:T(8,128)S(1)}, f32[50,8,128]{2,1,0:T(8,128)S(1)}, f32[50,8,128]{2,1,0:T(8,128)S(1)}, f32[50,8,128]{2,1,0:T(8,128)S(1)}) custom-call(s32[1]{0:T(128)} %bitcast.rank_ref, f32[16]{0:T(128)S(1)} %copy-done.4, f32[12,8,128]{2,1,0:T(8,128)S(1)} %copy-done.3, f32[10,5,16,128]{3,2,1,0:T(8,128)S(1)} %get-tuple-element.52.u0, ...), custom_call_target="tpu_custom_call" | custom-call | bytes 3489860 | tf_op jit(solution)/shard_map/pallas_call | solution.py:640
  72.2 1.3 %collective-permute-start.11 = (f32[50,8,128]{2,1,0:T(8,128)S(1)}, f32[50,8,128]{2,1,0:T(8,128)S(1)}, u32[]{:S(2)}, u32[]{:S(2)}) collective-permute-start(f32[50,8,128]{2,1,0:T(8,128)S(1)} %get-tuple-element.59), channel_id=1, source_target_pairs={{16,0},{24,8},{0,16},{8,24},{17,1},{25,9},{1,17},{9,25},{18,2},{26... | collective-permute-start | bytes 614408 | tf_op jit(solution)/shard_map/ppermute | solution.py:658
  73.5 1.4 %collective-permute-start.12 = (f32[50,8,128]{2,1,0:T(8,128)S(1)}, f32[50,8,128]{2,1,0:T(8,128)S(1)}, u32[]{:S(2)}, u32[]{:S(2)}) collective-permute-start(f32[50,8,128]{2,1,0:T(8,128)S(1)} %get-tuple-element.60), channel_id=1, source_target_pairs={{8,0},{16,8},{24,16},{0,24},{9,1},{17,9},{25,17},{1,25},{10,2},{18... | collective-permute-start | bytes 614408 | tf_op jit(solution)/shard_map/ppermute | solution.py:658
  74.9 1.1 %collective-permute-done.14.q2 = f32[50,8,128]{2,1,0:T(8,128)S(1)} collective-permute-done((f32[50,8,128]{2,1,0:T(8,128)S(1)}, f32[50,8,128]{2,1,0:T(8,128)S(1)}, u32[]{:S(2)}, u32[]{:S(2)}) %collective-permute-start.14) | collective-permute-done | bytes 204832 | tf_op jit(solution)/shard_map/ppermute | solution.py:658
  76.0 10.3 %collective-permute-done.15.q3 = f32[50,8,128]{2,1,0:T(8,128)S(1)} collective-permute-done((f32[50,8,128]{2,1,0:T(8,128)S(1)}, f32[50,8,128]{2,1,0:T(8,128)S(1)}, u32[]{:S(2)}, u32[]{:S(2)}) %collective-permute-start.15) | collective-permute-done | bytes 204832 | tf_op jit(solution)/shard_map/ppermute | solution.py:658
  86.3 1.1 %shard_map.52.before_hbm = f32[3200,128]{1,0:T(8,128)} custom-call(s32[1]{0:T(128)} %bitcast.rank_ref, f32[50,8,128]{2,1,0:T(8,128)S(1)} %get-tuple-element.61.q0, f32[50,8,128]{2,1,0:T(8,128)S(1)} %collective-permute-done.13.q1, f32[50,8,128]{2,1,0:T(8,128)S(1)} %collective-permute-done.14.q2, f32[50,8,128]{2,1,0:T(8,128)S(1)} %collective-permute-done.15.q3), custom_call_target="tpu_custom_call" | custom-call | bytes 2457604 | tf_op jit(solution)/shard_map/pallas_call | solution.py:640
  87.4 1.7 %collective-permute-done.10.q1 = f32[50,8,128]{2,1,0:T(8,128)S(1)} collective-permute-done((f32[50,8,128]{2,1,0:T(8,128)S(1)}, f32[50,8,128]{2,1,0:T(8,128)S(1)}, u32[]{:S(2)}, u32[]{:S(2)}) %collective-permute-start.10) | collective-permute-done | bytes 204832 | tf_op jit(solution)/shard_map/ppermute | solution.py:658
  89.2 4.1 %collective-permute-done.11.q2 = f32[50,8,128]{2,1,0:T(8,128)S(1)} collective-permute-done((f32[50,8,128]{2,1,0:T(8,128)S(1)}, f32[50,8,128]{2,1,0:T(8,128)S(1)}, u32[]{:S(2)}, u32[]{:S(2)}) %collective-permute-start.11) | collective-permute-done | bytes 204832 | tf_op jit(solution)/shard_map/ppermute | solution.py:658
  93.2 1.9 %collective-permute-done.12.q3 = f32[50,8,128]{2,1,0:T(8,128)S(1)} collective-permute-done((f32[50,8,128]{2,1,0:T(8,128)S(1)}, f32[50,8,128]{2,1,0:T(8,128)S(1)}, u32[]{:S(2)}, u32[]{:S(2)}) %collective-permute-start.12) | collective-permute-done | bytes 204832 | tf_op jit(solution)/shard_map/ppermute | solution.py:658
  95.1 1.1 %shard_map.53 = f32[3200,128]{1,0:T(8,128)} custom-call(s32[1]{0:T(128)} %bitcast.rank_ref, f32[50,8,128]{2,1,0:T(8,128)S(1)} %get-tuple-element.57.q0, f32[50,8,128]{2,1,0:T(8,128)S(1)} %collective-permute-done.10.q1, f32[50,8,128]{2,1,0:T(8,128)S(1)} %collective-permute-done.11.q2, ...), custom_call_target="tpu_custom_call", output_to_operand_aliasing={{}: (5, {})} | custom-call | bytes 4096004 | tf_op jit(solution)/shard_map/pallas_call | solution.py:640
  (18 shorter events, 3.2 us)
Async XLA Ops:
  0.0 1.4 %copy-start = (f32[5,4,4,4,1,1280]{5,4,3,2,1,0:T(1,128)S(1)}, f32[5,4,4,4,1,1280]{5,4,3,2,1,0:T(1,128)}, u32[]{:S(2)}) copy-start(f32[5,4,4,4,1,1280]{5,4,3,2,1,0:T(1,128)} %param.4) | copy-start | bytes 4915204
  1.4 0.8 copy-start.2
  8.1 19.6 %copy-start.1 = (f32[5,4,4,4,1,1280]{5,4,3,2,1,0:T(1,128)S(1)}, f32[5,4,4,4,1,1280]{5,4,3,2,1,0:T(1,128)}, u32[]{:S(2)}) copy-start(f32[5,4,4,4,1,1280]{5,4,3,2,1,0:T(1,128)} %param.4) | copy-start | bytes 4915204
  8.1 10.3 %collective-permute-start.1 = (f32[10,5,16,128]{3,2,1,0:T(8,128)S(1)}, f32[10,5,16,128]{3,2,1,0:T(8,128)S(1)}, u32[]{:S(2)}, u32[]{:S(2)}) collective-permute-start(f32[10,5,16,128]{3,2,1,0:T(8,128)S(1)} %get-tuple-element.36.u0), channel_id=1, source_target_pairs={{1,0},{2,1},{3,2},{4,3},{5,4},{6,5},{7,6},{0,7},{9,8},{10,9},{11,1... | collective-permute-start | bytes 1228808 | tf_op jit(solution)/shard_map/ppermute | solution.py:658
  8.8 10.4 %collective-permute-start = (f32[10,5,16,128]{3,2,1,0:T(8,128)S(1)}, f32[10,5,16,128]{3,2,1,0:T(8,128)S(1)}, u32[]{:S(2)}, u32[]{:S(2)}) collective-permute-start(f32[10,5,16,128]{3,2,1,0:T(8,128)S(1)} %get-tuple-element.39.u3), channel_id=1, source_target_pairs={{7,0},{0,1},{1,2},{2,3},{3,4},{4,5},{5,6},{6,7},{15,8},{8,9},{9,10... | collective-permute-start | bytes 1228808 | tf_op jit(solution)/shard_map/ppermute | solution.py:658
  10.0 16.3 %collective-permute-start.5 = (f32[57,8,128]{2,1,0:T(8,128)S(1)}, f32[57,8,128]{2,1,0:T(8,128)S(1)}, u32[]{:S(2)}, u32[]{:S(2)}) collective-permute-start(f32[57,8,128]{2,1,0:T(8,128)S(1)} %get-tuple-element.48), channel_id=1, source_target_pairs={{24,0},{0,8},{8,16},{16,24},{25,1},{1,9},{9,17},{17,25},{26,2},{2,... | collective-permute-start | bytes 700424 | tf_op jit(solution)/shard_map/ppermute | solution.py:658
  11.3 20.4 %collective-permute-start.6 = (f32[57,8,128]{2,1,0:T(8,128)S(1)}, f32[57,8,128]{2,1,0:T(8,128)S(1)}, u32[]{:S(2)}, u32[]{:S(2)}) collective-permute-start(f32[57,8,128]{2,1,0:T(8,128)S(1)} %get-tuple-element.49), channel_id=1, source_target_pairs={{16,0},{24,8},{0,16},{8,24},{17,1},{25,9},{1,17},{9,25},{18,2},{26... | collective-permute-start | bytes 700424 | tf_op jit(solution)/shard_map/ppermute | solution.py:658
  12.3 31.3 %collective-permute-start.7 = (f32[57,8,128]{2,1,0:T(8,128)S(1)}, f32[57,8,128]{2,1,0:T(8,128)S(1)}, u32[]{:S(2)}, u32[]{:S(2)}) collective-permute-start(f32[57,8,128]{2,1,0:T(8,128)S(1)} %get-tuple-element.50), channel_id=1, source_target_pairs={{8,0},{16,8},{24,16},{0,24},{9,1},{17,9},{25,17},{1,25},{10,2},{18... | collective-permute-start | bytes 700424 | tf_op jit(solution)/shard_map/ppermute | solution.py:658
  23.8 24.4 %collective-permute-start.2 = (f32[57,8,128]{2,1,0:T(8,128)S(1)}, f32[57,8,128]{2,1,0:T(8,128)S(1)}, u32[]{:S(2)}, u32[]{:S(2)}) collective-permute-start(f32[57,8,128]{2,1,0:T(8,128)S(1)} %get-tuple-element.43), channel_id=1, source_target_pairs={{24,0},{0,8},{8,16},{16,24},{25,1},{1,9},{9,17},{17,25},{26,2},{2,... | collective-permute-start | bytes 700424 | tf_op jit(solution)/shard_map/ppermute | solution.py:658
  25.2 26.5 %collective-permute-start.3 = (f32[57,8,128]{2,1,0:T(8,128)S(1)}, f32[57,8,128]{2,1,0:T(8,128)S(1)}, u32[]{:S(2)}, u32[]{:S(2)}) collective-permute-start(f32[57,8,128]{2,1,0:T(8,128)S(1)} %get-tuple-element.44), channel_id=1, source_target_pairs={{16,0},{24,8},{0,16},{8,24},{17,1},{25,9},{1,17},{9,25},{18,2},{26... | collective-permute-start | bytes 700424 | tf_op jit(solution)/shard_map/ppermute | solution.py:658
  26.3 27.3 %collective-permute-start.4 = (f32[57,8,128]{2,1,0:T(8,128)S(1)}, f32[57,8,128]{2,1,0:T(8,128)S(1)}, u32[]{:S(2)}, u32[]{:S(2)}) collective-permute-start(f32[57,8,128]{2,1,0:T(8,128)S(1)} %get-tuple-element.45), channel_id=1, source_target_pairs={{8,0},{16,8},{24,16},{0,24},{9,1},{17,9},{25,17},{1,25},{10,2},{18... | collective-permute-start | bytes 700424 | tf_op jit(solution)/shard_map/ppermute | solution.py:658
  27.7 15.9 %copy-start.4 = (f32[16]{0:T(128)S(1)}, f32[16]{0:T(128)}, u32[]{:S(2)}) copy-start(f32[16]{0:T(128)} %constant.9.clone.table_ref) | copy-start | bytes 196
  28.5 38.3 %copy-start.3 = (f32[12,8,128]{2,1,0:T(8,128)S(1)}, f32[12,8,128]{2,1,0:T(8,128)}, u32[]{:S(2)}) copy-start(f32[12,8,128]{2,1,0:T(8,128)} %constant.10.clone.coef_ref) | copy-start | bytes 147460
  56.0 10.5 %collective-permute-start.9 = (f32[10,5,16,128]{3,2,1,0:T(8,128)S(1)}, f32[10,5,16,128]{3,2,1,0:T(8,128)S(1)}, u32[]{:S(2)}, u32[]{:S(2)}) collective-permute-start(f32[10,5,16,128]{3,2,1,0:T(8,128)S(1)} %get-tuple-element.52.u0), channel_id=1, source_target_pairs={{1,0},{2,1},{3,2},{4,3},{5,4},{6,5},{7,6},{0,7},{9,8},{10,9},{11,1... | collective-permute-start | bytes 1228808 | tf_op jit(solution)/shard_map/ppermute | solution.py:658
  56.5 10.3 %collective-permute-start.8 = (f32[10,5,16,128]{3,2,1,0:T(8,128)S(1)}, f32[10,5,16,128]{3,2,1,0:T(8,128)S(1)}, u32[]{:S(2)}, u32[]{:S(2)}) collective-permute-start(f32[10,5,16,128]{3,2,1,0:T(8,128)S(1)} %get-tuple-element.53.u3), channel_id=1, source_target_pairs={{7,0},{0,1},{1,2},{2,3},{3,4},{4,5},{5,6},{6,7},{15,8},{8,9},{9,10... | collective-permute-start | bytes 1228808 | tf_op jit(solution)/shard_map/ppermute | solution.py:658
  57.8 15.6 %collective-permute-start.13 = (f32[50,8,128]{2,1,0:T(8,128)S(1)}, f32[50,8,128]{2,1,0:T(8,128)S(1)}, u32[]{:S(2)}, u32[]{:S(2)}) collective-permute-start(f32[50,8,128]{2,1,0:T(8,128)S(1)} %get-tuple-element.62), channel_id=1, source_target_pairs={{24,0},{0,8},{8,16},{16,24},{25,1},{1,9},{9,17},{17,25},{26,2},{2,... | collective-permute-start | bytes 614408 | tf_op jit(solution)/shard_map/ppermute | solution.py:658
  57.8 18.1 %collective-permute-start.14 = (f32[50,8,128]{2,1,0:T(8,128)S(1)}, f32[50,8,128]{2,1,0:T(8,128)S(1)}, u32[]{:S(2)}, u32[]{:S(2)}) collective-permute-start(f32[50,8,128]{2,1,0:T(8,128)S(1)} %get-tuple-element.63), channel_id=1, source_target_pairs={{16,0},{24,8},{0,16},{8,24},{17,1},{25,9},{1,17},{9,25},{18,2},{26... | collective-permute-start | bytes 614408 | tf_op jit(solution)/shard_map/ppermute | solution.py:658
  59.0 27.3 %collective-permute-start.15 = (f32[50,8,128]{2,1,0:T(8,128)S(1)}, f32[50,8,128]{2,1,0:T(8,128)S(1)}, u32[]{:S(2)}, u32[]{:S(2)}) collective-permute-start(f32[50,8,128]{2,1,0:T(8,128)S(1)} %get-tuple-element.64), channel_id=1, source_target_pairs={{8,0},{16,8},{24,16},{0,24},{9,1},{17,9},{25,17},{1,25},{10,2},{18... | collective-permute-start | bytes 614408 | tf_op jit(solution)/shard_map/ppermute | solution.py:658
  72.1 17.0 %collective-permute-start.10 = (f32[50,8,128]{2,1,0:T(8,128)S(1)}, f32[50,8,128]{2,1,0:T(8,128)S(1)}, u32[]{:S(2)}, u32[]{:S(2)}) collective-permute-start(f32[50,8,128]{2,1,0:T(8,128)S(1)} %get-tuple-element.58), channel_id=1, source_target_pairs={{24,0},{0,8},{8,16},{16,24},{25,1},{1,9},{9,17},{17,25},{26,2},{2,... | collective-permute-start | bytes 614408 | tf_op jit(solution)/shard_map/ppermute | solution.py:658
  72.2 21.0 %collective-permute-start.11 = (f32[50,8,128]{2,1,0:T(8,128)S(1)}, f32[50,8,128]{2,1,0:T(8,128)S(1)}, u32[]{:S(2)}, u32[]{:S(2)}) collective-permute-start(f32[50,8,128]{2,1,0:T(8,128)S(1)} %get-tuple-element.59), channel_id=1, source_target_pairs={{16,0},{24,8},{0,16},{8,24},{17,1},{25,9},{1,17},{9,25},{18,2},{26... | collective-permute-start | bytes 614408 | tf_op jit(solution)/shard_map/ppermute | solution.py:658
  73.5 21.6 %collective-permute-start.12 = (f32[50,8,128]{2,1,0:T(8,128)S(1)}, f32[50,8,128]{2,1,0:T(8,128)S(1)}, u32[]{:S(2)}, u32[]{:S(2)}) collective-permute-start(f32[50,8,128]{2,1,0:T(8,128)S(1)} %get-tuple-element.60), channel_id=1, source_target_pairs={{8,0},{16,8},{24,16},{0,24},{9,1},{17,9},{25,17},{1,25},{10,2},{18... | collective-permute-start | bytes 614408 | tf_op jit(solution)/shard_map/ppermute | solution.py:658
where the time goes:
time: 96.4 us; the launch traced here: 96.2 us
  waiting for transfers between devices  51.3 us (53%)
  Pallas kernels  25.9 us (27%)
  starting transfers between devices  16.7 us (17%)
  local copies, waits for them, and re-layouts  2.24 us (2%)
    ppermute x16, waiting for transfers between devices, shifted(): lax.ppermute(block, axis, [((i - distance) % count, i) for i in range(cou...  51.3 us
    pallas_call x8, Pallas kernels, call(): pl.pallas_call(kernel, out_shape=[f32(*shape) for _, shape in outs], in_s...  25.9 us
    ppermute x16, starting transfers between devices, shifted(): lax.ppermute(block, axis, [((i - distance) % count, i) for i in range(cou...  16.7 us
    unnamed x10, local copies, waits for them, and re-layouts  2.24 us
  transfers between devices with their start and end apart: 16, of which 13 were waited for; matrix products, arithmetic and copies ran while one was open for 0% of the time, Pallas kernels for 17%

commit v1 on v0

--- a/solution.py
+++ b/solution.py
@@ -214,12 +214,13 @@
     return result
 
 
-def volume_tile(t, states, targets, coef_ref, start, emit):
+def volume_tile(t, states, targets, coef_ref, start, emit, halves=(0, 1)):
     slot = sublanes() % 4
     state, prim = {}, {}
     for a, ref in states.items():
-        for r in range(2):
-            state[a, r] = load_state(ref, t, slice(8 * r, 8 * r + 8))
+        for r in halves:
+            rows = slice(8 * r, 8 * r + 8) if ref.shape[2] == 16 else slice(0, 8)
+            state[a, r] = load_state(ref, t, rows)
             prim[a, r] = primitive(state[a, r])
 
     def flux(a, r, v, direction):
@@ -227,7 +228,7 @@
 
     for v in range(5):
         total = {}
-        for r in range(2):
+        for r in halves:
             column = {a: flux(a, r, v, 0) for a in states}
             for a in targets:
                 value = start(v, a, r)
@@ -242,7 +243,7 @@
                 for r in range(2):
                     for k in range(4):
                         total[a, r] = total[a, r] - coef_ref[4 * r + k] * parts[k]
-            for r in range(2):
+            for r in halves:
                 acc = total[a, r]
                 if whole:
                     along = flux(a, r, v, 2)
@@ -254,18 +255,27 @@
                 emit(v, a, r, acc)
 
 
-def coefficient_table():
-    table = np.zeros((12, 8, 128), np.float32)
-    for s in range(8):
-        group, c = divmod(s, 4)
+def sublane_column(values):
+    row = sublanes()
+    block = jnp.full(VREG, float(values[0]), jnp.float32)
+    for s in range(1, 8):
+        if values[s] != values[s - 1]:
+            block = jnp.where(row >= s, float(values[s]), block)
+    return block
+
+
+def fill_coefficients(coef_ref):
+    table = np.zeros((12, 8), np.float32)
+    for row in range(8):
+        group, c = divmod(row, 4)
         for r in range(2):
-            b = 2 * r + group
             for k in range(4):
                 source = 2 * (k // 2) + (group if k % 2 == 0 else 1 - group)
-                table[4 * r + k, s, :] = DERIV[b, source]
+                table[4 * r + k, row] = DERIV[2 * r + group, source]
         for shift in range(4):
-            table[8 + shift, s, :] = DERIV[c, (c - shift) % 4]
-    return table
+            table[8 + shift, row] = DERIV[c, (c - shift) % 4]
+    for i in range(12):
+        coef_ref[i] = sublane_column(table[i])
 
 
 def y_face_tile(u_ref, py_ref, r_ref, which, t):
@@ -348,6 +358,7 @@
     ]
 
 
+HALF_ROWS = 25
 PACK_ROWS = 50
 HALO_ROWS = 57
 
@@ -376,7 +387,7 @@
     return halos
 
 
-def pack_message(load, quarter, out_ref):
+def pack_message(load, quarter, put):
     lane = lanes()
     low = lane < 64
     lower = sublanes() < 4
@@ -388,39 +399,54 @@
     over = lax.rem(base + 3, 10)
     below_shift = 80 - 64 * odd
     above_shift = 64 - 64 * odd
-    halos = []
-    for n in range(10):
-        top = [load(n, 0, base + i) for i in range(3)]
-        bottom = [load(n, 1, base + i) for i in range(3)]
-        turned = [[pltpu.roll(x, shift, 1) for x in half] for half in (top, bottom)]
+    halos = [None] * 10
+    for v in range(5):
+        tops = []
         for r in range(2):
-            out_ref[5 * n + 2 * r] = jnp.where(keep, turned[r][0], turned[r][1])
-            out_ref[5 * n + 2 * r + 1] = jnp.where(keep, turned[r][1], turned[r][2])
-        out_ref[5 * n + 4] = jnp.where(low, turned[0][2], pltpu.roll(bottom[2], above_shift, 1))
-        below = jnp.where(
-            lane < below_shift,
-            pltpu.roll(load(n, 1, under), below_shift, 1),
-            pltpu.roll(bottom[0], below_shift, 1),
-        )
-        above = jnp.where(
-            lane < above_shift,
-            pltpu.roll(top[2], above_shift, 1),
-            pltpu.roll(load(n, 0, over), above_shift, 1),
-        )
-        halos.append(jnp.where(lower, above, below))
+            blocks = [[load(which, v, r, base + i) for i in range(3)] for which in range(2)]
+            turned = [[pltpu.roll(x, shift, 1) for x in half] for half in blocks]
+            first = (5 * r + v) * 5
+            for which in range(2):
+                put(first + 2 * which, jnp.where(keep, turned[which][0], turned[which][1]))
+                put(first + 2 * which + 1, jnp.where(keep, turned[which][1], turned[which][2]))
+            put(first + 4, jnp.where(low, turned[0][2], pltpu.roll(blocks[1][2], above_shift, 1)))
+            tops.append(blocks)
+        for which in range(2):
+            below = jnp.where(
+                lane < below_shift,
+                pltpu.roll(load(which, v, 1, under), below_shift, 1),
+                pltpu.roll(tops[1][which][0], below_shift, 1),
+            )
+            above = jnp.where(
+                lane < above_shift,
+                pltpu.roll(tops[0][which][2], above_shift, 1),
+                pltpu.roll(load(which, v, 0, over), above_shift, 1),
+            )
+            halos[2 * v + which] = jnp.where(lower, above, below)
     for i, block in enumerate(pack_halo_parts(halos)):
-        out_ref[PACK_ROWS + i] = block
+        put(PACK_ROWS + i, block)
 
 
 def rate_loader(r_ref):
-    return lambda n, r, t: r_ref[t, n, 8 * r : 8 * r + 8, :]
+    return lambda which, v, r, t: r_ref[t, v * 2 + which, 8 * r : 8 * r + 8, :]
+
+
+def writer(*refs):
+    def put(row, block):
+        for ref in refs:
+            if row < ref.shape[0]:
+                ref[row] = block
+                return
+            row -= ref.shape[0]
+
+    return put
 
 
 def start_rows(v, a, r, t):
     return pl.ds(((v * 4 + a) * 16 + 8 * r) * 10 + t, 8, stride=10)
 
 
-def front_kernel(rank_ref, coef_ref, start_hbm, offset_hbm, u0, u1, u2, u3, r_ref, m1, m2, m3, start_ref, offset_ref, pz_ref, py1, py2, sems):
+def front_kernel(rank_ref, start_hbm, offset_hbm, u0, u1, u2, u3, r_ref, m1, m2, m3, start_ref, offset_ref, pz_ref, py1, py2, coef_ref, sems):
     copies = []
     for v in range(5):
         rows = pl.ds(640 * v, 640)
@@ -432,18 +458,16 @@
             copy.start()
         copies.append(pair)
     states = {0: u0, 1: u1, 2: u2, 3: u3}
+    fill_coefficients(coef_ref)
     for v in range(5):
         for copy in copies[v]:
             copy.wait()
+        rows = slice(640 * v, 640 * v + 640)
+        offset_ref[rows, :] = offset_ref[rows, :] + start_ref[rows, :]
         for a in range(4):
-
-            def one_tile(t, carry):
+            for t in range(TILES):
                 for r in range(2):
-                    rows = start_rows(v, a, r, t)
-                    states[a][t, v, 8 * r : 8 * r + 8, :] = start_ref[rows, :] + offset_ref[rows, :]
-                return carry
-
-            lax.fori_loop(0, TILES, one_tile, 0, unroll=True)
+                    states[a][t, v, 8 * r : 8 * r + 8, :] = offset_ref[start_rows(v, a, r, t), :]
     z_partners((u1, u2), pz_ref)
     y_partners(u1, py1)
     y_partners(u2, py2)
@@ -454,10 +478,11 @@
 
     lax.fori_loop(0, TILES, one_tile, 0)
     for d, out in ((1, m1), (2, m2), (3, m3)):
-        pack_message(rate_loader(r_ref), lax.rem(rank_ref[0] + d, 4), out)
-
-
-def edge_kernel(rank_ref, coef_ref, u0, u1, u2, u3, left_ref, right_ref, m1, m2, m3, r_ref, pz_ref, py0, py3):
+        pack_message(rate_loader(r_ref), lax.rem(rank_ref[0] + d, 4), writer(out))
+
+
+def edge_kernel(rank_ref, u0, u1, u2, u3, left_ref, right_ref, t1, t2, t3, m1, m2, m3, r_ref, pz_ref, py0, py3, coef_ref):
+    fill_coefficients(coef_ref)
     z_partners((u0, u3), pz_ref)
     y_partners(u0, py0)
     y_partners(u3, py3)
@@ -470,73 +495,79 @@
         return carry
 
     lax.fori_loop(0, TILES, one_tile, 0)
-    for d, out in ((1, m1), (2, m2), (3, m3)):
-        pack_message(rate_loader(r_ref), lax.rem(rank_ref[0] + d, 4), out)
+    for d, outs in ((1, (t1, m1)), (2, (t2, m2)), (3, (t3, m3))):
+        pack_message(rate_loader(r_ref), lax.rem(rank_ref[0] + d, 4), writer(*outs))
 
 
 def own_kernel(rank_ref, start_ref, mid_ref, edge_ref, start_mid, start_edge, own_mid, own_edge):
     rank = rank_ref[0]
     for pair, rates, start_out, own_out in (((1, 2), mid_ref, start_mid, own_mid), ((0, 3), edge_ref, start_edge, own_edge)):
 
-        def load(n, r, t):
-            return start_ref[start_rows(n // 2, pair[n % 2], r, t), :]
-
-        pack_message(load, rank, start_out)
-        pack_message(rate_loader(rates), rank, own_out)
-
-
-def assemble(rank_ref, table_ref, start_ref, rates, states, halos):
+        def load(which, v, r, t):
+            return start_ref[start_rows(v, pair[which], r, t), :]
+
+        pack_message(load, rank, writer(start_out))
+        pack_message(rate_loader(rates), rank, writer(own_out))
+
+
+def assemble(rank_ref, table_ref, start_ref, rates, skipped, halves, states, halos=None):
     rank = rank_ref[0]
     weight = [
         [table_ref[m * 4 + lax.rem(rank + 4 - d, 4)] for d in range(4)] for m in range(4)
     ]
 
     def node_state(m, row):
-        total = start_ref[row]
-        for d in range(4):
-            total = total + weight[m][d] * rates[d][row]
+        total = start_ref[row] + weight[m][0] * rates[0][row]
+        for d in range(1, 4):
+            total = total + weight[m][d] * rates[d][row - skipped]
         return total
 
     def one_variable(v, carry):
-        for which in range(2):
-            first = 10 * v + 5 * which
+        for r in halves:
+            first = (5 * r + v) * 5
             for pair in range(2):
                 pieces = [[node_state(2 * pair + half, first + i) for i in range(5)] for half in range(2)]
                 tiles = unpack_pair(*pieces)
                 for i in range(5):
-                    for r in range(2):
-                        states[which][5 * pair + i, v, 8 * r : 8 * r + 8, :] = tiles[i][r]
+                    for which in range(2):
+                        ref = states[which]
+                        rows = slice(8 * r, 8 * r + 8) if ref.shape[2] == 16 else slice(0, 8)
+                        ref[5 * pair + i, v, rows, :] = tiles[i][which]
         return carry
 
     lax.fori_loop(0, 5, one_variable, 0)
-    for m in range(4):
-        blocks = unpack_halo_parts([node_state(m, PACK_ROWS + i) for i in range(7)])
-        for n in range(10):
-            halos[n % 2][m, n // 2] = blocks[n]
-
-
-def send_increments(rank_ref, table_ref, r_ref, outs):
+    if halos is not None:
+        for m in range(4):
+            blocks = unpack_halo_parts([node_state(m, PACK_ROWS + i) for i in range(7)])
+            for n in range(10):
+                halos[n % 2][m, n // 2] = blocks[n]
+
+
+def send_increments(rank_ref, table_ref, r_ref, halves, outs):
     rank = rank_ref[0]
     weight = [[table_ref[lax.rem(rank + d, 4) * 4 + j] for j in range(4)] for d in range(4)]
 
-    def one_block(n, carry):
-        pieces = []
-        for pair in range(2):
-            tiles = [[r_ref[5 * pair + i, n, 8 * r : 8 * r + 8, :] for r in range(2)] for i in range(5)]
-            pieces.extend(pack_pair(tiles))
-        for d in range(4):
-            for i in range(5):
-                total = weight[d][0] * pieces[0][i]
-                for j in range(1, 4):
-                    total = total + weight[d][j] * pieces[j][i]
-                outs[d][5 * n + i] = total
-        return carry
-
-    lax.fori_loop(0, 10, one_block, 0)
-
-
-def middle_kernel(rank_ref, table_ref, coef_ref, start_ref, q0, q1, q2, q3, mid_ref, edge_ref, u1, u2, h1, h2, pz_ref, py1, py2):
-    assemble(rank_ref, table_ref, start_ref, (q0, q1, q2, q3), (u1, u2), (h1, h2))
+    def one_variable(v, carry):
+        for place, r in enumerate(halves):
+            rows = slice(8 * r, 8 * r + 8) if r_ref.shape[2] == 16 else slice(0, 8)
+            pieces = []
+            for pair in range(2):
+                tiles = [[r_ref[5 * pair + i, 2 * v + which, rows, :] for which in range(2)] for i in range(5)]
+                pieces.extend(pack_pair(tiles))
+            for d in range(4):
+                for i in range(5):
+                    total = weight[d][0] * pieces[0][i]
+                    for j in range(1, 4):
+                        total = total + weight[d][j] * pieces[j][i]
+                    outs[d][(5 * place + v) * 5 + i] = total
+        return carry
+
+    lax.fori_loop(0, 5, one_variable, 0)
+
+
+def middle_kernel(rank_ref, table_ref, start_ref, q0, q1, q2, q3, mid_ref, edge_ref, u1, u2, h1, h2, pz_ref, py1, py2, coef_ref):
+    fill_coefficients(coef_ref)
+    assemble(rank_ref, table_ref, start_ref, (q0, q1, q2, q3), 0, (0, 1), (u1, u2), (h1, h2))
     z_partners((u1, u2), pz_ref)
     y_partners(u1, py1, h1)
     y_partners(u2, py2, h2)
@@ -549,24 +580,35 @@
     lax.fori_loop(0, TILES, one_tile, 0)
 
 
-def join_kernel(rank_ref, table_ref, start_ref, q0, q1, q2, q3, mid_ref, u0, u3, h0, h3, o0, o1, o2, o3, r_ref):
-    assemble(rank_ref, table_ref, start_ref, (q0, q1, q2, q3), (u0, u3), (h0, h3))
-
+def complete_middle(rank_ref, table_ref, mid_ref, u0, u3, r, r_ref, outs):
     def one_tile(t, carry):
-        def start(v, a, r):
-            return mid_ref[t, v * 2 + a - 1, 8 * r : 8 * r + 8, :]
-
-        def emit(v, a, r, value):
-            r_ref[t, v * 2 + a - 1, 8 * r : 8 * r + 8, :] = value
-
-        volume_tile(t, {0: u0, 3: u3}, {1: False, 2: False}, None, start, emit)
+        def start(v, a, half):
+            return mid_ref[t, v * 2 + a - 1, 8 * half : 8 * half + 8, :]
+
+        def emit(v, a, half, value):
+            r_ref[t, v * 2 + a - 1] = value
+
+        volume_tile(t, {0: u0, 3: u3}, {1: False, 2: False}, None, start, emit, (r,))
         return carry
 
     lax.fori_loop(0, TILES, one_tile, 0)
-    send_increments(rank_ref, table_ref, r_ref, (o0, o1, o2, o3))
-
-
-def last_kernel(rank_ref, table_ref, coef_ref, u0, u3, h0, h3, partial_ref, left_ref, right_ref, o0, o1, o2, o3, r_ref, pz_ref, py0, py3):
+    send_increments(rank_ref, table_ref, r_ref, (r,), outs)
+
+
+def upper_kernel(rank_ref, table_ref, start_ref, q0, q1, q2, q3, mid_ref, w0, w3, o0, o1, o2, o3, r_ref):
+    assemble(rank_ref, table_ref, start_ref, (q0, q1, q2, q3), 0, (0,), (w0, w3))
+    complete_middle(rank_ref, table_ref, mid_ref, w0, w3, 0, r_ref, (o0, o1, o2, o3))
+
+
+def lower_kernel(rank_ref, table_ref, start_ref, q0, q1, q2, q3, mid_ref, w0, w3, u0, u3, h0, h3, o0, o1, o2, o3, r_ref):
+    assemble(rank_ref, table_ref, start_ref, (q0, q1, q2, q3), HALF_ROWS, (1,), (u0, u3), (h0, h3))
+    u0[:, :, 0:8, :] = w0[...]
+    u3[:, :, 0:8, :] = w3[...]
+    complete_middle(rank_ref, table_ref, mid_ref, u0, u3, 1, r_ref, (o0, o1, o2, o3))
+
+
+def last_inner_kernel(u0, u3, h0, h3, partial_ref, r_ref, pz_ref, py0, py3, coef_ref):
+    fill_coefficients(coef_ref)
     z_partners((u0, u3), pz_ref)
     y_partners(u0, py0, h0)
     y_partners(u3, py3, h3)
@@ -574,29 +616,42 @@
 
     def one_tile(t, carry):
         rates_tile(t, states, (0, 3), (0, 3), pz_ref, (py0, py3), r_ref, coef_ref, added=partial_ref)
+        return carry
+
+    lax.fori_loop(0, TILES, one_tile, 0)
+
+
+def last_outer_kernel(rank_ref, table_ref, u0, u3, inner_ref, left_ref, right_ref, o0, o1, o2, o3, r_ref):
+    def one_tile(t, carry):
+        r_ref[t] = inner_ref[t]
         x_face_tile(u0, left_ref, r_ref, 0, t)
         x_face_tile(u3, right_ref, r_ref, 1, t)
         return carry
 
     lax.fori_loop(0, TILES, one_tile, 0)
-    send_increments(rank_ref, table_ref, r_ref, (o0, o1, o2, o3))
-
-
-def finish(rank_ref, pieces, out_hbm, order_ref, stage_ref, sems, pair):
+    send_increments(rank_ref, table_ref, r_ref, (0, 1), (o0, o1, o2, o3))
+
+
+def finish(rank_ref, halves, out_hbm, order_ref, stage_ref, sems, pair):
     rank = rank_ref[0]
-    for d in range(4):
-        slot = lax.rem(rank + 4 - d, 4)
-        order_ref[slot] = pieces[d][...]
+    count = PACK_ROWS // len(halves)
+    for place, pieces in enumerate(halves):
+        for d in range(4):
+            slot = lax.rem(rank + 4 - d, 4)
+            order_ref[slot, count * place : count * (place + 1)] = pieces[d][...]
     copies = []
     for v in range(5):
+        for r in range(2):
+            for half in range(2):
+                first = (5 * r + v) * 5
+                blocks = [[order_ref[2 * half + k, first + i] for i in range(5)] for k in range(2)]
+                tiles = unpack_pair(*blocks)
+                for i in range(5):
+                    for which in range(2):
+                        row = (v * 2 + which) * 160 + 80 * r + 5 * half + i
+                        stage_ref[pl.ds(row, 8, stride=10), :] = tiles[i][which]
         for which in range(2):
             n = v * 2 + which
-            for half in range(2):
-                blocks = [[order_ref[2 * half + k, 5 * n + i] for i in range(5)] for k in range(2)]
-                tiles = unpack_pair(*blocks)
-                for i in range(5):
-                    for r in range(2):
-                        stage_ref[pl.ds(n * 160 + 80 * r + 5 * half + i, 8, stride=10), :] = tiles[i][r]
             copy = pltpu.make_async_copy(
                 stage_ref.at[pl.ds(n * 160, 160)],
                 out_hbm.at[pl.ds((v * 4 + pair[which]) * 160, 160)],
@@ -608,12 +663,12 @@
         copy.wait()
 
 
-def finish_middle(rank_ref, q0, q1, q2, q3, out_hbm, order_ref, stage_ref, sems):
-    finish(rank_ref, (q0, q1, q2, q3), out_hbm, order_ref, stage_ref, sems, (1, 2))
+def finish_middle(rank_ref, a0, a1, a2, a3, b0, b1, b2, b3, out_hbm, order_ref, stage_ref, sems):
+    finish(rank_ref, ((a0, a1, a2, a3), (b0, b1, b2, b3)), out_hbm, order_ref, stage_ref, sems, (1, 2))
 
 
 def finish_edge(rank_ref, q0, q1, q2, q3, before_hbm, out_hbm, order_ref, stage_ref, sems):
-    finish(rank_ref, (q0, q1, q2, q3), out_hbm, order_ref, stage_ref, sems, (0, 3))
+    finish(rank_ref, ((q0, q1, q2, q3),), out_hbm, order_ref, stage_ref, sems, (0, 3))
 
 
 def f32(*shape):
@@ -627,13 +682,17 @@
 FLAT = (3200, 128)
 MESSAGE = (HALO_ROWS, 8, 128)
 PIECE = (PACK_ROWS, 8, 128)
+UPPER = (HALF_ROWS, 8, 128)
+LOWER = (HALO_ROWS - HALF_ROWS, 8, 128)
+HALF = (TILES, 10, 8, 128)
+COEF = (12, 8, 128)
 
 
 def call(kernel, outs, args, scratch=(), flops=0, aliases=None):
     place = {
         "s": pl.BlockSpec(memory_space=pltpu.SMEM),
         "v": pl.BlockSpec(memory_space=pltpu.VMEM),
-        "h": pl.BlockSpec(memory_space=pl.ANY),
+        "h": pl.BlockSpec(memory_space=pltpu.HBM),
     }
     moved = sum(4 * math.prod(a.shape) for _, a in args)
     moved += sum(4 * math.prod(shape) for _, shape in outs)
@@ -648,7 +707,7 @@
         ],
         input_output_aliases=aliases or {},
         compiler_params=pltpu.CompilerParams(vmem_limit_bytes=VMEM_LIMIT),
-        cost_estimate=pl.CostEstimate(flops=flops, bytes_accessed=moved, transcendentals=0),
+        cost_estimate=pl.CostEstimate(flops=flops, bytes_accessed=1, transcendentals=0),
     )(*[a for _, a in args])
     return result
 
@@ -671,24 +730,24 @@
     offset_flat = node_offset.reshape(FLAT)
     rank = ("s", lax.axis_index("node").astype(jnp.int32).reshape(1))
     table = ("s", jnp.asarray(QUAD.reshape(16)))
-    coef = ("v", jnp.asarray(coefficient_table()))
 
     u0, u1, u2, u3, mid, *sent = call(
         front_kernel,
         v(TRACE, TRACE, TRACE, TRACE, RATE, MESSAGE, MESSAGE, MESSAGE),
-        [rank, coef, ("h", start_flat), ("h", offset_flat)],
-        scratch=[FLAT, FLAT, TRACE, SIDE, SIDE, (10,)],
+        [rank, ("h", start_flat), ("h", offset_flat)],
+        scratch=[FLAT, FLAT, TRACE, SIDE, SIDE, COEF, (10,)],
     )
     got_mid = exchange(sent)
     left = shifted(u3, "space", 1)
     right = shifted(u0, "space", -1)
     *sent, edge = call(
         edge_kernel,
-        v(MESSAGE, MESSAGE, MESSAGE, RATE),
-        [rank, coef] + v(u0, u1, u2, u3, left, right),
-        scratch=[TRACE, SIDE, SIDE],
-    )
-    got_edge = exchange(sent)
+        v(UPPER, UPPER, UPPER, LOWER, LOWER, LOWER, RATE),
+        [rank] + v(u0, u1, u2, u3, left, right),
+        scratch=[TRACE, SIDE, SIDE, COEF],
+    )
+    got_upper = exchange(sent[:3])
+    got_lower = exchange(sent[3:])
     start_mid, start_edge, own_mid, own_edge = call(
         own_kernel,
         v(MESSAGE, MESSAGE, MESSAGE, MESSAGE),
@@ -697,30 +756,43 @@
     mid, edge = call(
         middle_kernel,
         v(RATE, RATE),
-        [rank, table, coef] + v(start_mid, own_mid, *got_mid),
-        scratch=[TRACE, TRACE, HALO, HALO, TRACE, SIDE, SIDE],
-    )
-    u0, u3, h0, h3, own_mid, *sent = call(
-        join_kernel,
-        v(TRACE, TRACE, HALO, HALO, PIECE, PIECE, PIECE, PIECE),
-        [rank, table] + v(start_edge, own_edge, *got_edge, mid),
-        scratch=[RATE],
-    )
-    got_mid = exchange(sent)
+        [rank, table] + v(start_mid, own_mid, *got_mid),
+        scratch=[TRACE, TRACE, HALO, HALO, TRACE, SIDE, SIDE, COEF],
+    )
+    w0, w3, own_upper, *sent = call(
+        upper_kernel,
+        v(SIDE, SIDE, UPPER, UPPER, UPPER, UPPER),
+        [rank, table] + v(start_edge, own_edge, *got_upper, mid),
+        scratch=[HALF],
+    )
+    got_upper = exchange(sent)
+    u0, u3, h0, h3, own_lower, *sent = call(
+        lower_kernel,
+        v(TRACE, TRACE, HALO, HALO, UPPER, UPPER, UPPER, UPPER),
+        [rank, table] + v(start_edge, own_edge, *got_lower, mid, w0, w3),
+        scratch=[HALF],
+    )
+    got_lower = exchange(sent)
     left = shifted(u3, "space", 1)
     right = shifted(u0, "space", -1)
+    (inner,) = call(
+        last_inner_kernel,
+        v(RATE),
+        v(u0, u3, h0, h3, edge),
+        scratch=[TRACE, SIDE, SIDE, COEF],
+    )
     own_edge, *sent = call(
-        last_kernel,
+        last_outer_kernel,
         v(PIECE, PIECE, PIECE, PIECE),
-        [rank, table, coef] + v(u0, u3, h0, h3, edge, left, right),
-        scratch=[RATE, TRACE, SIDE, SIDE],
+        [rank, table] + v(u0, u3, inner, left, right),
+        scratch=[RATE],
     )
     got_edge = exchange(sent)
     finishing = [(4,) + PIECE, (1600, 128), (10,)]
     (result,) = call(
         finish_middle,
         [("h", FLAT)],
-        [rank] + v(own_mid, *got_mid),
+        [rank] + v(own_upper, *got_upper, own_lower, *got_lower),
         scratch=finishing,
     )
     (result,) = call(

time: 96.4 us -> 100 us (1.037); the launches traced: 96.2 us -> 98.5 us
  starting transfers between devices: 16.7 us -> 20.2 us
  waiting for transfers between devices: 51.3 us -> 49.9 us
    ppermute x16 -> x22, starting transfers between devices: 16.7 us -> 20.2 us  [shifted(): lax.ppermute(block, axis, [((i - distance) % count, i) for i in range(cou...]
    ppermute x16 -> x22, waiting for transfers between devices: 51.3 us -> 49.9 us  [shifted(): lax.ppermute(block, axis, [((i - distance) % count, i) for i in range(cou...]
    pallas_call x8 -> x10, Pallas kernels: 25.9 us -> 26.8 us  [call(): pl.pallas_call(kernel, out_shape=[f32(*shape) for _, shape in outs], in_s...]
    unnamed x10 -> x6, local copies, waits for them, and re-layouts: 2.24 us -> 1.44 us
  transfers between devices with their start and end apart: 16 -> 22, of which waited for: 13 -> 10; matrix products, arithmetic and copies ran while one was open for 0% -> 0% of each run, Pallas kernels for 17% -> 18%
where the time goes in v1:
time: 100 us; the launch traced here: 98.5 us
  waiting for transfers between devices  49.9 us (50%)
  Pallas kernels  26.8 us (27%)
  starting transfers between devices  20.2 us (20%)
  local copies, waits for them, and re-layouts  1.44 us (1%)
    ppermute x22, waiting for transfers between devices, shifted(): lax.ppermute(block, axis, [((i - distance) % count, i) for i in range(cou...  49.9 us
    pallas_call x10, Pallas kernels, call(): pl.pallas_call(kernel, out_shape=[f32(*shape) for _, shape in outs], in_s...  26.8 us
    ppermute x22, starting transfers between devices, shifted(): lax.ppermute(block, axis, [((i - distance) % count, i) for i in range(cou...  20.2 us
  transfers between devices with their start and end apart: 22, of which 10 were waited for; matrix products, arithmetic and copies ran while one was open for 0% of the time, Pallas kernels for 18%

profile of v1, /device:TPU:13, one launch (start us, length us, event | category | flops | bytes accessed | tf_op | source)
XLA Modules:
  0.0 98.5 jit_solution(9798857749615296558)
XLA Ops:
  0.0 1.4 %copy-done = f32[5,4,4,4,1,1280]{5,4,3,2,1,0:T(1,128)S(1)} copy-done((f32[5,4,4,4,1,1280]{5,4,3,2,1,0:T(1,128)S(1)}, f32[5,4,4,4,1,1280]{5,4,3,2,1,0:T(1,128)}, u32[]{:S(2)}) %copy-start) | copy-done | bytes 1638424
  1.4 5.9 %shard_map.37 = (f32[10,5,16,128]{3,2,1,0:T(8,128)S(1)}, f32[10,5,16,128]{3,2,1,0:T(8,128)S(1)}, f32[10,5,16,128]{3,2,1,0:T(8,128)S(1)}, f32[10,5,16,128]{3,2,1,...) custom-call(s32[1]{0:T(128)} %bitcast.rank_ref, ...), custom_call_target="tpu_custom_call" | custom-call | bytes 1 | tf_op jit(solution)/shard_map/pallas_call | solution.py:699
  8.0 1.2 %collective-permute-start = (f32[10,5,16,128]{3,2,1,0:T(8,128)S(1)}, f32[10,5,16,128]{3,2,1,0:T(8,128)S(1)}, u32[]{:S(2)}, u32[]{:S(2)}) collective-permute-start(f32[10,5,16,128]{3,2,1,0:T(8,128)S(1)} %get-tuple-element.48.u3), channel_id=1, source_target_pairs={{7,0},{0,1},{1,2},{2,3},{3,4},{4,5},{5,6},{6,7},{15,8},{8,9},{9,10... | collective-permute-start | bytes 1228808 | tf_op jit(solution)/shard_map/ppermute | solution.py:717
  9.2 1.3 %collective-permute-start.5 = (f32[57,8,128]{2,1,0:T(8,128)S(1)}, f32[57,8,128]{2,1,0:T(8,128)S(1)}, u32[]{:S(2)}, u32[]{:S(2)}) collective-permute-start(f32[57,8,128]{2,1,0:T(8,128)S(1)} %get-tuple-element.57), channel_id=1, source_target_pairs={{24,0},{0,8},{8,16},{16,24},{25,1},{1,9},{9,17},{17,25},{26,2},{2,... | collective-permute-start | bytes 700424 | tf_op jit(solution)/shard_map/ppermute | solution.py:717
  10.5 1.0 %collective-permute-start.6 = (f32[57,8,128]{2,1,0:T(8,128)S(1)}, f32[57,8,128]{2,1,0:T(8,128)S(1)}, u32[]{:S(2)}, u32[]{:S(2)}) collective-permute-start(f32[57,8,128]{2,1,0:T(8,128)S(1)} %get-tuple-element.58), channel_id=1, source_target_pairs={{16,0},{24,8},{0,16},{8,24},{17,1},{25,9},{1,17},{9,25},{18,2},{26... | collective-permute-start | bytes 700424 | tf_op jit(solution)/shard_map/ppermute | solution.py:717
  11.5 1.5 %collective-permute-start.7 = (f32[57,8,128]{2,1,0:T(8,128)S(1)}, f32[57,8,128]{2,1,0:T(8,128)S(1)}, u32[]{:S(2)}, u32[]{:S(2)}) collective-permute-start(f32[57,8,128]{2,1,0:T(8,128)S(1)} %get-tuple-element.59), channel_id=1, source_target_pairs={{8,0},{16,8},{24,16},{0,24},{9,1},{17,9},{25,17},{1,25},{10,2},{18... | collective-permute-start | bytes 700424 | tf_op jit(solution)/shard_map/ppermute | solution.py:717
  13.0 4.6 %collective-permute-done.1.right_ref = f32[10,5,16,128]{3,2,1,0:T(8,128)S(1)} collective-permute-done((f32[10,5,16,128]{3,2,1,0:T(8,128)S(1)}, f32[10,5,16,128]{3,2,1,0:T(8,128)S(1)}, u32[]{:S(2)}, u32[]{:S(2)}) %collective-permute-start.1) | collective-permute-done | bytes 409632 | tf_op jit(solution)/shard_map/ppermute | solution.py:717
  17.6 0.8 collective-permute-done.left_ref
  18.4 4.6 %shard_map.38 = (f32[25,8,128]{2,1,0:T(8,128)S(1)}, f32[25,8,128]{2,1,0:T(8,128)S(1)}, f32[25,8,128]{2,1,0:T(8,128)S(1)}, f32[32,8,128]{2,1,0:T(8,128)S(1)}, f32...) custom-call(s32[1]{0:T(128)} %bitcast.rank_ref, ...), custom_call_target="tpu_custom_call" | custom-call | bytes 1 | tf_op jit(solution)/shard_map/pallas_call | solution.py:699
  23.0 1.3 %collective-permute-start.8 = (f32[25,8,128]{2,1,0:T(8,128)S(1)}, f32[25,8,128]{2,1,0:T(8,128)S(1)}, u32[]{:S(2)}, u32[]{:S(2)}) collective-permute-start(f32[25,8,128]{2,1,0:T(8,128)S(1)} %get-tuple-element.61), channel_id=1, source_target_pairs={{24,0},{0,8},{8,16},{16,24},{25,1},{1,9},{9,17},{17,25},{26,2},{2,... | collective-permute-start | bytes 307208 | tf_op jit(solution)/shard_map/ppermute | solution.py:717
  24.4 1.3 %collective-permute-start.2 = (f32[32,8,128]{2,1,0:T(8,128)S(1)}, f32[32,8,128]{2,1,0:T(8,128)S(1)}, u32[]{:S(2)}, u32[]{:S(2)}) collective-permute-start(f32[32,8,128]{2,1,0:T(8,128)S(1)} %get-tuple-element.52), channel_id=1, source_target_pairs={{24,0},{0,8},{8,16},{16,24},{25,1},{1,9},{9,17},{17,25},{26,2},{2,... | collective-permute-start | bytes 393224 | tf_op jit(solution)/shard_map/ppermute | solution.py:717
  25.7 1.0 collective-permute-start.3
  26.7 4.3 %collective-permute-done.6.q2 = f32[57,8,128]{2,1,0:T(8,128)S(1)} collective-permute-done((f32[57,8,128]{2,1,0:T(8,128)S(1)}, f32[57,8,128]{2,1,0:T(8,128)S(1)}, u32[]{:S(2)}, u32[]{:S(2)}) %collective-permute-start.6) | collective-permute-done | bytes 233504 | tf_op jit(solution)/shard_map/ppermute | solution.py:717
  30.9 9.6 %collective-permute-done.7.q3 = f32[57,8,128]{2,1,0:T(8,128)S(1)} collective-permute-done((f32[57,8,128]{2,1,0:T(8,128)S(1)}, f32[57,8,128]{2,1,0:T(8,128)S(1)}, u32[]{:S(2)}, u32[]{:S(2)}) %collective-permute-start.7) | collective-permute-done | bytes 233504 | tf_op jit(solution)/shard_map/ppermute | solution.py:717
  41.9 4.7 %shard_map.40 = (f32[10,10,16,128]{3,2,1,0:T(8,128)S(1)}, f32[10,10,16,128]{3,2,1,0:T(8,128)S(1)}) custom-call(s32[1]{0:T(128)} %bitcast.rank_ref, f32[16]{0:T(128)S(1)} %copy-done.2, f32[57,8,128]{2,1,0:T(8,128)S(1)} %get-tuple-element.55.start_ref, f32[57,8,128]{2,1,0:T(8,128)S(1)} %get-tuple-element.56.q0, f32[57,8,128]{2,1,0:T(8,128)S(1)} %collective-permute-done.5.q1, ...), custom_call_target="tpu_custom_call" | custom-call | bytes 1 | tf_op jit(solution)/shard_map/pallas_call | solution.py:699
  46.5 4.3 %collective-permute-done.9.q2 = f32[25,8,128]{2,1,0:T(8,128)S(1)} collective-permute-done((f32[25,8,128]{2,1,0:T(8,128)S(1)}, f32[25,8,128]{2,1,0:T(8,128)S(1)}, u32[]{:S(2)}, u32[]{:S(2)}) %collective-permute-start.9) | collective-permute-done | bytes 102432 | tf_op jit(solution)/shard_map/ppermute | solution.py:717
  50.9 1.9 %collective-permute-done.10.q3 = f32[25,8,128]{2,1,0:T(8,128)S(1)} collective-permute-done((f32[25,8,128]{2,1,0:T(8,128)S(1)}, f32[25,8,128]{2,1,0:T(8,128)S(1)}, u32[]{:S(2)}, u32[]{:S(2)}) %collective-permute-start.10) | collective-permute-done | bytes 102432 | tf_op jit(solution)/shard_map/ppermute | solution.py:717
  52.8 1.7 %shard_map.41 = (f32[10,5,8,128]{3,2,1,0:T(8,128)S(1)}, f32[10,5,8,128]{3,2,1,0:T(8,128)S(1)}, f32[25,8,128]{2,1,0:T(8,128)S(1)}, f32[25,8,128]{2,1,0:T(8,128)S(...) custom-call(s32[1]{0:T(128)} %bitcast.rank_ref, f32[16]{0:T(128)S(1)} %copy-done.2, ...), custom_call_target="tpu_custom_call" | custom-call | bytes 1 | tf_op jit(solution)/shard_map/pallas_call | solution.py:699
  54.5 1.9 %shard_map.42 = (f32[10,5,16,128]{3,2,1,0:T(8,128)S(1)}, f32[10,5,16,128]{3,2,1,0:T(8,128)S(1)}, f32[4,5,8,128]{3,2,1,0:T(8,128)S(1)}, f32[4,5,8,128]{3,2,1,0:T(...) custom-call(s32[1]{0:T(128)} %bitcast.rank_ref, ...), custom_call_target="tpu_custom_call" | custom-call | bytes 1 | tf_op jit(solution)/shard_map/pallas_call | solution.py:699
  56.9 1.3 %collective-permute-start.11 = (f32[10,5,16,128]{3,2,1,0:T(8,128)S(1)}, f32[10,5,16,128]{3,2,1,0:T(8,128)S(1)}, u32[]{:S(2)}, u32[]{:S(2)}) collective-permute-start(f32[10,5,16,128]{3,2,1,0:T(8,128)S(1)} %get-tuple-element.67.u3), channel_id=1, source_target_pairs={{7,0},{0,1},{1,2},{2,3},{3,4},{4,5},{5,6},{6,7},{15,8},{8,9},{9,10... | collective-permute-start | bytes 1228808 | tf_op jit(solution)/shard_map/ppermute | solution.py:717
  58.2 1.2 %collective-permute-start.17 = (f32[25,8,128]{2,1,0:T(8,128)S(1)}, f32[25,8,128]{2,1,0:T(8,128)S(1)}, u32[]{:S(2)}, u32[]{:S(2)}) collective-permute-start(f32[25,8,128]{2,1,0:T(8,128)S(1)} %get-tuple-element.77), channel_id=1, source_target_pairs={{16,0},{24,8},{0,16},{8,24},{17,1},{25,9},{1,17},{9,25},{18,2},{26... | collective-permute-start | bytes 307208 | tf_op jit(solution)/shard_map/ppermute | solution.py:717
  59.4 1.5 %collective-permute-start.18 = (f32[25,8,128]{2,1,0:T(8,128)S(1)}, f32[25,8,128]{2,1,0:T(8,128)S(1)}, u32[]{:S(2)}, u32[]{:S(2)}) collective-permute-start(f32[25,8,128]{2,1,0:T(8,128)S(1)} %get-tuple-element.78), channel_id=1, source_target_pairs={{8,0},{16,8},{24,16},{0,24},{9,1},{17,9},{25,17},{1,25},{10,2},{18... | collective-permute-start | bytes 307208 | tf_op jit(solution)/shard_map/ppermute | solution.py:717
  60.9 3.4 %shard_map.43.inner_ref = f32[10,10,16,128]{3,2,1,0:T(8,128)S(1)} custom-call(f32[10,5,16,128]{3,2,1,0:T(8,128)S(1)} %get-tuple-element.66.u0, f32[10,5,16,128]{3,2,1,0:T(8,128)S(1)} %get-tuple-element.67.u3, f32[4,5,8,128]{3,2,1,0:T(8,128)S(1)} %get-tuple-element.68.h0, f32[4,5,8,128]{3,2,1,0:T(8,128)S(1)} %get-tuple-element.69.h3, ...), custom_call_target="tpu_custom_call" | custom-call | bytes 1 | tf_op jit(solution)/shard_map/pallas_call | solution.py:699
  64.3 2.7 %collective-permute-done.12.right_ref = f32[10,5,16,128]{3,2,1,0:T(8,128)S(1)} collective-permute-done((f32[10,5,16,128]{3,2,1,0:T(8,128)S(1)}, f32[10,5,16,128]{3,2,1,0:T(8,128)S(1)}, u32[]{:S(2)}, u32[]{:S(2)}) %collective-permute-start.12) | collective-permute-done | bytes 409632 | tf_op jit(solution)/shard_map/ppermute | solution.py:717
  67.2 1.6 %shard_map.44 = (f32[50,8,128]{2,1,0:T(8,128)S(1)}, f32[50,8,128]{2,1,0:T(8,128)S(1)}, f32[50,8,128]{2,1,0:T(8,128)S(1)}, f32[50,8,128]{2,1,0:T(8,128)S(1)}) custom-call(s32[1]{0:T(128)} %bitcast.rank_ref, f32[16]{0:T(128)S(1)} %copy-done.2, f32[10,5,16,128]{3,2,1,0:T(8,128)S(1)} %get-tuple-element.66.u0, f32[10,5,16,128]{3,2,1,0:T(8,128)S(1)} %get-tuple-element.67.u3, ...), custom_call_target="tpu_custom_call" | custom-call | bytes 1 | tf_op jit(solution)/shard_map/pallas_call | solution.py:699
  68.8 1.3 %collective-permute-start.13 = (f32[50,8,128]{2,1,0:T(8,128)S(1)}, f32[50,8,128]{2,1,0:T(8,128)S(1)}, u32[]{:S(2)}, u32[]{:S(2)}) collective-permute-start(f32[50,8,128]{2,1,0:T(8,128)S(1)} %get-tuple-element.72), channel_id=1, source_target_pairs={{24,0},{0,8},{8,16},{16,24},{25,1},{1,9},{9,17},{17,25},{26,2},{2,... | collective-permute-start | bytes 614408 | tf_op jit(solution)/shard_map/ppermute | solution.py:717
  70.1 2.1 %collective-permute-start.14 = (f32[50,8,128]{2,1,0:T(8,128)S(1)}, f32[50,8,128]{2,1,0:T(8,128)S(1)}, u32[]{:S(2)}, u32[]{:S(2)}) collective-permute-start(f32[50,8,128]{2,1,0:T(8,128)S(1)} %get-tuple-element.73), channel_id=1, source_target_pairs={{16,0},{24,8},{0,16},{8,24},{17,1},{25,9},{1,17},{9,25},{18,2},{26... | collective-permute-start | bytes 614408 | tf_op jit(solution)/shard_map/ppermute | solution.py:717
  72.7 2.1 %collective-permute-start.21 = (f32[25,8,128]{2,1,0:T(8,128)S(1)}, f32[25,8,128]{2,1,0:T(8,128)S(1)}, u32[]{:S(2)}, u32[]{:S(2)}) collective-permute-start(f32[25,8,128]{2,1,0:T(8,128)S(1)} %get-tuple-element.82), channel_id=1, source_target_pairs={{8,0},{16,8},{24,16},{0,24},{9,1},{17,9},{25,17},{1,25},{10,2},{18... | collective-permute-start | bytes 307208 | tf_op jit(solution)/shard_map/ppermute | solution.py:717
  74.9 18.7 %collective-permute-done.20.b2 = f32[25,8,128]{2,1,0:T(8,128)S(1)} collective-permute-done((f32[25,8,128]{2,1,0:T(8,128)S(1)}, f32[25,8,128]{2,1,0:T(8,128)S(1)}, u32[]{:S(2)}, u32[]{:S(2)}) %collective-permute-start.20) | collective-permute-done | bytes 102432 | tf_op jit(solution)/shard_map/ppermute | solution.py:717
  93.6 2.6 %collective-permute-done.21.b3 = f32[25,8,128]{2,1,0:T(8,128)S(1)} collective-permute-done((f32[25,8,128]{2,1,0:T(8,128)S(1)}, f32[25,8,128]{2,1,0:T(8,128)S(1)}, u32[]{:S(2)}, u32[]{:S(2)}) %collective-permute-start.21) | collective-permute-done | bytes 102432 | tf_op jit(solution)/shard_map/ppermute | solution.py:717
  96.2 1.1 %shard_map.45.before_hbm = f32[3200,128]{1,0:T(8,128)} custom-call(s32[1]{0:T(128)} %bitcast.rank_ref, f32[25,8,128]{2,1,0:T(8,128)S(1)} %get-tuple-element.75.a0, f32[25,8,128]{2,1,0:T(8,128)S(1)} %collective-permute-done.16.a1, f32[25,8,128]{2,1,0:T(8,128)S(1)} %collective-permute-done.17.a2, f32[25,8,128]{2,1,0:T(8,128)S(1)} %collective-permute-done.18.a3, ...), custom_call_target="tpu_custom_call" | custom-call | bytes 1 | tf_op jit(solution)/shard_map/pallas_call | solution.py:699
  97.4 1.1 %shard_map.46 = f32[3200,128]{1,0:T(8,128)} custom-call(s32[1]{0:T(128)} %bitcast.rank_ref, f32[50,8,128]{2,1,0:T(8,128)S(1)} %get-tuple-element.71.q0, f32[50,8,128]{2,1,0:T(8,128)S(1)} %collective-permute-done.13.q1, f32[50,8,128]{2,1,0:T(8,128)S(1)} %collective-permute-done.14.q2, ...), custom_call_target="tpu_custom_call", output_to_operand_aliasing={{}: (5, {})} | custom-call | bytes 1 | tf_op jit(solution)/shard_map/pallas_call | solution.py:699
  (28 shorter events, 3.2 us)
Async XLA Ops:
  0.0 1.4 %copy-start = (f32[5,4,4,4,1,1280]{5,4,3,2,1,0:T(1,128)S(1)}, f32[5,4,4,4,1,1280]{5,4,3,2,1,0:T(1,128)}, u32[]{:S(2)}) copy-start(f32[5,4,4,4,1,1280]{5,4,3,2,1,0:T(1,128)} %param.3) | copy-start | bytes 4915204
  7.3 33.7 %copy-start.1 = (f32[5,4,4,4,1,1280]{5,4,3,2,1,0:T(1,128)S(1)}, f32[5,4,4,4,1,1280]{5,4,3,2,1,0:T(1,128)}, u32[]{:S(2)}) copy-start(f32[5,4,4,4,1,1280]{5,4,3,2,1,0:T(1,128)} %param.3) | copy-start | bytes 4915204
  7.3 10.3 %collective-permute-start.1 = (f32[10,5,16,128]{3,2,1,0:T(8,128)S(1)}, f32[10,5,16,128]{3,2,1,0:T(8,128)S(1)}, u32[]{:S(2)}, u32[]{:S(2)}) collective-permute-start(f32[10,5,16,128]{3,2,1,0:T(8,128)S(1)} %get-tuple-element.45.u0), channel_id=1, source_target_pairs={{1,0},{2,1},{3,2},{4,3},{5,4},{6,5},{7,6},{0,7},{9,8},{10,9},{11,1... | collective-permute-start | bytes 1228808 | tf_op jit(solution)/shard_map/ppermute | solution.py:717
  8.0 10.4 %collective-permute-start = (f32[10,5,16,128]{3,2,1,0:T(8,128)S(1)}, f32[10,5,16,128]{3,2,1,0:T(8,128)S(1)}, u32[]{:S(2)}, u32[]{:S(2)}) collective-permute-start(f32[10,5,16,128]{3,2,1,0:T(8,128)S(1)} %get-tuple-element.48.u3), channel_id=1, source_target_pairs={{7,0},{0,1},{1,2},{2,3},{3,4},{4,5},{5,6},{6,7},{15,8},{8,9},{9,10... | collective-permute-start | bytes 1228808 | tf_op jit(solution)/shard_map/ppermute | solution.py:717
  9.2 16.5 %collective-permute-start.5 = (f32[57,8,128]{2,1,0:T(8,128)S(1)}, f32[57,8,128]{2,1,0:T(8,128)S(1)}, u32[]{:S(2)}, u32[]{:S(2)}) collective-permute-start(f32[57,8,128]{2,1,0:T(8,128)S(1)} %get-tuple-element.57), channel_id=1, source_target_pairs={{24,0},{0,8},{8,16},{16,24},{25,1},{1,9},{9,17},{17,25},{26,2},{2,... | collective-permute-start | bytes 700424 | tf_op jit(solution)/shard_map/ppermute | solution.py:717
  10.5 20.4 %collective-permute-start.6 = (f32[57,8,128]{2,1,0:T(8,128)S(1)}, f32[57,8,128]{2,1,0:T(8,128)S(1)}, u32[]{:S(2)}, u32[]{:S(2)}) collective-permute-start(f32[57,8,128]{2,1,0:T(8,128)S(1)} %get-tuple-element.58), channel_id=1, source_target_pairs={{16,0},{24,8},{0,16},{8,24},{17,1},{25,9},{1,17},{9,25},{18,2},{26... | collective-permute-start | bytes 700424 | tf_op jit(solution)/shard_map/ppermute | solution.py:717
  11.5 29.1 %collective-permute-start.7 = (f32[57,8,128]{2,1,0:T(8,128)S(1)}, f32[57,8,128]{2,1,0:T(8,128)S(1)}, u32[]{:S(2)}, u32[]{:S(2)}) collective-permute-start(f32[57,8,128]{2,1,0:T(8,128)S(1)} %get-tuple-element.59), channel_id=1, source_target_pairs={{8,0},{16,8},{24,16},{0,24},{9,1},{17,9},{25,17},{1,25},{10,2},{18... | collective-permute-start | bytes 700424 | tf_op jit(solution)/shard_map/ppermute | solution.py:717
  23.0 17.5 %collective-permute-start.8 = (f32[25,8,128]{2,1,0:T(8,128)S(1)}, f32[25,8,128]{2,1,0:T(8,128)S(1)}, u32[]{:S(2)}, u32[]{:S(2)}) collective-permute-start(f32[25,8,128]{2,1,0:T(8,128)S(1)} %get-tuple-element.61), channel_id=1, source_target_pairs={{24,0},{0,8},{8,16},{16,24},{25,1},{1,9},{9,17},{17,25},{26,2},{2,... | collective-permute-start | bytes 307208 | tf_op jit(solution)/shard_map/ppermute | solution.py:717
  24.4 30.1 %collective-permute-start.2 = (f32[32,8,128]{2,1,0:T(8,128)S(1)}, f32[32,8,128]{2,1,0:T(8,128)S(1)}, u32[]{:S(2)}, u32[]{:S(2)}) collective-permute-start(f32[32,8,128]{2,1,0:T(8,128)S(1)} %get-tuple-element.52), channel_id=1, source_target_pairs={{24,0},{0,8},{8,16},{16,24},{25,1},{1,9},{9,17},{17,25},{26,2},{2,... | collective-permute-start | bytes 393224 | tf_op jit(solution)/shard_map/ppermute | solution.py:717
  25.7 28.8 %collective-permute-start.3 = (f32[32,8,128]{2,1,0:T(8,128)S(1)}, f32[32,8,128]{2,1,0:T(8,128)S(1)}, u32[]{:S(2)}, u32[]{:S(2)}) collective-permute-start(f32[32,8,128]{2,1,0:T(8,128)S(1)} %get-tuple-element.53), channel_id=1, source_target_pairs={{16,0},{24,8},{0,16},{8,24},{17,1},{25,9},{1,17},{9,25},{18,2},{26... | collective-permute-start | bytes 393224 | tf_op jit(solution)/shard_map/ppermute | solution.py:717
  30.9 23.6 %collective-permute-start.4 = (f32[32,8,128]{2,1,0:T(8,128)S(1)}, f32[32,8,128]{2,1,0:T(8,128)S(1)}, u32[]{:S(2)}, u32[]{:S(2)}) collective-permute-start(f32[32,8,128]{2,1,0:T(8,128)S(1)} %get-tuple-element.54), channel_id=1, source_target_pairs={{8,0},{16,8},{24,16},{0,24},{9,1},{17,9},{25,17},{1,25},{10,2},{18... | collective-permute-start | bytes 393224 | tf_op jit(solution)/shard_map/ppermute | solution.py:717
  40.6 10.3 %collective-permute-start.9 = (f32[25,8,128]{2,1,0:T(8,128)S(1)}, f32[25,8,128]{2,1,0:T(8,128)S(1)}, u32[]{:S(2)}, u32[]{:S(2)}) collective-permute-start(f32[25,8,128]{2,1,0:T(8,128)S(1)} %get-tuple-element.62), channel_id=1, source_target_pairs={{16,0},{24,8},{0,16},{8,24},{17,1},{25,9},{1,17},{9,25},{18,2},{26... | collective-permute-start | bytes 307208 | tf_op jit(solution)/shard_map/ppermute | solution.py:717
  40.6 12.2 %collective-permute-start.10 = (f32[25,8,128]{2,1,0:T(8,128)S(1)}, f32[25,8,128]{2,1,0:T(8,128)S(1)}, u32[]{:S(2)}, u32[]{:S(2)}) collective-permute-start(f32[25,8,128]{2,1,0:T(8,128)S(1)} %get-tuple-element.63), channel_id=1, source_target_pairs={{8,0},{16,8},{24,16},{0,24},{9,1},{17,9},{25,17},{1,25},{10,2},{18... | collective-permute-start | bytes 307208 | tf_op jit(solution)/shard_map/ppermute | solution.py:717
  41.0 0.8 copy-start.2
  56.4 10.5 %collective-permute-start.12 = (f32[10,5,16,128]{3,2,1,0:T(8,128)S(1)}, f32[10,5,16,128]{3,2,1,0:T(8,128)S(1)}, u32[]{:S(2)}, u32[]{:S(2)}) collective-permute-start(f32[10,5,16,128]{3,2,1,0:T(8,128)S(1)} %get-tuple-element.66.u0), channel_id=1, source_target_pairs={{1,0},{2,1},{3,2},{4,3},{5,4},{6,5},{7,6},{0,7},{9,8},{10,9},{11,1... | collective-permute-start | bytes 1228808 | tf_op jit(solution)/shard_map/ppermute | solution.py:717
  56.9 10.3 %collective-permute-start.11 = (f32[10,5,16,128]{3,2,1,0:T(8,128)S(1)}, f32[10,5,16,128]{3,2,1,0:T(8,128)S(1)}, u32[]{:S(2)}, u32[]{:S(2)}) collective-permute-start(f32[10,5,16,128]{3,2,1,0:T(8,128)S(1)} %get-tuple-element.67.u3), channel_id=1, source_target_pairs={{7,0},{0,1},{1,2},{2,3},{3,4},{4,5},{5,6},{6,7},{15,8},{8,9},{9,10... | collective-permute-start | bytes 1228808 | tf_op jit(solution)/shard_map/ppermute | solution.py:717
  58.2 11.9 %collective-permute-start.16 = (f32[25,8,128]{2,1,0:T(8,128)S(1)}, f32[25,8,128]{2,1,0:T(8,128)S(1)}, u32[]{:S(2)}, u32[]{:S(2)}) collective-permute-start(f32[25,8,128]{2,1,0:T(8,128)S(1)} %get-tuple-element.76), channel_id=1, source_target_pairs={{24,0},{0,8},{8,16},{16,24},{25,1},{1,9},{9,17},{17,25},{26,2},{2,... | collective-permute-start | bytes 307208 | tf_op jit(solution)/shard_map/ppermute | solution.py:717
  58.2 14.0 %collective-permute-start.17 = (f32[25,8,128]{2,1,0:T(8,128)S(1)}, f32[25,8,128]{2,1,0:T(8,128)S(1)}, u32[]{:S(2)}, u32[]{:S(2)}) collective-permute-start(f32[25,8,128]{2,1,0:T(8,128)S(1)} %get-tuple-element.77), channel_id=1, source_target_pairs={{16,0},{24,8},{0,16},{8,24},{17,1},{25,9},{1,17},{9,25},{18,2},{26... | collective-permute-start | bytes 307208 | tf_op jit(solution)/shard_map/ppermute | solution.py:717
  59.4 12.8 %collective-permute-start.18 = (f32[25,8,128]{2,1,0:T(8,128)S(1)}, f32[25,8,128]{2,1,0:T(8,128)S(1)}, u32[]{:S(2)}, u32[]{:S(2)}) collective-permute-start(f32[25,8,128]{2,1,0:T(8,128)S(1)} %get-tuple-element.78), channel_id=1, source_target_pairs={{8,0},{16,8},{24,16},{0,24},{9,1},{17,9},{25,17},{1,25},{10,2},{18... | collective-permute-start | bytes 307208 | tf_op jit(solution)/shard_map/ppermute | solution.py:717
  67.0 5.8 %collective-permute-start.19 = (f32[25,8,128]{2,1,0:T(8,128)S(1)}, f32[25,8,128]{2,1,0:T(8,128)S(1)}, u32[]{:S(2)}, u32[]{:S(2)}) collective-permute-start(f32[25,8,128]{2,1,0:T(8,128)S(1)} %get-tuple-element.80), channel_id=1, source_target_pairs={{24,0},{0,8},{8,16},{16,24},{25,1},{1,9},{9,17},{17,25},{26,2},{2,... | collective-permute-start | bytes 307208 | tf_op jit(solution)/shard_map/ppermute | solution.py:717
  68.8 28.5 %collective-permute-start.13 = (f32[50,8,128]{2,1,0:T(8,128)S(1)}, f32[50,8,128]{2,1,0:T(8,128)S(1)}, u32[]{:S(2)}, u32[]{:S(2)}) collective-permute-start(f32[50,8,128]{2,1,0:T(8,128)S(1)} %get-tuple-element.72), channel_id=1, source_target_pairs={{24,0},{0,8},{8,16},{16,24},{25,1},{1,9},{9,17},{17,25},{26,2},{2,... | collective-permute-start | bytes 614408 | tf_op jit(solution)/shard_map/ppermute | solution.py:717
  70.1 27.2 %collective-permute-start.14 = (f32[50,8,128]{2,1,0:T(8,128)S(1)}, f32[50,8,128]{2,1,0:T(8,128)S(1)}, u32[]{:S(2)}, u32[]{:S(2)}) collective-permute-start(f32[50,8,128]{2,1,0:T(8,128)S(1)} %get-tuple-element.73), channel_id=1, source_target_pairs={{16,0},{24,8},{0,16},{8,24},{17,1},{25,9},{1,17},{9,25},{18,2},{26... | collective-permute-start | bytes 614408 | tf_op jit(solution)/shard_map/ppermute | solution.py:717
  72.2 25.1 %collective-permute-start.15 = (f32[50,8,128]{2,1,0:T(8,128)S(1)}, f32[50,8,128]{2,1,0:T(8,128)S(1)}, u32[]{:S(2)}, u32[]{:S(2)}) collective-permute-start(f32[50,8,128]{2,1,0:T(8,128)S(1)} %get-tuple-element.74), channel_id=1, source_target_pairs={{8,0},{16,8},{24,16},{0,24},{9,1},{17,9},{25,17},{1,25},{10,2},{18... | collective-permute-start | bytes 614408 | tf_op jit(solution)/shard_map/ppermute | solution.py:717
  72.2 21.3 %collective-permute-start.20 = (f32[25,8,128]{2,1,0:T(8,128)S(1)}, f32[25,8,128]{2,1,0:T(8,128)S(1)}, u32[]{:S(2)}, u32[]{:S(2)}) collective-permute-start(f32[25,8,128]{2,1,0:T(8,128)S(1)} %get-tuple-element.81), channel_id=1, source_target_pairs={{16,0},{24,8},{0,16},{8,24},{17,1},{25,9},{1,17},{9,25},{18,2},{26... | collective-permute-start | bytes 307208 | tf_op jit(solution)/shard_map/ppermute | solution.py:717
  72.7 23.4 %collective-permute-start.21 = (f32[25,8,128]{2,1,0:T(8,128)S(1)}, f32[25,8,128]{2,1,0:T(8,128)S(1)}, u32[]{:S(2)}, u32[]{:S(2)}) collective-permute-start(f32[25,8,128]{2,1,0:T(8,128)S(1)} %get-tuple-element.82), channel_id=1, source_target_pairs={{8,0},{16,8},{24,16},{0,24},{9,1},{17,9},{25,17},{1,25},{10,2},{18... | collective-permute-start | bytes 307208 | tf_op jit(solution)/shard_map/ppermute | solution.py:717

commit v2 on v1

--- a/solution.py
+++ b/solution.py
@@ -125,7 +125,7 @@
     return terms
 
 
-def z_partners(pair, pz_ref):
+def z_partners(pair, pz_ref, only=None):
     lane = lanes()
     slot = sublanes() % 4
     even_ref, odd_ref = pair
@@ -151,10 +151,13 @@
                 pz_ref[t, v, rows, :] = jnp.where(slot < 2, low, high)
         return carry
 
-    lax.fori_loop(0, 5, one_variable, 0)
-
-
-def y_partners(u_ref, py_ref, halo_ref=None):
+    if only is None:
+        lax.fori_loop(0, 5, one_variable, 0)
+    else:
+        one_variable(only, 0)
+
+
+def y_partners(u_ref, py_ref, halo_ref=None, only=None):
     lane = lanes()
     lower = sublanes() < 4
 
@@ -184,7 +187,10 @@
             py_ref[t, v] = jnp.where(lower, before[t], after[t])
         return carry
 
-    lax.fori_loop(0, 5, one_variable, 0)
+    if only is None:
+        lax.fori_loop(0, 5, one_variable, 0)
+    else:
+        one_variable(only, 0)
 
 
 def load_state(u_ref, t, rows):
@@ -358,7 +364,6 @@
     ]
 
 
-HALF_ROWS = 25
 PACK_ROWS = 50
 HALO_ROWS = 57
 
@@ -468,9 +473,9 @@
             for t in range(TILES):
                 for r in range(2):
                     states[a][t, v, 8 * r : 8 * r + 8, :] = offset_ref[start_rows(v, a, r, t), :]
-    z_partners((u1, u2), pz_ref)
-    y_partners(u1, py1)
-    y_partners(u2, py2)
+        z_partners((u1, u2), pz_ref, v)
+        y_partners(u1, py1, None, v)
+        y_partners(u2, py2, None, v)
 
     def one_tile(t, carry):
         rates_tile(t, states, (1, 2), (0, 1, 2, 3), pz_ref, (py1, py2), r_ref, coef_ref)
@@ -481,7 +486,7 @@
         pack_message(rate_loader(r_ref), lax.rem(rank_ref[0] + d, 4), writer(out))
 
 
-def edge_kernel(rank_ref, u0, u1, u2, u3, left_ref, right_ref, t1, t2, t3, m1, m2, m3, r_ref, pz_ref, py0, py3, coef_ref):
+def edge_inner_kernel(u0, u1, u2, u3, r_ref, pz_ref, py0, py3, coef_ref):
     fill_coefficients(coef_ref)
     z_partners((u0, u3), pz_ref)
     y_partners(u0, py0)
@@ -490,17 +495,32 @@
 
     def one_tile(t, carry):
         rates_tile(t, states, (0, 3), (0, 1, 2, 3), pz_ref, (py0, py3), r_ref, coef_ref)
+        return carry
+
+    lax.fori_loop(0, TILES, one_tile, 0)
+
+
+def add_x_faces(u0, u3, inner_ref, left_ref, right_ref, r_ref):
+    def one_tile(t, carry):
+        r_ref[t] = inner_ref[t]
         x_face_tile(u0, left_ref, r_ref, 0, t)
         x_face_tile(u3, right_ref, r_ref, 1, t)
         return carry
 
     lax.fori_loop(0, TILES, one_tile, 0)
-    for d, outs in ((1, (t1, m1)), (2, (t2, m2)), (3, (t3, m3))):
-        pack_message(rate_loader(r_ref), lax.rem(rank_ref[0] + d, 4), writer(*outs))
-
-
-def own_kernel(rank_ref, start_ref, mid_ref, edge_ref, start_mid, start_edge, own_mid, own_edge):
+
+
+def edge_outer_kernel(rank_ref, u0, u3, inner_ref, left_ref, right_ref, m1, m2, m3, r_ref):
+    add_x_faces(u0, u3, inner_ref, left_ref, right_ref, r_ref)
+    for d, out in ((1, m1), (2, m2), (3, m3)):
+        pack_message(rate_loader(r_ref), lax.rem(rank_ref[0] + d, 4), writer(out))
+
+
+def own_kernel(rank_ref, start_hbm, mid_ref, edge_ref, start_mid, start_edge, own_mid, own_edge, start_ref, sems):
     rank = rank_ref[0]
+    copy = pltpu.make_async_copy(start_hbm, start_ref, sems.at[0])
+    copy.start()
+    copy.wait()
     for pair, rates, start_out, own_out in (((1, 2), mid_ref, start_mid, own_mid), ((0, 3), edge_ref, start_edge, own_edge)):
 
         def load(which, v, r, t):
@@ -510,37 +530,43 @@
         pack_message(rate_loader(rates), rank, writer(own_out))
 
 
-def assemble(rank_ref, table_ref, start_ref, rates, skipped, halves, states, halos=None):
+def node_weights(rank_ref, table_ref):
     rank = rank_ref[0]
-    weight = [
-        [table_ref[m * 4 + lax.rem(rank + 4 - d, 4)] for d in range(4)] for m in range(4)
-    ]
-
-    def node_state(m, row):
-        total = start_ref[row] + weight[m][0] * rates[0][row]
-        for d in range(1, 4):
-            total = total + weight[m][d] * rates[d][row - skipped]
-        return total
-
+    return [[table_ref[m * 4 + lax.rem(rank + 4 - d, 4)] for d in range(4)] for m in range(4)]
+
+
+def node_state(weight, start_ref, rates, m, row):
+    total = start_ref[row]
+    for d in range(4):
+        total = total + weight[m][d] * rates[d][row]
+    return total
+
+
+def assemble(weight, start_ref, rates, states):
     def one_variable(v, carry):
-        for r in halves:
+        for r in range(2):
             first = (5 * r + v) * 5
             for pair in range(2):
-                pieces = [[node_state(2 * pair + half, first + i) for i in range(5)] for half in range(2)]
+                pieces = [
+                    [node_state(weight, start_ref, rates, 2 * pair + half, first + i) for i in range(5)]
+                    for half in range(2)
+                ]
                 tiles = unpack_pair(*pieces)
                 for i in range(5):
                     for which in range(2):
-                        ref = states[which]
-                        rows = slice(8 * r, 8 * r + 8) if ref.shape[2] == 16 else slice(0, 8)
-                        ref[5 * pair + i, v, rows, :] = tiles[i][which]
+                        states[which][5 * pair + i, v, 8 * r : 8 * r + 8, :] = tiles[i][which]
         return carry
 
     lax.fori_loop(0, 5, one_variable, 0)
-    if halos is not None:
-        for m in range(4):
-            blocks = unpack_halo_parts([node_state(m, PACK_ROWS + i) for i in range(7)])
-            for n in range(10):
-                halos[n % 2][m, n // 2] = blocks[n]
+
+
+def assemble_halos(weight, start_ref, rates, halos):
+    for m in range(4):
+        blocks = unpack_halo_parts(
+            [node_state(weight, start_ref, rates, m, PACK_ROWS + i) for i in range(7)]
+        )
+        for n in range(10):
+            halos[n % 2][m, n // 2] = blocks[n]
 
 
 def send_increments(rank_ref, table_ref, r_ref, halves, outs):
@@ -567,7 +593,9 @@
 
 def middle_kernel(rank_ref, table_ref, start_ref, q0, q1, q2, q3, mid_ref, edge_ref, u1, u2, h1, h2, pz_ref, py1, py2, coef_ref):
     fill_coefficients(coef_ref)
-    assemble(rank_ref, table_ref, start_ref, (q0, q1, q2, q3), 0, (0, 1), (u1, u2), (h1, h2))
+    weight = node_weights(rank_ref, table_ref)
+    assemble(weight, start_ref, (q0, q1, q2, q3), (u1, u2))
+    assemble_halos(weight, start_ref, (q0, q1, q2, q3), (h1, h2))
     z_partners((u1, u2), pz_ref)
     y_partners(u1, py1, h1)
     y_partners(u2, py2, h2)
@@ -580,35 +608,26 @@
     lax.fori_loop(0, TILES, one_tile, 0)
 
 
-def complete_middle(rank_ref, table_ref, mid_ref, u0, u3, r, r_ref, outs):
+def join_kernel(rank_ref, table_ref, start_ref, q0, q1, q2, q3, mid_ref, u0, u3, o0, o1, o2, o3, r_ref):
+    assemble(node_weights(rank_ref, table_ref), start_ref, (q0, q1, q2, q3), (u0, u3))
+
     def one_tile(t, carry):
-        def start(v, a, half):
-            return mid_ref[t, v * 2 + a - 1, 8 * half : 8 * half + 8, :]
-
-        def emit(v, a, half, value):
-            r_ref[t, v * 2 + a - 1] = value
-
-        volume_tile(t, {0: u0, 3: u3}, {1: False, 2: False}, None, start, emit, (r,))
+        def start(v, a, r):
+            return mid_ref[t, v * 2 + a - 1, 8 * r : 8 * r + 8, :]
+
+        def emit(v, a, r, value):
+            r_ref[t, v * 2 + a - 1, 8 * r : 8 * r + 8, :] = value
+
+        volume_tile(t, {0: u0, 3: u3}, {1: False, 2: False}, None, start, emit)
         return carry
 
     lax.fori_loop(0, TILES, one_tile, 0)
-    send_increments(rank_ref, table_ref, r_ref, (r,), outs)
-
-
-def upper_kernel(rank_ref, table_ref, start_ref, q0, q1, q2, q3, mid_ref, w0, w3, o0, o1, o2, o3, r_ref):
-    assemble(rank_ref, table_ref, start_ref, (q0, q1, q2, q3), 0, (0,), (w0, w3))
-    complete_middle(rank_ref, table_ref, mid_ref, w0, w3, 0, r_ref, (o0, o1, o2, o3))
-
-
-def lower_kernel(rank_ref, table_ref, start_ref, q0, q1, q2, q3, mid_ref, w0, w3, u0, u3, h0, h3, o0, o1, o2, o3, r_ref):
-    assemble(rank_ref, table_ref, start_ref, (q0, q1, q2, q3), HALF_ROWS, (1,), (u0, u3), (h0, h3))
-    u0[:, :, 0:8, :] = w0[...]
-    u3[:, :, 0:8, :] = w3[...]
-    complete_middle(rank_ref, table_ref, mid_ref, u0, u3, 1, r_ref, (o0, o1, o2, o3))
-
-
-def last_inner_kernel(u0, u3, h0, h3, partial_ref, r_ref, pz_ref, py0, py3, coef_ref):
+    send_increments(rank_ref, table_ref, r_ref, (0, 1), (o0, o1, o2, o3))
+
+
+def last_inner_kernel(rank_ref, table_ref, u0, u3, start_ref, q0, q1, q2, q3, partial_ref, r_ref, h0, h3, pz_ref, py0, py3, coef_ref):
     fill_coefficients(coef_ref)
+    assemble_halos(node_weights(rank_ref, table_ref), start_ref, (q0, q1, q2, q3), (h0, h3))
     z_partners((u0, u3), pz_ref)
     y_partners(u0, py0, h0)
     y_partners(u3, py3, h3)
@@ -622,23 +641,14 @@
 
 
 def last_outer_kernel(rank_ref, table_ref, u0, u3, inner_ref, left_ref, right_ref, o0, o1, o2, o3, r_ref):
-    def one_tile(t, carry):
-        r_ref[t] = inner_ref[t]
-        x_face_tile(u0, left_ref, r_ref, 0, t)
-        x_face_tile(u3, right_ref, r_ref, 1, t)
-        return carry
-
-    lax.fori_loop(0, TILES, one_tile, 0)
+    add_x_faces(u0, u3, inner_ref, left_ref, right_ref, r_ref)
     send_increments(rank_ref, table_ref, r_ref, (0, 1), (o0, o1, o2, o3))
 
 
-def finish(rank_ref, halves, out_hbm, order_ref, stage_ref, sems, pair):
+def finish(rank_ref, pieces, out_hbm, order_ref, stage_ref, sems, pair):
     rank = rank_ref[0]
-    count = PACK_ROWS // len(halves)
-    for place, pieces in enumerate(halves):
-        for d in range(4):
-            slot = lax.rem(rank + 4 - d, 4)
-            order_ref[slot, count * place : count * (place + 1)] = pieces[d][...]
+    for d in range(4):
+        order_ref[lax.rem(rank + 4 - d, 4)] = pieces[d][...]
     copies = []
     for v in range(5):
         for r in range(2):
@@ -663,12 +673,12 @@
         copy.wait()
 
 
-def finish_middle(rank_ref, a0, a1, a2, a3, b0, b1, b2, b3, out_hbm, order_ref, stage_ref, sems):
-    finish(rank_ref, ((a0, a1, a2, a3), (b0, b1, b2, b3)), out_hbm, order_ref, stage_ref, sems, (1, 2))
+def finish_middle(rank_ref, q0, q1, q2, q3, out_hbm, order_ref, stage_ref, sems):
+    finish(rank_ref, (q0, q1, q2, q3), out_hbm, order_ref, stage_ref, sems, (1, 2))
 
 
 def finish_edge(rank_ref, q0, q1, q2, q3, before_hbm, out_hbm, order_ref, stage_ref, sems):
-    finish(rank_ref, ((q0, q1, q2, q3),), out_hbm, order_ref, stage_ref, sems, (0, 3))
+    finish(rank_ref, (q0, q1, q2, q3), out_hbm, order_ref, stage_ref, sems, (0, 3))
 
 
 def f32(*shape):
@@ -682,9 +692,6 @@
 FLAT = (3200, 128)
 MESSAGE = (HALO_ROWS, 8, 128)
 PIECE = (PACK_ROWS, 8, 128)
-UPPER = (HALF_ROWS, 8, 128)
-LOWER = (HALO_ROWS - HALF_ROWS, 8, 128)
-HALF = (TILES, 10, 8, 128)
 COEF = (12, 8, 128)
 
 
@@ -740,18 +747,23 @@
     got_mid = exchange(sent)
     left = shifted(u3, "space", 1)
     right = shifted(u0, "space", -1)
+    (inner,) = call(
+        edge_inner_kernel,
+        v(RATE),
+        v(u0, u1, u2, u3),
+        scratch=[TRACE, SIDE, SIDE, COEF],
+    )
     *sent, edge = call(
-        edge_kernel,
-        v(UPPER, UPPER, UPPER, LOWER, LOWER, LOWER, RATE),
-        [rank] + v(u0, u1, u2, u3, left, right),
-        scratch=[TRACE, SIDE, SIDE, COEF],
-    )
-    got_upper = exchange(sent[:3])
-    got_lower = exchange(sent[3:])
+        edge_outer_kernel,
+        v(MESSAGE, MESSAGE, MESSAGE, RATE),
+        [rank] + v(u0, u3, inner, left, right),
+    )
+    got_edge = exchange(sent)
     start_mid, start_edge, own_mid, own_edge = call(
         own_kernel,
         v(MESSAGE, MESSAGE, MESSAGE, MESSAGE),
-        [rank] + v(start_flat, mid, edge),
+        [rank, ("h", start_flat)] + v(mid, edge),
+        scratch=[FLAT, (1,)],
     )
     mid, edge = call(
         middle_kernel,
@@ -759,27 +771,20 @@
         [rank, table] + v(start_mid, own_mid, *got_mid),
         scratch=[TRACE, TRACE, HALO, HALO, TRACE, SIDE, SIDE, COEF],
     )
-    w0, w3, own_upper, *sent = call(
-        upper_kernel,
-        v(SIDE, SIDE, UPPER, UPPER, UPPER, UPPER),
-        [rank, table] + v(start_edge, own_edge, *got_upper, mid),
-        scratch=[HALF],
-    )
-    got_upper = exchange(sent)
-    u0, u3, h0, h3, own_lower, *sent = call(
-        lower_kernel,
-        v(TRACE, TRACE, HALO, HALO, UPPER, UPPER, UPPER, UPPER),
-        [rank, table] + v(start_edge, own_edge, *got_lower, mid, w0, w3),
-        scratch=[HALF],
-    )
-    got_lower = exchange(sent)
+    u0, u3, own_mid, *sent = call(
+        join_kernel,
+        v(TRACE, TRACE, PIECE, PIECE, PIECE, PIECE),
+        [rank, table] + v(start_edge, own_edge, *got_edge, mid),
+        scratch=[RATE],
+    )
+    got_mid = exchange(sent)
     left = shifted(u3, "space", 1)
     right = shifted(u0, "space", -1)
     (inner,) = call(
         last_inner_kernel,
         v(RATE),
-        v(u0, u3, h0, h3, edge),
-        scratch=[TRACE, SIDE, SIDE, COEF],
+        [rank, table] + v(u0, u3, start_edge, own_edge, *got_edge, edge),
+        scratch=[HALO, HALO, TRACE, SIDE, SIDE, COEF],
     )
     own_edge, *sent = call(
         last_outer_kernel,
@@ -792,7 +797,7 @@
     (result,) = call(
         finish_middle,
         [("h", FLAT)],
-        [rank] + v(own_upper, *got_upper, own_lower, *got_lower),
+        [rank] + v(own_mid, *got_mid),
         scratch=finishing,
     )
     (result,) = call(

time: 100 us -> 94.1 us (0.941); the launches traced: 98.5 us -> 94 us
  starting transfers between devices: 20.2 us -> 16.6 us
  Pallas kernels: 26.8 us -> 25.2 us
    ppermute x22 -> x16, starting transfers between devices: 20.2 us -> 16.6 us  [shifted(): lax.ppermute(block, axis, [((i - distance) % count, i) for i in range(cou...]
    pallas_call x10, Pallas kernels: 26.8 us -> 25.2 us  [call(): pl.pallas_call(kernel, out_shape=[f32(*shape) for _, shape in outs], in_s...]
    ppermute x22 -> x16, waiting for transfers between devices: 49.9 us -> 50.6 us  [shifted(): lax.ppermute(block, axis, [((i - distance) % count, i) for i in range(cou...]
  transfers between devices with their start and end apart: 22 -> 16, of which waited for: 10 -> 13; matrix products, arithmetic and copies ran while one was open for 0% -> 0% of each run, Pallas kernels for 18% -> 18%
where the time goes in v2:
time: 94.1 us; the launch traced here: 94 us
  waiting for transfers between devices  50.6 us (54%)
  Pallas kernels  25.2 us (27%)
  starting transfers between devices  16.6 us (18%)
  local copies, waits for them, and re-layouts  1.44 us (2%)
    ppermute x16, waiting for transfers between devices, shifted(): lax.ppermute(block, axis, [((i - distance) % count, i) for i in range(cou...  50.6 us
    pallas_call x10, Pallas kernels, call(): pl.pallas_call(kernel, out_shape=[f32(*shape) for _, shape in outs], in_s...  25.2 us
    ppermute x16, starting transfers between devices, shifted(): lax.ppermute(block, axis, [((i - distance) % count, i) for i in range(cou...  16.6 us
  transfers between devices with their start and end apart: 16, of which 13 were waited for; matrix products, arithmetic and copies ran while one was open for 0% of the time, Pallas kernels for 18%

profile of v2, /device:TPU:13, one launch (start us, length us, event | category | flops | bytes accessed | tf_op | source)
XLA Modules:
  0.0 94.0 jit_solution(8425301983789158264)
XLA Ops:
  0.0 1.4 %copy-done = f32[5,4,4,4,1,1280]{5,4,3,2,1,0:T(1,128)S(1)} copy-done((f32[5,4,4,4,1,1280]{5,4,3,2,1,0:T(1,128)S(1)}, f32[5,4,4,4,1,1280]{5,4,3,2,1,0:T(1,128)}, u32[]{:S(2)}) %copy-start) | copy-done | bytes 1638424
  1.4 4.9 %shard_map.37 = (f32[10,5,16,128]{3,2,1,0:T(8,128)S(1)}, f32[10,5,16,128]{3,2,1,0:T(8,128)S(1)}, f32[10,5,16,128]{3,2,1,0:T(8,128)S(1)}, f32[10,5,16,128]{3,2,1,...) custom-call(s32[1]{0:T(128)} %bitcast.rank_ref, ...), custom_call_target="tpu_custom_call" | custom-call | bytes 1 | tf_op jit(solution)/shard_map/pallas_call | solution.py:706
  7.0 1.2 %collective-permute-start = (f32[10,5,16,128]{3,2,1,0:T(8,128)S(1)}, f32[10,5,16,128]{3,2,1,0:T(8,128)S(1)}, u32[]{:S(2)}, u32[]{:S(2)}) collective-permute-start(f32[10,5,16,128]{3,2,1,0:T(8,128)S(1)} %get-tuple-element.35.u3), channel_id=1, source_target_pairs={{7,0},{0,1},{1,2},{2,3},{3,4},{4,5},{5,6},{6,7},{15,8},{8,9},{9,10... | collective-permute-start | bytes 1228808 | tf_op jit(solution)/shard_map/ppermute | solution.py:724
  8.2 1.3 %collective-permute-start.5 = (f32[57,8,128]{2,1,0:T(8,128)S(1)}, f32[57,8,128]{2,1,0:T(8,128)S(1)}, u32[]{:S(2)}, u32[]{:S(2)}) collective-permute-start(f32[57,8,128]{2,1,0:T(8,128)S(1)} %get-tuple-element.46), channel_id=1, source_target_pairs={{24,0},{0,8},{8,16},{16,24},{25,1},{1,9},{9,17},{17,25},{26,2},{2,... | collective-permute-start | bytes 700424 | tf_op jit(solution)/shard_map/ppermute | solution.py:724
  10.5 1.5 %collective-permute-start.7 = (f32[57,8,128]{2,1,0:T(8,128)S(1)}, f32[57,8,128]{2,1,0:T(8,128)S(1)}, u32[]{:S(2)}, u32[]{:S(2)}) collective-permute-start(f32[57,8,128]{2,1,0:T(8,128)S(1)} %get-tuple-element.48), channel_id=1, source_target_pairs={{8,0},{16,8},{24,16},{0,24},{9,1},{17,9},{25,17},{1,25},{10,2},{18... | collective-permute-start | bytes 700424 | tf_op jit(solution)/shard_map/ppermute | solution.py:724
  12.0 3.5 %shard_map.38.inner_ref = f32[10,10,16,128]{3,2,1,0:T(8,128)S(1)} custom-call(f32[10,5,16,128]{3,2,1,0:T(8,128)S(1)} %get-tuple-element.34.u0, f32[10,5,16,128]{3,2,1,0:T(8,128)S(1)} %get-tuple-element.36.u1, f32[10,5,16,128]{3,2,1,0:T(8,128)S(1)} %get-tuple-element.37.u2, f32[10,5,16,128]{3,2,1,0:T(8,128)S(1)} %get-tuple-element.35.u3), custom_call_target="tpu_custom_call" | custom-call | bytes 1 | tf_op jit(solution)/shard_map/pallas_call | solution.py:706
  15.5 1.1 %collective-permute-done.1.right_ref = f32[10,5,16,128]{3,2,1,0:T(8,128)S(1)} collective-permute-done((f32[10,5,16,128]{3,2,1,0:T(8,128)S(1)}, f32[10,5,16,128]{3,2,1,0:T(8,128)S(1)}, u32[]{:S(2)}, u32[]{:S(2)}) %collective-permute-start.1) | collective-permute-done | bytes 409632 | tf_op jit(solution)/shard_map/ppermute | solution.py:724
  17.4 1.2 %shard_map.39 = (f32[57,8,128]{2,1,0:T(8,128)S(1)}, f32[57,8,128]{2,1,0:T(8,128)S(1)}, f32[57,8,128]{2,1,0:T(8,128)S(1)}, f32[10,10,16,128]{3,2,1,0:T(8,128)S(1)}) custom-call(s32[1]{0:T(128)} %bitcast.rank_ref, f32[10,5,16,128]{3,2,1,0:T(8,128)S(1)} %get-tuple-element.34.u0, f32[10,5,16,128]{3,2,1,0:T(8,128)S(1)} %get-tuple-element.35.u3, ...), custom_call_target="tpu_custom_call" | custom-call | bytes 1 | tf_op jit(solution)/shard_map/pallas_call | solution.py:706
  18.6 1.3 %collective-permute-start.2 = (f32[57,8,128]{2,1,0:T(8,128)S(1)}, f32[57,8,128]{2,1,0:T(8,128)S(1)}, u32[]{:S(2)}, u32[]{:S(2)}) collective-permute-start(f32[57,8,128]{2,1,0:T(8,128)S(1)} %get-tuple-element.41), channel_id=1, source_target_pairs={{24,0},{0,8},{8,16},{16,24},{25,1},{1,9},{9,17},{17,25},{26,2},{2,... | collective-permute-start | bytes 700424 | tf_op jit(solution)/shard_map/ppermute | solution.py:724
  20.0 1.1 %collective-permute-start.3 = (f32[57,8,128]{2,1,0:T(8,128)S(1)}, f32[57,8,128]{2,1,0:T(8,128)S(1)}, u32[]{:S(2)}, u32[]{:S(2)}) collective-permute-start(f32[57,8,128]{2,1,0:T(8,128)S(1)} %get-tuple-element.42), channel_id=1, source_target_pairs={{16,0},{24,8},{0,16},{8,24},{17,1},{25,9},{1,17},{9,25},{18,2},{26... | collective-permute-start | bytes 700424 | tf_op jit(solution)/shard_map/ppermute | solution.py:724
  21.1 1.4 %collective-permute-start.4 = (f32[57,8,128]{2,1,0:T(8,128)S(1)}, f32[57,8,128]{2,1,0:T(8,128)S(1)}, u32[]{:S(2)}, u32[]{:S(2)}) collective-permute-start(f32[57,8,128]{2,1,0:T(8,128)S(1)} %get-tuple-element.43), channel_id=1, source_target_pairs={{8,0},{16,8},{24,16},{0,24},{9,1},{17,9},{25,17},{1,25},{10,2},{18... | collective-permute-start | bytes 700424 | tf_op jit(solution)/shard_map/ppermute | solution.py:724
  23.5 6.4 %collective-permute-done.6.q2 = f32[57,8,128]{2,1,0:T(8,128)S(1)} collective-permute-done((f32[57,8,128]{2,1,0:T(8,128)S(1)}, f32[57,8,128]{2,1,0:T(8,128)S(1)}, u32[]{:S(2)}, u32[]{:S(2)}) %collective-permute-start.6) | collective-permute-done | bytes 233504 | tf_op jit(solution)/shard_map/ppermute | solution.py:724
  29.9 11.9 %collective-permute-done.7.q3 = f32[57,8,128]{2,1,0:T(8,128)S(1)} collective-permute-done((f32[57,8,128]{2,1,0:T(8,128)S(1)}, f32[57,8,128]{2,1,0:T(8,128)S(1)}, u32[]{:S(2)}, u32[]{:S(2)}) %collective-permute-start.7) | collective-permute-done | bytes 233504 | tf_op jit(solution)/shard_map/ppermute | solution.py:724
  41.8 4.7 %shard_map.41 = (f32[10,10,16,128]{3,2,1,0:T(8,128)S(1)}, f32[10,10,16,128]{3,2,1,0:T(8,128)S(1)}) custom-call(s32[1]{0:T(128)} %bitcast.rank_ref, f32[16]{0:T(128)S(1)} %copy-done.2, f32[57,8,128]{2,1,0:T(8,128)S(1)} %get-tuple-element.44.start_ref, f32[57,8,128]{2,1,0:T(8,128)S(1)} %get-tuple-element.45.q0, f32[57,8,128]{2,1,0:T(8,128)S(1)} %collective-permute-done.5.q1, ...), custom_call_target="tpu_custom_call" | custom-call | bytes 1 | tf_op jit(solution)/shard_map/pallas_call | solution.py:706
  46.5 3.4 %collective-permute-done.3.q2 = f32[57,8,128]{2,1,0:T(8,128)S(1)} collective-permute-done((f32[57,8,128]{2,1,0:T(8,128)S(1)}, f32[57,8,128]{2,1,0:T(8,128)S(1)}, u32[]{:S(2)}, u32[]{:S(2)}) %collective-permute-start.3) | collective-permute-done | bytes 233504 | tf_op jit(solution)/shard_map/ppermute | solution.py:724
  49.9 1.9 %collective-permute-done.4.q3 = f32[57,8,128]{2,1,0:T(8,128)S(1)} collective-permute-done((f32[57,8,128]{2,1,0:T(8,128)S(1)}, f32[57,8,128]{2,1,0:T(8,128)S(1)}, u32[]{:S(2)}, u32[]{:S(2)}) %collective-permute-start.4) | collective-permute-done | bytes 233504 | tf_op jit(solution)/shard_map/ppermute | solution.py:724
  51.8 2.0 %shard_map.42 = (f32[10,5,16,128]{3,2,1,0:T(8,128)S(1)}, f32[10,5,16,128]{3,2,1,0:T(8,128)S(1)}, f32[50,8,128]{2,1,0:T(8,128)S(1)}, f32[50,8,128]{2,1,0:T(8,128)...) custom-call(s32[1]{0:T(128)} %bitcast.rank_ref, f32[16]{0:T(128)S(1)} %copy-done.2, ...), custom_call_target="tpu_custom_call" | custom-call | bytes 1 | tf_op jit(solution)/shard_map/pallas_call | solution.py:706
  54.3 1.3 %collective-permute-start.8 = (f32[10,5,16,128]{3,2,1,0:T(8,128)S(1)}, f32[10,5,16,128]{3,2,1,0:T(8,128)S(1)}, u32[]{:S(2)}, u32[]{:S(2)}) collective-permute-start(f32[10,5,16,128]{3,2,1,0:T(8,128)S(1)} %get-tuple-element.51.u3), channel_id=1, source_target_pairs={{7,0},{0,1},{1,2},{2,3},{3,4},{4,5},{5,6},{6,7},{15,8},{8,9},{9,10... | collective-permute-start | bytes 1228808 | tf_op jit(solution)/shard_map/ppermute | solution.py:724
  55.6 1.2 %collective-permute-start.14 = (f32[50,8,128]{2,1,0:T(8,128)S(1)}, f32[50,8,128]{2,1,0:T(8,128)S(1)}, u32[]{:S(2)}, u32[]{:S(2)}) collective-permute-start(f32[50,8,128]{2,1,0:T(8,128)S(1)} %get-tuple-element.59), channel_id=1, source_target_pairs={{16,0},{24,8},{0,16},{8,24},{17,1},{25,9},{1,17},{9,25},{18,2},{26... | collective-permute-start | bytes 614408 | tf_op jit(solution)/shard_map/ppermute | solution.py:724
  56.8 1.5 %collective-permute-start.15 = (f32[50,8,128]{2,1,0:T(8,128)S(1)}, f32[50,8,128]{2,1,0:T(8,128)S(1)}, u32[]{:S(2)}, u32[]{:S(2)}) collective-permute-start(f32[50,8,128]{2,1,0:T(8,128)S(1)} %get-tuple-element.60), channel_id=1, source_target_pairs={{8,0},{16,8},{24,16},{0,24},{9,1},{17,9},{25,17},{1,25},{10,2},{18... | collective-permute-start | bytes 614408 | tf_op jit(solution)/shard_map/ppermute | solution.py:724
  58.2 4.1 %shard_map.43.inner_ref = f32[10,10,16,128]{3,2,1,0:T(8,128)S(1)} custom-call(s32[1]{0:T(128)} %bitcast.rank_ref, f32[16]{0:T(128)S(1)} %copy-done.2, f32[10,5,16,128]{3,2,1,0:T(8,128)S(1)} %get-tuple-element.50.u0, f32[10,5,16,128]{3,2,1,0:T(8,128)S(1)} %get-tuple-element.51.u3, f32[57,8,128]{2,1,0:T(8,128)S(1)} %get-tuple-element.39.start_ref, ...), custom_call_target="tpu_custom_call" | custom-call | bytes 1 | tf_op jit(solution)/shard_map/pallas_call | solution.py:706
  62.3 2.1 %collective-permute-done.9.right_ref = f32[10,5,16,128]{3,2,1,0:T(8,128)S(1)} collective-permute-done((f32[10,5,16,128]{3,2,1,0:T(8,128)S(1)}, f32[10,5,16,128]{3,2,1,0:T(8,128)S(1)}, u32[]{:S(2)}, u32[]{:S(2)}) %collective-permute-start.9) | collective-permute-done | bytes 409632 | tf_op jit(solution)/shard_map/ppermute | solution.py:724
  64.6 1.6 %shard_map.44 = (f32[50,8,128]{2,1,0:T(8,128)S(1)}, f32[50,8,128]{2,1,0:T(8,128)S(1)}, f32[50,8,128]{2,1,0:T(8,128)S(1)}, f32[50,8,128]{2,1,0:T(8,128)S(1)}) custom-call(s32[1]{0:T(128)} %bitcast.rank_ref, f32[16]{0:T(128)S(1)} %copy-done.2, f32[10,5,16,128]{3,2,1,0:T(8,128)S(1)} %get-tuple-element.50.u0, f32[10,5,16,128]{3,2,1,0:T(8,128)S(1)} %get-tuple-element.51.u3, ...), custom_call_target="tpu_custom_call" | custom-call | bytes 1 | tf_op jit(solution)/shard_map/pallas_call | solution.py:706
  66.3 1.2 %collective-permute-start.11 = (f32[50,8,128]{2,1,0:T(8,128)S(1)}, f32[50,8,128]{2,1,0:T(8,128)S(1)}, u32[]{:S(2)}, u32[]{:S(2)}) collective-permute-start(f32[50,8,128]{2,1,0:T(8,128)S(1)} %get-tuple-element.55), channel_id=1, source_target_pairs={{16,0},{24,8},{0,16},{8,24},{17,1},{25,9},{1,17},{9,25},{18,2},{26... | collective-permute-start | bytes 614408 | tf_op jit(solution)/shard_map/ppermute | solution.py:724
  67.5 1.4 %collective-permute-start.12 = (f32[50,8,128]{2,1,0:T(8,128)S(1)}, f32[50,8,128]{2,1,0:T(8,128)S(1)}, u32[]{:S(2)}, u32[]{:S(2)}) collective-permute-start(f32[50,8,128]{2,1,0:T(8,128)S(1)} %get-tuple-element.56), channel_id=1, source_target_pairs={{8,0},{16,8},{24,16},{0,24},{9,1},{17,9},{25,17},{1,25},{10,2},{18... | collective-permute-start | bytes 614408 | tf_op jit(solution)/shard_map/ppermute | solution.py:724
  68.9 4.8 %collective-permute-done.14.q2 = f32[50,8,128]{2,1,0:T(8,128)S(1)} collective-permute-done((f32[50,8,128]{2,1,0:T(8,128)S(1)}, f32[50,8,128]{2,1,0:T(8,128)S(1)}, u32[]{:S(2)}, u32[]{:S(2)}) %collective-permute-start.14) | collective-permute-done | bytes 204832 | tf_op jit(solution)/shard_map/ppermute | solution.py:724
  73.8 10.3 %collective-permute-done.15.q3 = f32[50,8,128]{2,1,0:T(8,128)S(1)} collective-permute-done((f32[50,8,128]{2,1,0:T(8,128)S(1)}, f32[50,8,128]{2,1,0:T(8,128)S(1)}, u32[]{:S(2)}, u32[]{:S(2)}) %collective-permute-start.15) | collective-permute-done | bytes 204832 | tf_op jit(solution)/shard_map/ppermute | solution.py:724
  84.0 1.1 %shard_map.45.before_hbm = f32[3200,128]{1,0:T(8,128)} custom-call(s32[1]{0:T(128)} %bitcast.rank_ref, f32[50,8,128]{2,1,0:T(8,128)S(1)} %get-tuple-element.57.q0, f32[50,8,128]{2,1,0:T(8,128)S(1)} %collective-permute-done.13.q1, f32[50,8,128]{2,1,0:T(8,128)S(1)} %collective-permute-done.14.q2, f32[50,8,128]{2,1,0:T(8,128)S(1)} %collective-permute-done.15.q3), custom_call_target="tpu_custom_call" | custom-call | bytes 1 | tf_op jit(solution)/shard_map/pallas_call | solution.py:706
  85.2 1.7 %collective-permute-done.10.q1 = f32[50,8,128]{2,1,0:T(8,128)S(1)} collective-permute-done((f32[50,8,128]{2,1,0:T(8,128)S(1)}, f32[50,8,128]{2,1,0:T(8,128)S(1)}, u32[]{:S(2)}, u32[]{:S(2)}) %collective-permute-start.10) | collective-permute-done | bytes 204832 | tf_op jit(solution)/shard_map/ppermute | solution.py:724
  86.9 4.1 %collective-permute-done.11.q2 = f32[50,8,128]{2,1,0:T(8,128)S(1)} collective-permute-done((f32[50,8,128]{2,1,0:T(8,128)S(1)}, f32[50,8,128]{2,1,0:T(8,128)S(1)}, u32[]{:S(2)}, u32[]{:S(2)}) %collective-permute-start.11) | collective-permute-done | bytes 204832 | tf_op jit(solution)/shard_map/ppermute | solution.py:724
  91.0 1.8 %collective-permute-done.12.q3 = f32[50,8,128]{2,1,0:T(8,128)S(1)} collective-permute-done((f32[50,8,128]{2,1,0:T(8,128)S(1)}, f32[50,8,128]{2,1,0:T(8,128)S(1)}, u32[]{:S(2)}, u32[]{:S(2)}) %collective-permute-start.12) | collective-permute-done | bytes 204832 | tf_op jit(solution)/shard_map/ppermute | solution.py:724
  92.8 1.1 %shard_map.46 = f32[3200,128]{1,0:T(8,128)} custom-call(s32[1]{0:T(128)} %bitcast.rank_ref, f32[50,8,128]{2,1,0:T(8,128)S(1)} %get-tuple-element.53.q0, f32[50,8,128]{2,1,0:T(8,128)S(1)} %collective-permute-done.10.q1, f32[50,8,128]{2,1,0:T(8,128)S(1)} %collective-permute-done.11.q2, ...), custom_call_target="tpu_custom_call", output_to_operand_aliasing={{}: (5, {})} | custom-call | bytes 1 | tf_op jit(solution)/shard_map/pallas_call | solution.py:706
  (16 shorter events, 4.4 us)
Async XLA Ops:
  0.0 1.4 %copy-start = (f32[5,4,4,4,1,1280]{5,4,3,2,1,0:T(1,128)S(1)}, f32[5,4,4,4,1,1280]{5,4,3,2,1,0:T(1,128)}, u32[]{:S(2)}) copy-start(f32[5,4,4,4,1,1280]{5,4,3,2,1,0:T(1,128)} %param.3) | copy-start | bytes 4915204
  6.3 10.3 %collective-permute-start.1 = (f32[10,5,16,128]{3,2,1,0:T(8,128)S(1)}, f32[10,5,16,128]{3,2,1,0:T(8,128)S(1)}, u32[]{:S(2)}, u32[]{:S(2)}) collective-permute-start(f32[10,5,16,128]{3,2,1,0:T(8,128)S(1)} %get-tuple-element.34.u0), channel_id=1, source_target_pairs={{1,0},{2,1},{3,2},{4,3},{5,4},{6,5},{7,6},{0,7},{9,8},{10,9},{11,1... | collective-permute-start | bytes 1228808 | tf_op jit(solution)/shard_map/ppermute | solution.py:724
  7.0 10.4 %collective-permute-start = (f32[10,5,16,128]{3,2,1,0:T(8,128)S(1)}, f32[10,5,16,128]{3,2,1,0:T(8,128)S(1)}, u32[]{:S(2)}, u32[]{:S(2)}) collective-permute-start(f32[10,5,16,128]{3,2,1,0:T(8,128)S(1)} %get-tuple-element.35.u3), channel_id=1, source_target_pairs={{7,0},{0,1},{1,2},{2,3},{3,4},{4,5},{5,6},{6,7},{15,8},{8,9},{9,10... | collective-permute-start | bytes 1228808 | tf_op jit(solution)/shard_map/ppermute | solution.py:724
  8.2 12.9 %collective-permute-start.5 = (f32[57,8,128]{2,1,0:T(8,128)S(1)}, f32[57,8,128]{2,1,0:T(8,128)S(1)}, u32[]{:S(2)}, u32[]{:S(2)}) collective-permute-start(f32[57,8,128]{2,1,0:T(8,128)S(1)} %get-tuple-element.46), channel_id=1, source_target_pairs={{24,0},{0,8},{8,16},{16,24},{25,1},{1,9},{9,17},{17,25},{26,2},{2,... | collective-permute-start | bytes 700424 | tf_op jit(solution)/shard_map/ppermute | solution.py:724
  9.5 20.4 %collective-permute-start.6 = (f32[57,8,128]{2,1,0:T(8,128)S(1)}, f32[57,8,128]{2,1,0:T(8,128)S(1)}, u32[]{:S(2)}, u32[]{:S(2)}) collective-permute-start(f32[57,8,128]{2,1,0:T(8,128)S(1)} %get-tuple-element.47), channel_id=1, source_target_pairs={{16,0},{24,8},{0,16},{8,24},{17,1},{25,9},{1,17},{9,25},{18,2},{26... | collective-permute-start | bytes 700424 | tf_op jit(solution)/shard_map/ppermute | solution.py:724
  10.5 31.3 %collective-permute-start.7 = (f32[57,8,128]{2,1,0:T(8,128)S(1)}, f32[57,8,128]{2,1,0:T(8,128)S(1)}, u32[]{:S(2)}, u32[]{:S(2)}) collective-permute-start(f32[57,8,128]{2,1,0:T(8,128)S(1)} %get-tuple-element.48), channel_id=1, source_target_pairs={{8,0},{16,8},{24,16},{0,24},{9,1},{17,9},{25,17},{1,25},{10,2},{18... | collective-permute-start | bytes 700424 | tf_op jit(solution)/shard_map/ppermute | solution.py:724
  15.5 6.9 %copy-start.1 = (f32[5,4,4,4,1,1280]{5,4,3,2,1,0:T(1,128)S(1)}, f32[5,4,4,4,1,1280]{5,4,3,2,1,0:T(1,128)}, u32[]{:S(2)}) copy-start(f32[5,4,4,4,1,1280]{5,4,3,2,1,0:T(1,128)} %param.3) | copy-start | bytes 4915204
  18.6 27.9 %collective-permute-start.2 = (f32[57,8,128]{2,1,0:T(8,128)S(1)}, f32[57,8,128]{2,1,0:T(8,128)S(1)}, u32[]{:S(2)}, u32[]{:S(2)}) collective-permute-start(f32[57,8,128]{2,1,0:T(8,128)S(1)} %get-tuple-element.41), channel_id=1, source_target_pairs={{24,0},{0,8},{8,16},{16,24},{25,1},{1,9},{9,17},{17,25},{26,2},{2,... | collective-permute-start | bytes 700424 | tf_op jit(solution)/shard_map/ppermute | solution.py:724
  20.0 29.9 %collective-permute-start.3 = (f32[57,8,128]{2,1,0:T(8,128)S(1)}, f32[57,8,128]{2,1,0:T(8,128)S(1)}, u32[]{:S(2)}, u32[]{:S(2)}) collective-permute-start(f32[57,8,128]{2,1,0:T(8,128)S(1)} %get-tuple-element.42), channel_id=1, source_target_pairs={{16,0},{24,8},{0,16},{8,24},{17,1},{25,9},{1,17},{9,25},{18,2},{26... | collective-permute-start | bytes 700424 | tf_op jit(solution)/shard_map/ppermute | solution.py:724
  21.1 30.8 %collective-permute-start.4 = (f32[57,8,128]{2,1,0:T(8,128)S(1)}, f32[57,8,128]{2,1,0:T(8,128)S(1)}, u32[]{:S(2)}, u32[]{:S(2)}) collective-permute-start(f32[57,8,128]{2,1,0:T(8,128)S(1)} %get-tuple-element.43), channel_id=1, source_target_pairs={{8,0},{16,8},{24,16},{0,24},{9,1},{17,9},{25,17},{1,25},{10,2},{18... | collective-permute-start | bytes 700424 | tf_op jit(solution)/shard_map/ppermute | solution.py:724
  22.4 19.4 %copy-start.2 = (f32[16]{0:T(128)S(1)}, f32[16]{0:T(128)}, u32[]{:S(2)}) copy-start(f32[16]{0:T(128)} %constant.7.clone.table_ref) | copy-start | bytes 196
  53.8 10.6 %collective-permute-start.9 = (f32[10,5,16,128]{3,2,1,0:T(8,128)S(1)}, f32[10,5,16,128]{3,2,1,0:T(8,128)S(1)}, u32[]{:S(2)}, u32[]{:S(2)}) collective-permute-start(f32[10,5,16,128]{3,2,1,0:T(8,128)S(1)} %get-tuple-element.50.u0), channel_id=1, source_target_pairs={{1,0},{2,1},{3,2},{4,3},{5,4},{6,5},{7,6},{0,7},{9,8},{10,9},{11,1... | collective-permute-start | bytes 1228808 | tf_op jit(solution)/shard_map/ppermute | solution.py:724
  54.3 10.3 %collective-permute-start.8 = (f32[10,5,16,128]{3,2,1,0:T(8,128)S(1)}, f32[10,5,16,128]{3,2,1,0:T(8,128)S(1)}, u32[]{:S(2)}, u32[]{:S(2)}) collective-permute-start(f32[10,5,16,128]{3,2,1,0:T(8,128)S(1)} %get-tuple-element.51.u3), channel_id=1, source_target_pairs={{7,0},{0,1},{1,2},{2,3},{3,4},{4,5},{5,6},{6,7},{15,8},{8,9},{9,10... | collective-permute-start | bytes 1228808 | tf_op jit(solution)/shard_map/ppermute | solution.py:724
  55.6 11.9 %collective-permute-start.13 = (f32[50,8,128]{2,1,0:T(8,128)S(1)}, f32[50,8,128]{2,1,0:T(8,128)S(1)}, u32[]{:S(2)}, u32[]{:S(2)}) collective-permute-start(f32[50,8,128]{2,1,0:T(8,128)S(1)} %get-tuple-element.58), channel_id=1, source_target_pairs={{24,0},{0,8},{8,16},{16,24},{25,1},{1,9},{9,17},{17,25},{26,2},{2,... | collective-permute-start | bytes 614408 | tf_op jit(solution)/shard_map/ppermute | solution.py:724
  55.6 18.2 %collective-permute-start.14 = (f32[50,8,128]{2,1,0:T(8,128)S(1)}, f32[50,8,128]{2,1,0:T(8,128)S(1)}, u32[]{:S(2)}, u32[]{:S(2)}) collective-permute-start(f32[50,8,128]{2,1,0:T(8,128)S(1)} %get-tuple-element.59), channel_id=1, source_target_pairs={{16,0},{24,8},{0,16},{8,24},{17,1},{25,9},{1,17},{9,25},{18,2},{26... | collective-permute-start | bytes 614408 | tf_op jit(solution)/shard_map/ppermute | solution.py:724
  56.8 27.3 %collective-permute-start.15 = (f32[50,8,128]{2,1,0:T(8,128)S(1)}, f32[50,8,128]{2,1,0:T(8,128)S(1)}, u32[]{:S(2)}, u32[]{:S(2)}) collective-permute-start(f32[50,8,128]{2,1,0:T(8,128)S(1)} %get-tuple-element.60), channel_id=1, source_target_pairs={{8,0},{16,8},{24,16},{0,24},{9,1},{17,9},{25,17},{1,25},{10,2},{18... | collective-permute-start | bytes 614408 | tf_op jit(solution)/shard_map/ppermute | solution.py:724
  66.2 20.7 %collective-permute-start.10 = (f32[50,8,128]{2,1,0:T(8,128)S(1)}, f32[50,8,128]{2,1,0:T(8,128)S(1)}, u32[]{:S(2)}, u32[]{:S(2)}) collective-permute-start(f32[50,8,128]{2,1,0:T(8,128)S(1)} %get-tuple-element.54), channel_id=1, source_target_pairs={{24,0},{0,8},{8,16},{16,24},{25,1},{1,9},{9,17},{17,25},{26,2},{2,... | collective-permute-start | bytes 614408 | tf_op jit(solution)/shard_map/ppermute | solution.py:724
  66.3 24.7 %collective-permute-start.11 = (f32[50,8,128]{2,1,0:T(8,128)S(1)}, f32[50,8,128]{2,1,0:T(8,128)S(1)}, u32[]{:S(2)}, u32[]{:S(2)}) collective-permute-start(f32[50,8,128]{2,1,0:T(8,128)S(1)} %get-tuple-element.55), channel_id=1, source_target_pairs={{16,0},{24,8},{0,16},{8,24},{17,1},{25,9},{1,17},{9,25},{18,2},{26... | collective-permute-start | bytes 614408 | tf_op jit(solution)/shard_map/ppermute | solution.py:724
  67.5 25.3 %collective-permute-start.12 = (f32[50,8,128]{2,1,0:T(8,128)S(1)}, f32[50,8,128]{2,1,0:T(8,128)S(1)}, u32[]{:S(2)}, u32[]{:S(2)}) collective-permute-start(f32[50,8,128]{2,1,0:T(8,128)S(1)} %get-tuple-element.56), channel_id=1, source_target_pairs={{8,0},{16,8},{24,16},{0,24},{9,1},{17,9},{25,17},{1,25},{10,2},{18... | collective-permute-start | bytes 614408 | tf_op jit(solution)/shard_map/ppermute | solution.py:724

commit v3 on v2

--- a/solution.py
+++ b/solution.py
@@ -16,6 +16,7 @@
 gamma_gas = 1.4
 step_length = 0.01
 VMEM_LIMIT = 48 * 1024 * 1024
+FRONT_LIMIT = 53_000_000
 
 
 def lobatto_derivative():
@@ -695,7 +696,7 @@
 COEF = (12, 8, 128)
 
 
-def call(kernel, outs, args, scratch=(), flops=0, aliases=None):
+def call(kernel, outs, args, scratch=(), flops=0, aliases=None, limit=VMEM_LIMIT):
     place = {
         "s": pl.BlockSpec(memory_space=pltpu.SMEM),
         "v": pl.BlockSpec(memory_space=pltpu.VMEM),
@@ -713,7 +714,7 @@
             for shape in scratch
         ],
         input_output_aliases=aliases or {},
-        compiler_params=pltpu.CompilerParams(vmem_limit_bytes=VMEM_LIMIT),
+        compiler_params=pltpu.CompilerParams(vmem_limit_bytes=limit),
         cost_estimate=pl.CostEstimate(flops=flops, bytes_accessed=1, transcendentals=0),
     )(*[a for _, a in args])
     return result
@@ -743,6 +744,7 @@
         v(TRACE, TRACE, TRACE, TRACE, RATE, MESSAGE, MESSAGE, MESSAGE),
         [rank, ("h", start_flat), ("h", offset_flat)],
         scratch=[FLAT, FLAT, TRACE, SIDE, SIDE, COEF, (10,)],
+        limit=FRONT_LIMIT,
     )
     got_mid = exchange(sent)
     left = shifted(u3, "space", 1)

time: 94.1 us -> 92.7 us (0.985)
  local copies, waits for them, and re-layouts: 1.44 us -> 0.01 us
    unnamed x6 -> x4, local copies, waits for them, and re-layouts: 1.44 us -> 0.01 us
  transfers between devices with their start and end apart: 16 -> 16, of which waited for: 13 -> 13; matrix products, arithmetic and copies ran while one was open for 0% -> 0% of each run, Pallas kernels for 18% -> 19%
where the time goes in v3:
time: 92.7 us; the launch traced here: 92.6 us
  waiting for transfers between devices  50.6 us (55%)
  Pallas kernels  25.2 us (27%)
  starting transfers between devices  16.6 us (18%)
    ppermute x16, waiting for transfers between devices, shifted(): lax.ppermute(block, axis, [((i - distance) % count, i) for i in range(cou...  50.6 us
    pallas_call x10, Pallas kernels, call(): pl.pallas_call(kernel, out_shape=[f32(*shape) for _, shape in outs], in_s...  25.2 us
    ppermute x16, starting transfers between devices, shifted(): lax.ppermute(block, axis, [((i - distance) % count, i) for i in range(cou...  16.6 us
  transfers between devices with their start and end apart: 16, of which 13 were waited for; matrix products, arithmetic and copies ran while one was open for 0% of the time, Pallas kernels for 19%

profile of v3, /device:TPU:13, one launch (start us, length us, event | category | flops | bytes accessed | tf_op | source)
XLA Modules:
  0.0 92.6 jit_solution(12621664576046518990)
XLA Ops:
  0.0 4.9 %shard_map.37 = (f32[10,5,16,128]{3,2,1,0:T(8,128)S(1)}, f32[10,5,16,128]{3,2,1,0:T(8,128)S(1)}, f32[10,5,16,128]{3,2,1,0:T(8,128)S(1)}, f32[10,5,16,128]{3,2,1,...) custom-call(s32[1]{0:T(128)} %bitcast.rank_ref, ...), custom_call_target="tpu_custom_call" | custom-call | bytes 1 | tf_op jit(solution)/shard_map/pallas_call | solution.py:707
  5.6 1.2 %collective-permute-start = (f32[10,5,16,128]{3,2,1,0:T(8,128)S(1)}, f32[10,5,16,128]{3,2,1,0:T(8,128)S(1)}, u32[]{:S(2)}, u32[]{:S(2)}) collective-permute-start(f32[10,5,16,128]{3,2,1,0:T(8,128)S(1)} %get-tuple-element.35.u3), channel_id=1, source_target_pairs={{7,0},{0,1},{1,2},{2,3},{3,4},{4,5},{5,6},{6,7},{15,8},{8,9},{9,10... | collective-permute-start | bytes 1228808 | tf_op jit(solution)/shard_map/ppermute | solution.py:725
  6.8 1.3 %collective-permute-start.5 = (f32[57,8,128]{2,1,0:T(8,128)S(1)}, f32[57,8,128]{2,1,0:T(8,128)S(1)}, u32[]{:S(2)}, u32[]{:S(2)}) collective-permute-start(f32[57,8,128]{2,1,0:T(8,128)S(1)} %get-tuple-element.46), channel_id=1, source_target_pairs={{24,0},{0,8},{8,16},{16,24},{25,1},{1,9},{9,17},{17,25},{26,2},{2,... | collective-permute-start | bytes 700424 | tf_op jit(solution)/shard_map/ppermute | solution.py:725
  8.1 1.0 %collective-permute-start.6 = (f32[57,8,128]{2,1,0:T(8,128)S(1)}, f32[57,8,128]{2,1,0:T(8,128)S(1)}, u32[]{:S(2)}, u32[]{:S(2)}) collective-permute-start(f32[57,8,128]{2,1,0:T(8,128)S(1)} %get-tuple-element.47), channel_id=1, source_target_pairs={{16,0},{24,8},{0,16},{8,24},{17,1},{25,9},{1,17},{9,25},{18,2},{26... | collective-permute-start | bytes 700424 | tf_op jit(solution)/shard_map/ppermute | solution.py:725
  9.1 1.5 %collective-permute-start.7 = (f32[57,8,128]{2,1,0:T(8,128)S(1)}, f32[57,8,128]{2,1,0:T(8,128)S(1)}, u32[]{:S(2)}, u32[]{:S(2)}) collective-permute-start(f32[57,8,128]{2,1,0:T(8,128)S(1)} %get-tuple-element.48), channel_id=1, source_target_pairs={{8,0},{16,8},{24,16},{0,24},{9,1},{17,9},{25,17},{1,25},{10,2},{18... | collective-permute-start | bytes 700424 | tf_op jit(solution)/shard_map/ppermute | solution.py:725
  10.6 3.5 %shard_map.38.inner_ref = f32[10,10,16,128]{3,2,1,0:T(8,128)S(1)} custom-call(f32[10,5,16,128]{3,2,1,0:T(8,128)S(1)} %get-tuple-element.34.u0, f32[10,5,16,128]{3,2,1,0:T(8,128)S(1)} %get-tuple-element.36.u1, f32[10,5,16,128]{3,2,1,0:T(8,128)S(1)} %get-tuple-element.37.u2, f32[10,5,16,128]{3,2,1,0:T(8,128)S(1)} %get-tuple-element.35.u3), custom_call_target="tpu_custom_call" | custom-call | bytes 1 | tf_op jit(solution)/shard_map/pallas_call | solution.py:707
  14.1 1.1 %collective-permute-done.1.right_ref = f32[10,5,16,128]{3,2,1,0:T(8,128)S(1)} collective-permute-done((f32[10,5,16,128]{3,2,1,0:T(8,128)S(1)}, f32[10,5,16,128]{3,2,1,0:T(8,128)S(1)}, u32[]{:S(2)}, u32[]{:S(2)}) %collective-permute-start.1) | collective-permute-done | bytes 409632 | tf_op jit(solution)/shard_map/ppermute | solution.py:725
  16.0 1.2 %shard_map.39 = (f32[57,8,128]{2,1,0:T(8,128)S(1)}, f32[57,8,128]{2,1,0:T(8,128)S(1)}, f32[57,8,128]{2,1,0:T(8,128)S(1)}, f32[10,10,16,128]{3,2,1,0:T(8,128)S(1)}) custom-call(s32[1]{0:T(128)} %bitcast.rank_ref, f32[10,5,16,128]{3,2,1,0:T(8,128)S(1)} %get-tuple-element.34.u0, f32[10,5,16,128]{3,2,1,0:T(8,128)S(1)} %get-tuple-element.35.u3, ...), custom_call_target="tpu_custom_call" | custom-call | bytes 1 | tf_op jit(solution)/shard_map/pallas_call | solution.py:707
  17.2 1.3 %collective-permute-start.2 = (f32[57,8,128]{2,1,0:T(8,128)S(1)}, f32[57,8,128]{2,1,0:T(8,128)S(1)}, u32[]{:S(2)}, u32[]{:S(2)}) collective-permute-start(f32[57,8,128]{2,1,0:T(8,128)S(1)} %get-tuple-element.41), channel_id=1, source_target_pairs={{24,0},{0,8},{8,16},{16,24},{25,1},{1,9},{9,17},{17,25},{26,2},{2,... | collective-permute-start | bytes 700424 | tf_op jit(solution)/shard_map/ppermute | solution.py:725
  18.6 1.1 %collective-permute-start.3 = (f32[57,8,128]{2,1,0:T(8,128)S(1)}, f32[57,8,128]{2,1,0:T(8,128)S(1)}, u32[]{:S(2)}, u32[]{:S(2)}) collective-permute-start(f32[57,8,128]{2,1,0:T(8,128)S(1)} %get-tuple-element.42), channel_id=1, source_target_pairs={{16,0},{24,8},{0,16},{8,24},{17,1},{25,9},{1,17},{9,25},{18,2},{26... | collective-permute-start | bytes 700424 | tf_op jit(solution)/shard_map/ppermute | solution.py:725
  19.6 1.4 %collective-permute-start.4 = (f32[57,8,128]{2,1,0:T(8,128)S(1)}, f32[57,8,128]{2,1,0:T(8,128)S(1)}, u32[]{:S(2)}, u32[]{:S(2)}) collective-permute-start(f32[57,8,128]{2,1,0:T(8,128)S(1)} %get-tuple-element.43), channel_id=1, source_target_pairs={{8,0},{16,8},{24,16},{0,24},{9,1},{17,9},{25,17},{1,25},{10,2},{18... | collective-permute-start | bytes 700424 | tf_op jit(solution)/shard_map/ppermute | solution.py:725
  22.1 6.4 %collective-permute-done.6.q2 = f32[57,8,128]{2,1,0:T(8,128)S(1)} collective-permute-done((f32[57,8,128]{2,1,0:T(8,128)S(1)}, f32[57,8,128]{2,1,0:T(8,128)S(1)}, u32[]{:S(2)}, u32[]{:S(2)}) %collective-permute-start.6) | collective-permute-done | bytes 233504 | tf_op jit(solution)/shard_map/ppermute | solution.py:725
  28.5 11.9 %collective-permute-done.7.q3 = f32[57,8,128]{2,1,0:T(8,128)S(1)} collective-permute-done((f32[57,8,128]{2,1,0:T(8,128)S(1)}, f32[57,8,128]{2,1,0:T(8,128)S(1)}, u32[]{:S(2)}, u32[]{:S(2)}) %collective-permute-start.7) | collective-permute-done | bytes 233504 | tf_op jit(solution)/shard_map/ppermute | solution.py:725
  40.4 4.7 %shard_map.41 = (f32[10,10,16,128]{3,2,1,0:T(8,128)S(1)}, f32[10,10,16,128]{3,2,1,0:T(8,128)S(1)}) custom-call(s32[1]{0:T(128)} %bitcast.rank_ref, f32[16]{0:T(128)S(1)} %copy-done.1, f32[57,8,128]{2,1,0:T(8,128)S(1)} %get-tuple-element.44.start_ref, f32[57,8,128]{2,1,0:T(8,128)S(1)} %get-tuple-element.45.q0, f32[57,8,128]{2,1,0:T(8,128)S(1)} %collective-permute-done.5.q1, ...), custom_call_target="tpu_custom_call" | custom-call | bytes 1 | tf_op jit(solution)/shard_map/pallas_call | solution.py:707
  45.1 3.4 %collective-permute-done.3.q2 = f32[57,8,128]{2,1,0:T(8,128)S(1)} collective-permute-done((f32[57,8,128]{2,1,0:T(8,128)S(1)}, f32[57,8,128]{2,1,0:T(8,128)S(1)}, u32[]{:S(2)}, u32[]{:S(2)}) %collective-permute-start.3) | collective-permute-done | bytes 233504 | tf_op jit(solution)/shard_map/ppermute | solution.py:725
  48.5 1.9 %collective-permute-done.4.q3 = f32[57,8,128]{2,1,0:T(8,128)S(1)} collective-permute-done((f32[57,8,128]{2,1,0:T(8,128)S(1)}, f32[57,8,128]{2,1,0:T(8,128)S(1)}, u32[]{:S(2)}, u32[]{:S(2)}) %collective-permute-start.4) | collective-permute-done | bytes 233504 | tf_op jit(solution)/shard_map/ppermute | solution.py:725
  50.4 2.0 %shard_map.42 = (f32[10,5,16,128]{3,2,1,0:T(8,128)S(1)}, f32[10,5,16,128]{3,2,1,0:T(8,128)S(1)}, f32[50,8,128]{2,1,0:T(8,128)S(1)}, f32[50,8,128]{2,1,0:T(8,128)...) custom-call(s32[1]{0:T(128)} %bitcast.rank_ref, f32[16]{0:T(128)S(1)} %copy-done.1, ...), custom_call_target="tpu_custom_call" | custom-call | bytes 1 | tf_op jit(solution)/shard_map/pallas_call | solution.py:707
  52.9 1.3 %collective-permute-start.8 = (f32[10,5,16,128]{3,2,1,0:T(8,128)S(1)}, f32[10,5,16,128]{3,2,1,0:T(8,128)S(1)}, u32[]{:S(2)}, u32[]{:S(2)}) collective-permute-start(f32[10,5,16,128]{3,2,1,0:T(8,128)S(1)} %get-tuple-element.51.u3), channel_id=1, source_target_pairs={{7,0},{0,1},{1,2},{2,3},{3,4},{4,5},{5,6},{6,7},{15,8},{8,9},{9,10... | collective-permute-start | bytes 1228808 | tf_op jit(solution)/shard_map/ppermute | solution.py:725
  54.2 1.2 %collective-permute-start.14 = (f32[50,8,128]{2,1,0:T(8,128)S(1)}, f32[50,8,128]{2,1,0:T(8,128)S(1)}, u32[]{:S(2)}, u32[]{:S(2)}) collective-permute-start(f32[50,8,128]{2,1,0:T(8,128)S(1)} %get-tuple-element.59), channel_id=1, source_target_pairs={{16,0},{24,8},{0,16},{8,24},{17,1},{25,9},{1,17},{9,25},{18,2},{26... | collective-permute-start | bytes 614408 | tf_op jit(solution)/shard_map/ppermute | solution.py:725
  55.4 1.5 %collective-permute-start.15 = (f32[50,8,128]{2,1,0:T(8,128)S(1)}, f32[50,8,128]{2,1,0:T(8,128)S(1)}, u32[]{:S(2)}, u32[]{:S(2)}) collective-permute-start(f32[50,8,128]{2,1,0:T(8,128)S(1)} %get-tuple-element.60), channel_id=1, source_target_pairs={{8,0},{16,8},{24,16},{0,24},{9,1},{17,9},{25,17},{1,25},{10,2},{18... | collective-permute-start | bytes 614408 | tf_op jit(solution)/shard_map/ppermute | solution.py:725
  56.8 4.1 %shard_map.43.inner_ref = f32[10,10,16,128]{3,2,1,0:T(8,128)S(1)} custom-call(s32[1]{0:T(128)} %bitcast.rank_ref, f32[16]{0:T(128)S(1)} %copy-done.1, f32[10,5,16,128]{3,2,1,0:T(8,128)S(1)} %get-tuple-element.50.u0, f32[10,5,16,128]{3,2,1,0:T(8,128)S(1)} %get-tuple-element.51.u3, f32[57,8,128]{2,1,0:T(8,128)S(1)} %get-tuple-element.39.start_ref, ...), custom_call_target="tpu_custom_call" | custom-call | bytes 1 | tf_op jit(solution)/shard_map/pallas_call | solution.py:707
  60.9 2.1 %collective-permute-done.9.right_ref = f32[10,5,16,128]{3,2,1,0:T(8,128)S(1)} collective-permute-done((f32[10,5,16,128]{3,2,1,0:T(8,128)S(1)}, f32[10,5,16,128]{3,2,1,0:T(8,128)S(1)}, u32[]{:S(2)}, u32[]{:S(2)}) %collective-permute-start.9) | collective-permute-done | bytes 409632 | tf_op jit(solution)/shard_map/ppermute | solution.py:725
  63.2 1.6 %shard_map.44 = (f32[50,8,128]{2,1,0:T(8,128)S(1)}, f32[50,8,128]{2,1,0:T(8,128)S(1)}, f32[50,8,128]{2,1,0:T(8,128)S(1)}, f32[50,8,128]{2,1,0:T(8,128)S(1)}) custom-call(s32[1]{0:T(128)} %bitcast.rank_ref, f32[16]{0:T(128)S(1)} %copy-done.1, f32[10,5,16,128]{3,2,1,0:T(8,128)S(1)} %get-tuple-element.50.u0, f32[10,5,16,128]{3,2,1,0:T(8,128)S(1)} %get-tuple-element.51.u3, ...), custom_call_target="tpu_custom_call" | custom-call | bytes 1 | tf_op jit(solution)/shard_map/pallas_call | solution.py:707
  64.9 1.2 %collective-permute-start.11 = (f32[50,8,128]{2,1,0:T(8,128)S(1)}, f32[50,8,128]{2,1,0:T(8,128)S(1)}, u32[]{:S(2)}, u32[]{:S(2)}) collective-permute-start(f32[50,8,128]{2,1,0:T(8,128)S(1)} %get-tuple-element.55), channel_id=1, source_target_pairs={{16,0},{24,8},{0,16},{8,24},{17,1},{25,9},{1,17},{9,25},{18,2},{26... | collective-permute-start | bytes 614408 | tf_op jit(solution)/shard_map/ppermute | solution.py:725
  66.1 1.4 %collective-permute-start.12 = (f32[50,8,128]{2,1,0:T(8,128)S(1)}, f32[50,8,128]{2,1,0:T(8,128)S(1)}, u32[]{:S(2)}, u32[]{:S(2)}) collective-permute-start(f32[50,8,128]{2,1,0:T(8,128)S(1)} %get-tuple-element.56), channel_id=1, source_target_pairs={{8,0},{16,8},{24,16},{0,24},{9,1},{17,9},{25,17},{1,25},{10,2},{18... | collective-permute-start | bytes 614408 | tf_op jit(solution)/shard_map/ppermute | solution.py:725
  67.5 4.8 %collective-permute-done.14.q2 = f32[50,8,128]{2,1,0:T(8,128)S(1)} collective-permute-done((f32[50,8,128]{2,1,0:T(8,128)S(1)}, f32[50,8,128]{2,1,0:T(8,128)S(1)}, u32[]{:S(2)}, u32[]{:S(2)}) %collective-permute-start.14) | collective-permute-done | bytes 204832 | tf_op jit(solution)/shard_map/ppermute | solution.py:725
  72.3 10.3 %collective-permute-done.15.q3 = f32[50,8,128]{2,1,0:T(8,128)S(1)} collective-permute-done((f32[50,8,128]{2,1,0:T(8,128)S(1)}, f32[50,8,128]{2,1,0:T(8,128)S(1)}, u32[]{:S(2)}, u32[]{:S(2)}) %collective-permute-start.15) | collective-permute-done | bytes 204832 | tf_op jit(solution)/shard_map/ppermute | solution.py:725
  82.6 1.1 %shard_map.45.before_hbm = f32[3200,128]{1,0:T(8,128)} custom-call(s32[1]{0:T(128)} %bitcast.rank_ref, f32[50,8,128]{2,1,0:T(8,128)S(1)} %get-tuple-element.57.q0, f32[50,8,128]{2,1,0:T(8,128)S(1)} %collective-permute-done.13.q1, f32[50,8,128]{2,1,0:T(8,128)S(1)} %collective-permute-done.14.q2, f32[50,8,128]{2,1,0:T(8,128)S(1)} %collective-permute-done.15.q3), custom_call_target="tpu_custom_call" | custom-call | bytes 1 | tf_op jit(solution)/shard_map/pallas_call | solution.py:707
  83.8 1.7 %collective-permute-done.10.q1 = f32[50,8,128]{2,1,0:T(8,128)S(1)} collective-permute-done((f32[50,8,128]{2,1,0:T(8,128)S(1)}, f32[50,8,128]{2,1,0:T(8,128)S(1)}, u32[]{:S(2)}, u32[]{:S(2)}) %collective-permute-start.10) | collective-permute-done | bytes 204832 | tf_op jit(solution)/shard_map/ppermute | solution.py:725
  85.5 4.1 %collective-permute-done.11.q2 = f32[50,8,128]{2,1,0:T(8,128)S(1)} collective-permute-done((f32[50,8,128]{2,1,0:T(8,128)S(1)}, f32[50,8,128]{2,1,0:T(8,128)S(1)}, u32[]{:S(2)}, u32[]{:S(2)}) %collective-permute-start.11) | collective-permute-done | bytes 204832 | tf_op jit(solution)/shard_map/ppermute | solution.py:725
  89.6 1.8 %collective-permute-done.12.q3 = f32[50,8,128]{2,1,0:T(8,128)S(1)} collective-permute-done((f32[50,8,128]{2,1,0:T(8,128)S(1)}, f32[50,8,128]{2,1,0:T(8,128)S(1)}, u32[]{:S(2)}, u32[]{:S(2)}) %collective-permute-start.12) | collective-permute-done | bytes 204832 | tf_op jit(solution)/shard_map/ppermute | solution.py:725
  91.4 1.1 %shard_map.46 = f32[3200,128]{1,0:T(8,128)} custom-call(s32[1]{0:T(128)} %bitcast.rank_ref, f32[50,8,128]{2,1,0:T(8,128)S(1)} %get-tuple-element.53.q0, f32[50,8,128]{2,1,0:T(8,128)S(1)} %collective-permute-done.10.q1, f32[50,8,128]{2,1,0:T(8,128)S(1)} %collective-permute-done.11.q2, ...), custom_call_target="tpu_custom_call", output_to_operand_aliasing={{}: (5, {})} | custom-call | bytes 1 | tf_op jit(solution)/shard_map/pallas_call | solution.py:707
  (14 shorter events, 3.3 us)
Async XLA Ops:
  4.9 10.3 %collective-permute-start.1 = (f32[10,5,16,128]{3,2,1,0:T(8,128)S(1)}, f32[10,5,16,128]{3,2,1,0:T(8,128)S(1)}, u32[]{:S(2)}, u32[]{:S(2)}) collective-permute-start(f32[10,5,16,128]{3,2,1,0:T(8,128)S(1)} %get-tuple-element.34.u0), channel_id=1, source_target_pairs={{1,0},{2,1},{3,2},{4,3},{5,4},{6,5},{7,6},{0,7},{9,8},{10,9},{11,1... | collective-permute-start | bytes 1228808 | tf_op jit(solution)/shard_map/ppermute | solution.py:725
  5.6 10.4 %collective-permute-start = (f32[10,5,16,128]{3,2,1,0:T(8,128)S(1)}, f32[10,5,16,128]{3,2,1,0:T(8,128)S(1)}, u32[]{:S(2)}, u32[]{:S(2)}) collective-permute-start(f32[10,5,16,128]{3,2,1,0:T(8,128)S(1)} %get-tuple-element.35.u3), channel_id=1, source_target_pairs={{7,0},{0,1},{1,2},{2,3},{3,4},{4,5},{5,6},{6,7},{15,8},{8,9},{9,10... | collective-permute-start | bytes 1228808 | tf_op jit(solution)/shard_map/ppermute | solution.py:725
  6.8 12.9 %collective-permute-start.5 = (f32[57,8,128]{2,1,0:T(8,128)S(1)}, f32[57,8,128]{2,1,0:T(8,128)S(1)}, u32[]{:S(2)}, u32[]{:S(2)}) collective-permute-start(f32[57,8,128]{2,1,0:T(8,128)S(1)} %get-tuple-element.46), channel_id=1, source_target_pairs={{24,0},{0,8},{8,16},{16,24},{25,1},{1,9},{9,17},{17,25},{26,2},{2,... | collective-permute-start | bytes 700424 | tf_op jit(solution)/shard_map/ppermute | solution.py:725
  8.1 20.4 %collective-permute-start.6 = (f32[57,8,128]{2,1,0:T(8,128)S(1)}, f32[57,8,128]{2,1,0:T(8,128)S(1)}, u32[]{:S(2)}, u32[]{:S(2)}) collective-permute-start(f32[57,8,128]{2,1,0:T(8,128)S(1)} %get-tuple-element.47), channel_id=1, source_target_pairs={{16,0},{24,8},{0,16},{8,24},{17,1},{25,9},{1,17},{9,25},{18,2},{26... | collective-permute-start | bytes 700424 | tf_op jit(solution)/shard_map/ppermute | solution.py:725
  9.1 31.3 %collective-permute-start.7 = (f32[57,8,128]{2,1,0:T(8,128)S(1)}, f32[57,8,128]{2,1,0:T(8,128)S(1)}, u32[]{:S(2)}, u32[]{:S(2)}) collective-permute-start(f32[57,8,128]{2,1,0:T(8,128)S(1)} %get-tuple-element.48), channel_id=1, source_target_pairs={{8,0},{16,8},{24,16},{0,24},{9,1},{17,9},{25,17},{1,25},{10,2},{18... | collective-permute-start | bytes 700424 | tf_op jit(solution)/shard_map/ppermute | solution.py:725
  14.1 6.9 %copy-start = (f32[5,4,4,4,1,1280]{5,4,3,2,1,0:T(1,128)S(1)}, f32[5,4,4,4,1,1280]{5,4,3,2,1,0:T(1,128)}, u32[]{:S(2)}) copy-start(f32[5,4,4,4,1,1280]{5,4,3,2,1,0:T(1,128)} %param.3) | copy-start | bytes 4915204
  17.2 27.9 %collective-permute-start.2 = (f32[57,8,128]{2,1,0:T(8,128)S(1)}, f32[57,8,128]{2,1,0:T(8,128)S(1)}, u32[]{:S(2)}, u32[]{:S(2)}) collective-permute-start(f32[57,8,128]{2,1,0:T(8,128)S(1)} %get-tuple-element.41), channel_id=1, source_target_pairs={{24,0},{0,8},{8,16},{16,24},{25,1},{1,9},{9,17},{17,25},{26,2},{2,... | collective-permute-start | bytes 700424 | tf_op jit(solution)/shard_map/ppermute | solution.py:725
  18.6 29.9 %collective-permute-start.3 = (f32[57,8,128]{2,1,0:T(8,128)S(1)}, f32[57,8,128]{2,1,0:T(8,128)S(1)}, u32[]{:S(2)}, u32[]{:S(2)}) collective-permute-start(f32[57,8,128]{2,1,0:T(8,128)S(1)} %get-tuple-element.42), channel_id=1, source_target_pairs={{16,0},{24,8},{0,16},{8,24},{17,1},{25,9},{1,17},{9,25},{18,2},{26... | collective-permute-start | bytes 700424 | tf_op jit(solution)/shard_map/ppermute | solution.py:725
  19.6 30.8 %collective-permute-start.4 = (f32[57,8,128]{2,1,0:T(8,128)S(1)}, f32[57,8,128]{2,1,0:T(8,128)S(1)}, u32[]{:S(2)}, u32[]{:S(2)}) collective-permute-start(f32[57,8,128]{2,1,0:T(8,128)S(1)} %get-tuple-element.43), channel_id=1, source_target_pairs={{8,0},{16,8},{24,16},{0,24},{9,1},{17,9},{25,17},{1,25},{10,2},{18... | collective-permute-start | bytes 700424 | tf_op jit(solution)/shard_map/ppermute | solution.py:725
  21.0 19.4 %copy-start.1 = (f32[16]{0:T(128)S(1)}, f32[16]{0:T(128)}, u32[]{:S(2)}) copy-start(f32[16]{0:T(128)} %constant.7.clone.table_ref) | copy-start | bytes 196
  52.4 10.6 %collective-permute-start.9 = (f32[10,5,16,128]{3,2,1,0:T(8,128)S(1)}, f32[10,5,16,128]{3,2,1,0:T(8,128)S(1)}, u32[]{:S(2)}, u32[]{:S(2)}) collective-permute-start(f32[10,5,16,128]{3,2,1,0:T(8,128)S(1)} %get-tuple-element.50.u0), channel_id=1, source_target_pairs={{1,0},{2,1},{3,2},{4,3},{5,4},{6,5},{7,6},{0,7},{9,8},{10,9},{11,1... | collective-permute-start | bytes 1228808 | tf_op jit(solution)/shard_map/ppermute | solution.py:725
  52.9 10.3 %collective-permute-start.8 = (f32[10,5,16,128]{3,2,1,0:T(8,128)S(1)}, f32[10,5,16,128]{3,2,1,0:T(8,128)S(1)}, u32[]{:S(2)}, u32[]{:S(2)}) collective-permute-start(f32[10,5,16,128]{3,2,1,0:T(8,128)S(1)} %get-tuple-element.51.u3), channel_id=1, source_target_pairs={{7,0},{0,1},{1,2},{2,3},{3,4},{4,5},{5,6},{6,7},{15,8},{8,9},{9,10... | collective-permute-start | bytes 1228808 | tf_op jit(solution)/shard_map/ppermute | solution.py:725
  54.2 11.9 %collective-permute-start.13 = (f32[50,8,128]{2,1,0:T(8,128)S(1)}, f32[50,8,128]{2,1,0:T(8,128)S(1)}, u32[]{:S(2)}, u32[]{:S(2)}) collective-permute-start(f32[50,8,128]{2,1,0:T(8,128)S(1)} %get-tuple-element.58), channel_id=1, source_target_pairs={{24,0},{0,8},{8,16},{16,24},{25,1},{1,9},{9,17},{17,25},{26,2},{2,... | collective-permute-start | bytes 614408 | tf_op jit(solution)/shard_map/ppermute | solution.py:725
  54.2 18.2 %collective-permute-start.14 = (f32[50,8,128]{2,1,0:T(8,128)S(1)}, f32[50,8,128]{2,1,0:T(8,128)S(1)}, u32[]{:S(2)}, u32[]{:S(2)}) collective-permute-start(f32[50,8,128]{2,1,0:T(8,128)S(1)} %get-tuple-element.59), channel_id=1, source_target_pairs={{16,0},{24,8},{0,16},{8,24},{17,1},{25,9},{1,17},{9,25},{18,2},{26... | collective-permute-start | bytes 614408 | tf_op jit(solution)/shard_map/ppermute | solution.py:725
  55.4 27.3 %collective-permute-start.15 = (f32[50,8,128]{2,1,0:T(8,128)S(1)}, f32[50,8,128]{2,1,0:T(8,128)S(1)}, u32[]{:S(2)}, u32[]{:S(2)}) collective-permute-start(f32[50,8,128]{2,1,0:T(8,128)S(1)} %get-tuple-element.60), channel_id=1, source_target_pairs={{8,0},{16,8},{24,16},{0,24},{9,1},{17,9},{25,17},{1,25},{10,2},{18... | collective-permute-start | bytes 614408 | tf_op jit(solution)/shard_map/ppermute | solution.py:725
  64.8 20.7 %collective-permute-start.10 = (f32[50,8,128]{2,1,0:T(8,128)S(1)}, f32[50,8,128]{2,1,0:T(8,128)S(1)}, u32[]{:S(2)}, u32[]{:S(2)}) collective-permute-start(f32[50,8,128]{2,1,0:T(8,128)S(1)} %get-tuple-element.54), channel_id=1, source_target_pairs={{24,0},{0,8},{8,16},{16,24},{25,1},{1,9},{9,17},{17,25},{26,2},{2,... | collective-permute-start | bytes 614408 | tf_op jit(solution)/shard_map/ppermute | solution.py:725
  64.9 24.7 %collective-permute-start.11 = (f32[50,8,128]{2,1,0:T(8,128)S(1)}, f32[50,8,128]{2,1,0:T(8,128)S(1)}, u32[]{:S(2)}, u32[]{:S(2)}) collective-permute-start(f32[50,8,128]{2,1,0:T(8,128)S(1)} %get-tuple-element.55), channel_id=1, source_target_pairs={{16,0},{24,8},{0,16},{8,24},{17,1},{25,9},{1,17},{9,25},{18,2},{26... | collective-permute-start | bytes 614408 | tf_op jit(solution)/shard_map/ppermute | solution.py:725
  66.1 25.3 %collective-permute-start.12 = (f32[50,8,128]{2,1,0:T(8,128)S(1)}, f32[50,8,128]{2,1,0:T(8,128)S(1)}, u32[]{:S(2)}, u32[]{:S(2)}) collective-permute-start(f32[50,8,128]{2,1,0:T(8,128)S(1)} %get-tuple-element.56), channel_id=1, source_target_pairs={{8,0},{16,8},{24,16},{0,24},{9,1},{17,9},{25,17},{1,25},{10,2},{18... | collective-permute-start | bytes 614408 | tf_op jit(solution)/shard_map/ppermute | solution.py:725

commit v4 on v3

--- a/solution.py
+++ b/solution.py
@@ -558,7 +558,7 @@
                         states[which][5 * pair + i, v, 8 * r : 8 * r + 8, :] = tiles[i][which]
         return carry
 
-    lax.fori_loop(0, 5, one_variable, 0)
+    lax.fori_loop(0, 5, one_variable, 0, unroll=True)
 
 
 def assemble_halos(weight, start_ref, rates, halos):
@@ -589,7 +589,7 @@
                     outs[d][(5 * place + v) * 5 + i] = total
         return carry
 
-    lax.fori_loop(0, 5, one_variable, 0)
+    lax.fori_loop(0, 5, one_variable, 0, unroll=True)
 
 
 def middle_kernel(rank_ref, table_ref, start_ref, q0, q1, q2, q3, mid_ref, edge_ref, u1, u2, h1, h2, pz_ref, py1, py2, coef_ref):
@@ -622,7 +622,7 @@
         volume_tile(t, {0: u0, 3: u3}, {1: False, 2: False}, None, start, emit)
         return carry
 
-    lax.fori_loop(0, TILES, one_tile, 0)
+    lax.fori_loop(0, TILES, one_tile, 0, unroll=5)
     send_increments(rank_ref, table_ref, r_ref, (0, 1), (o0, o1, o2, o3))
 
 

time: 92.7 us -> 92.1 us (level)
  Pallas kernels: 25.2 us -> 23.9 us
    pallas_call x10, Pallas kernels: 25.2 us -> 23.9 us  [call(): pl.pallas_call(kernel, out_shape=[f32(*shape) for _, shape in outs], in_s...]
  transfers between devices with their start and end apart: 16 -> 16, of which waited for: 13 -> 13; matrix products, arithmetic and copies ran while one was open for 0% -> 0% of each run, Pallas kernels for 19% -> 18%
where the time goes in v4:
time: 92.1 us; the launch traced here: 91.9 us
  waiting for transfers between devices  51.3 us (56%)
  Pallas kernels  23.9 us (26%)
  starting transfers between devices  16.6 us (18%)
    ppermute x16, waiting for transfers between devices, shifted(): lax.ppermute(block, axis, [((i - distance) % count, i) for i in range(cou...  51.3 us
    pallas_call x10, Pallas kernels, call(): pl.pallas_call(kernel, out_shape=[f32(*shape) for _, shape in outs], in_s...  23.9 us
    ppermute x16, starting transfers between devices, shifted(): lax.ppermute(block, axis, [((i - distance) % count, i) for i in range(cou...  16.6 us
  transfers between devices with their start and end apart: 16, of which 13 were waited for; matrix products, arithmetic and copies ran while one was open for 0% of the time, Pallas kernels for 18%

profile of v4, /device:TPU:13, one launch (start us, length us, event | category | flops | bytes accessed | tf_op | source)
XLA Modules:
  0.0 91.9 jit_solution(17999070738079407869)
XLA Ops:
  0.0 4.9 %shard_map.37 = (f32[10,5,16,128]{3,2,1,0:T(8,128)S(1)}, f32[10,5,16,128]{3,2,1,0:T(8,128)S(1)}, f32[10,5,16,128]{3,2,1,0:T(8,128)S(1)}, f32[10,5,16,128]{3,2,1,...) custom-call(s32[1]{0:T(128)} %bitcast.rank_ref, ...), custom_call_target="tpu_custom_call" | custom-call | bytes 1 | tf_op jit(solution)/shard_map/pallas_call | solution.py:707
  5.6 1.2 %collective-permute-start = (f32[10,5,16,128]{3,2,1,0:T(8,128)S(1)}, f32[10,5,16,128]{3,2,1,0:T(8,128)S(1)}, u32[]{:S(2)}, u32[]{:S(2)}) collective-permute-start(f32[10,5,16,128]{3,2,1,0:T(8,128)S(1)} %get-tuple-element.35.u3), channel_id=1, source_target_pairs={{7,0},{0,1},{1,2},{2,3},{3,4},{4,5},{5,6},{6,7},{15,8},{8,9},{9,10... | collective-permute-start | bytes 1228808 | tf_op jit(solution)/shard_map/ppermute | solution.py:725
  6.8 1.3 %collective-permute-start.5 = (f32[57,8,128]{2,1,0:T(8,128)S(1)}, f32[57,8,128]{2,1,0:T(8,128)S(1)}, u32[]{:S(2)}, u32[]{:S(2)}) collective-permute-start(f32[57,8,128]{2,1,0:T(8,128)S(1)} %get-tuple-element.46), channel_id=1, source_target_pairs={{24,0},{0,8},{8,16},{16,24},{25,1},{1,9},{9,17},{17,25},{26,2},{2,... | collective-permute-start | bytes 700424 | tf_op jit(solution)/shard_map/ppermute | solution.py:725
  8.1 1.0 %collective-permute-start.6 = (f32[57,8,128]{2,1,0:T(8,128)S(1)}, f32[57,8,128]{2,1,0:T(8,128)S(1)}, u32[]{:S(2)}, u32[]{:S(2)}) collective-permute-start(f32[57,8,128]{2,1,0:T(8,128)S(1)} %get-tuple-element.47), channel_id=1, source_target_pairs={{16,0},{24,8},{0,16},{8,24},{17,1},{25,9},{1,17},{9,25},{18,2},{26... | collective-permute-start | bytes 700424 | tf_op jit(solution)/shard_map/ppermute | solution.py:725
  9.1 1.5 %collective-permute-start.7 = (f32[57,8,128]{2,1,0:T(8,128)S(1)}, f32[57,8,128]{2,1,0:T(8,128)S(1)}, u32[]{:S(2)}, u32[]{:S(2)}) collective-permute-start(f32[57,8,128]{2,1,0:T(8,128)S(1)} %get-tuple-element.48), channel_id=1, source_target_pairs={{8,0},{16,8},{24,16},{0,24},{9,1},{17,9},{25,17},{1,25},{10,2},{18... | collective-permute-start | bytes 700424 | tf_op jit(solution)/shard_map/ppermute | solution.py:725
  10.6 3.5 %shard_map.38.inner_ref = f32[10,10,16,128]{3,2,1,0:T(8,128)S(1)} custom-call(f32[10,5,16,128]{3,2,1,0:T(8,128)S(1)} %get-tuple-element.34.u0, f32[10,5,16,128]{3,2,1,0:T(8,128)S(1)} %get-tuple-element.36.u1, f32[10,5,16,128]{3,2,1,0:T(8,128)S(1)} %get-tuple-element.37.u2, f32[10,5,16,128]{3,2,1,0:T(8,128)S(1)} %get-tuple-element.35.u3), custom_call_target="tpu_custom_call" | custom-call | bytes 1 | tf_op jit(solution)/shard_map/pallas_call | solution.py:707
  14.1 1.1 %collective-permute-done.1.right_ref = f32[10,5,16,128]{3,2,1,0:T(8,128)S(1)} collective-permute-done((f32[10,5,16,128]{3,2,1,0:T(8,128)S(1)}, f32[10,5,16,128]{3,2,1,0:T(8,128)S(1)}, u32[]{:S(2)}, u32[]{:S(2)}) %collective-permute-start.1) | collective-permute-done | bytes 409632 | tf_op jit(solution)/shard_map/ppermute | solution.py:725
  16.0 1.2 %shard_map.39 = (f32[57,8,128]{2,1,0:T(8,128)S(1)}, f32[57,8,128]{2,1,0:T(8,128)S(1)}, f32[57,8,128]{2,1,0:T(8,128)S(1)}, f32[10,10,16,128]{3,2,1,0:T(8,128)S(1)}) custom-call(s32[1]{0:T(128)} %bitcast.rank_ref, f32[10,5,16,128]{3,2,1,0:T(8,128)S(1)} %get-tuple-element.34.u0, f32[10,5,16,128]{3,2,1,0:T(8,128)S(1)} %get-tuple-element.35.u3, ...), custom_call_target="tpu_custom_call" | custom-call | bytes 1 | tf_op jit(solution)/shard_map/pallas_call | solution.py:707
  17.2 1.3 %collective-permute-start.2 = (f32[57,8,128]{2,1,0:T(8,128)S(1)}, f32[57,8,128]{2,1,0:T(8,128)S(1)}, u32[]{:S(2)}, u32[]{:S(2)}) collective-permute-start(f32[57,8,128]{2,1,0:T(8,128)S(1)} %get-tuple-element.41), channel_id=1, source_target_pairs={{24,0},{0,8},{8,16},{16,24},{25,1},{1,9},{9,17},{17,25},{26,2},{2,... | collective-permute-start | bytes 700424 | tf_op jit(solution)/shard_map/ppermute | solution.py:725
  18.6 1.1 %collective-permute-start.3 = (f32[57,8,128]{2,1,0:T(8,128)S(1)}, f32[57,8,128]{2,1,0:T(8,128)S(1)}, u32[]{:S(2)}, u32[]{:S(2)}) collective-permute-start(f32[57,8,128]{2,1,0:T(8,128)S(1)} %get-tuple-element.42), channel_id=1, source_target_pairs={{16,0},{24,8},{0,16},{8,24},{17,1},{25,9},{1,17},{9,25},{18,2},{26... | collective-permute-start | bytes 700424 | tf_op jit(solution)/shard_map/ppermute | solution.py:725
  19.6 1.4 %collective-permute-start.4 = (f32[57,8,128]{2,1,0:T(8,128)S(1)}, f32[57,8,128]{2,1,0:T(8,128)S(1)}, u32[]{:S(2)}, u32[]{:S(2)}) collective-permute-start(f32[57,8,128]{2,1,0:T(8,128)S(1)} %get-tuple-element.43), channel_id=1, source_target_pairs={{8,0},{16,8},{24,16},{0,24},{9,1},{17,9},{25,17},{1,25},{10,2},{18... | collective-permute-start | bytes 700424 | tf_op jit(solution)/shard_map/ppermute | solution.py:725
  22.1 6.4 %collective-permute-done.6.q2 = f32[57,8,128]{2,1,0:T(8,128)S(1)} collective-permute-done((f32[57,8,128]{2,1,0:T(8,128)S(1)}, f32[57,8,128]{2,1,0:T(8,128)S(1)}, u32[]{:S(2)}, u32[]{:S(2)}) %collective-permute-start.6) | collective-permute-done | bytes 233504 | tf_op jit(solution)/shard_map/ppermute | solution.py:725
  28.5 11.9 %collective-permute-done.7.q3 = f32[57,8,128]{2,1,0:T(8,128)S(1)} collective-permute-done((f32[57,8,128]{2,1,0:T(8,128)S(1)}, f32[57,8,128]{2,1,0:T(8,128)S(1)}, u32[]{:S(2)}, u32[]{:S(2)}) %collective-permute-start.7) | collective-permute-done | bytes 233504 | tf_op jit(solution)/shard_map/ppermute | solution.py:725
  40.4 4.3 %shard_map.41 = (f32[10,10,16,128]{3,2,1,0:T(8,128)S(1)}, f32[10,10,16,128]{3,2,1,0:T(8,128)S(1)}) custom-call(s32[1]{0:T(128)} %bitcast.rank_ref, f32[16]{0:T(128)S(1)} %copy-done.1, f32[57,8,128]{2,1,0:T(8,128)S(1)} %get-tuple-element.44.start_ref, f32[57,8,128]{2,1,0:T(8,128)S(1)} %get-tuple-element.45.q0, f32[57,8,128]{2,1,0:T(8,128)S(1)} %collective-permute-done.5.q1, ...), custom_call_target="tpu_custom_call" | custom-call | bytes 1 | tf_op jit(solution)/shard_map/pallas_call | solution.py:707
  44.7 3.7 %collective-permute-done.3.q2 = f32[57,8,128]{2,1,0:T(8,128)S(1)} collective-permute-done((f32[57,8,128]{2,1,0:T(8,128)S(1)}, f32[57,8,128]{2,1,0:T(8,128)S(1)}, u32[]{:S(2)}, u32[]{:S(2)}) %collective-permute-start.3) | collective-permute-done | bytes 233504 | tf_op jit(solution)/shard_map/ppermute | solution.py:725
  48.5 1.9 %collective-permute-done.4.q3 = f32[57,8,128]{2,1,0:T(8,128)S(1)} collective-permute-done((f32[57,8,128]{2,1,0:T(8,128)S(1)}, f32[57,8,128]{2,1,0:T(8,128)S(1)}, u32[]{:S(2)}, u32[]{:S(2)}) %collective-permute-start.4) | collective-permute-done | bytes 233504 | tf_op jit(solution)/shard_map/ppermute | solution.py:725
  50.4 1.4 %shard_map.42 = (f32[10,5,16,128]{3,2,1,0:T(8,128)S(1)}, f32[10,5,16,128]{3,2,1,0:T(8,128)S(1)}, f32[50,8,128]{2,1,0:T(8,128)S(1)}, f32[50,8,128]{2,1,0:T(8,128)...) custom-call(s32[1]{0:T(128)} %bitcast.rank_ref, f32[16]{0:T(128)S(1)} %copy-done.1, ...), custom_call_target="tpu_custom_call" | custom-call | bytes 1 | tf_op jit(solution)/shard_map/pallas_call | solution.py:707
  52.3 1.3 %collective-permute-start.8 = (f32[10,5,16,128]{3,2,1,0:T(8,128)S(1)}, f32[10,5,16,128]{3,2,1,0:T(8,128)S(1)}, u32[]{:S(2)}, u32[]{:S(2)}) collective-permute-start(f32[10,5,16,128]{3,2,1,0:T(8,128)S(1)} %get-tuple-element.51.u3), channel_id=1, source_target_pairs={{7,0},{0,1},{1,2},{2,3},{3,4},{4,5},{5,6},{6,7},{15,8},{8,9},{9,10... | collective-permute-start | bytes 1228808 | tf_op jit(solution)/shard_map/ppermute | solution.py:725
  53.6 1.2 %collective-permute-start.14 = (f32[50,8,128]{2,1,0:T(8,128)S(1)}, f32[50,8,128]{2,1,0:T(8,128)S(1)}, u32[]{:S(2)}, u32[]{:S(2)}) collective-permute-start(f32[50,8,128]{2,1,0:T(8,128)S(1)} %get-tuple-element.59), channel_id=1, source_target_pairs={{16,0},{24,8},{0,16},{8,24},{17,1},{25,9},{1,17},{9,25},{18,2},{26... | collective-permute-start | bytes 614408 | tf_op jit(solution)/shard_map/ppermute | solution.py:725
  54.7 1.5 %collective-permute-start.15 = (f32[50,8,128]{2,1,0:T(8,128)S(1)}, f32[50,8,128]{2,1,0:T(8,128)S(1)}, u32[]{:S(2)}, u32[]{:S(2)}) collective-permute-start(f32[50,8,128]{2,1,0:T(8,128)S(1)} %get-tuple-element.60), channel_id=1, source_target_pairs={{8,0},{16,8},{24,16},{0,24},{9,1},{17,9},{25,17},{1,25},{10,2},{18... | collective-permute-start | bytes 614408 | tf_op jit(solution)/shard_map/ppermute | solution.py:725
  56.2 4.1 %shard_map.43.inner_ref = f32[10,10,16,128]{3,2,1,0:T(8,128)S(1)} custom-call(s32[1]{0:T(128)} %bitcast.rank_ref, f32[16]{0:T(128)S(1)} %copy-done.1, f32[10,5,16,128]{3,2,1,0:T(8,128)S(1)} %get-tuple-element.50.u0, f32[10,5,16,128]{3,2,1,0:T(8,128)S(1)} %get-tuple-element.51.u3, f32[57,8,128]{2,1,0:T(8,128)S(1)} %get-tuple-element.39.start_ref, ...), custom_call_target="tpu_custom_call" | custom-call | bytes 1 | tf_op jit(solution)/shard_map/pallas_call | solution.py:707
  60.3 2.1 %collective-permute-done.9.right_ref = f32[10,5,16,128]{3,2,1,0:T(8,128)S(1)} collective-permute-done((f32[10,5,16,128]{3,2,1,0:T(8,128)S(1)}, f32[10,5,16,128]{3,2,1,0:T(8,128)S(1)}, u32[]{:S(2)}, u32[]{:S(2)}) %collective-permute-start.9) | collective-permute-done | bytes 409632 | tf_op jit(solution)/shard_map/ppermute | solution.py:725
  62.5 1.4 %shard_map.44 = (f32[50,8,128]{2,1,0:T(8,128)S(1)}, f32[50,8,128]{2,1,0:T(8,128)S(1)}, f32[50,8,128]{2,1,0:T(8,128)S(1)}, f32[50,8,128]{2,1,0:T(8,128)S(1)}) custom-call(s32[1]{0:T(128)} %bitcast.rank_ref, f32[16]{0:T(128)S(1)} %copy-done.1, f32[10,5,16,128]{3,2,1,0:T(8,128)S(1)} %get-tuple-element.50.u0, f32[10,5,16,128]{3,2,1,0:T(8,128)S(1)} %get-tuple-element.51.u3, ...), custom_call_target="tpu_custom_call" | custom-call | bytes 1 | tf_op jit(solution)/shard_map/pallas_call | solution.py:707
  64.0 1.2 %collective-permute-start.11 = (f32[50,8,128]{2,1,0:T(8,128)S(1)}, f32[50,8,128]{2,1,0:T(8,128)S(1)}, u32[]{:S(2)}, u32[]{:S(2)}) collective-permute-start(f32[50,8,128]{2,1,0:T(8,128)S(1)} %get-tuple-element.55), channel_id=1, source_target_pairs={{16,0},{24,8},{0,16},{8,24},{17,1},{25,9},{1,17},{9,25},{18,2},{26... | collective-permute-start | bytes 614408 | tf_op jit(solution)/shard_map/ppermute | solution.py:725
  65.2 1.4 %collective-permute-start.12 = (f32[50,8,128]{2,1,0:T(8,128)S(1)}, f32[50,8,128]{2,1,0:T(8,128)S(1)}, u32[]{:S(2)}, u32[]{:S(2)}) collective-permute-start(f32[50,8,128]{2,1,0:T(8,128)S(1)} %get-tuple-element.56), channel_id=1, source_target_pairs={{8,0},{16,8},{24,16},{0,24},{9,1},{17,9},{25,17},{1,25},{10,2},{18... | collective-permute-start | bytes 614408 | tf_op jit(solution)/shard_map/ppermute | solution.py:725
  66.6 5.1 %collective-permute-done.14.q2 = f32[50,8,128]{2,1,0:T(8,128)S(1)} collective-permute-done((f32[50,8,128]{2,1,0:T(8,128)S(1)}, f32[50,8,128]{2,1,0:T(8,128)S(1)}, u32[]{:S(2)}, u32[]{:S(2)}) %collective-permute-start.14) | collective-permute-done | bytes 204832 | tf_op jit(solution)/shard_map/ppermute | solution.py:725
  71.7 10.3 %collective-permute-done.15.q3 = f32[50,8,128]{2,1,0:T(8,128)S(1)} collective-permute-done((f32[50,8,128]{2,1,0:T(8,128)S(1)}, f32[50,8,128]{2,1,0:T(8,128)S(1)}, u32[]{:S(2)}, u32[]{:S(2)}) %collective-permute-start.15) | collective-permute-done | bytes 204832 | tf_op jit(solution)/shard_map/ppermute | solution.py:725
  82.0 1.1 %shard_map.45.before_hbm = f32[3200,128]{1,0:T(8,128)} custom-call(s32[1]{0:T(128)} %bitcast.rank_ref, f32[50,8,128]{2,1,0:T(8,128)S(1)} %get-tuple-element.57.q0, f32[50,8,128]{2,1,0:T(8,128)S(1)} %collective-permute-done.13.q1, f32[50,8,128]{2,1,0:T(8,128)S(1)} %collective-permute-done.14.q2, f32[50,8,128]{2,1,0:T(8,128)S(1)} %collective-permute-done.15.q3), custom_call_target="tpu_custom_call" | custom-call | bytes 1 | tf_op jit(solution)/shard_map/pallas_call | solution.py:707
  83.2 1.7 %collective-permute-done.10.q1 = f32[50,8,128]{2,1,0:T(8,128)S(1)} collective-permute-done((f32[50,8,128]{2,1,0:T(8,128)S(1)}, f32[50,8,128]{2,1,0:T(8,128)S(1)}, u32[]{:S(2)}, u32[]{:S(2)}) %collective-permute-start.10) | collective-permute-done | bytes 204832 | tf_op jit(solution)/shard_map/ppermute | solution.py:725
  84.9 4.1 %collective-permute-done.11.q2 = f32[50,8,128]{2,1,0:T(8,128)S(1)} collective-permute-done((f32[50,8,128]{2,1,0:T(8,128)S(1)}, f32[50,8,128]{2,1,0:T(8,128)S(1)}, u32[]{:S(2)}, u32[]{:S(2)}) %collective-permute-start.11) | collective-permute-done | bytes 204832 | tf_op jit(solution)/shard_map/ppermute | solution.py:725
  89.0 1.8 %collective-permute-done.12.q3 = f32[50,8,128]{2,1,0:T(8,128)S(1)} collective-permute-done((f32[50,8,128]{2,1,0:T(8,128)S(1)}, f32[50,8,128]{2,1,0:T(8,128)S(1)}, u32[]{:S(2)}, u32[]{:S(2)}) %collective-permute-start.12) | collective-permute-done | bytes 204832 | tf_op jit(solution)/shard_map/ppermute | solution.py:725
  90.8 1.1 %shard_map.46 = f32[3200,128]{1,0:T(8,128)} custom-call(s32[1]{0:T(128)} %bitcast.rank_ref, f32[50,8,128]{2,1,0:T(8,128)S(1)} %get-tuple-element.53.q0, f32[50,8,128]{2,1,0:T(8,128)S(1)} %collective-permute-done.10.q1, f32[50,8,128]{2,1,0:T(8,128)S(1)} %collective-permute-done.11.q2, ...), custom_call_target="tpu_custom_call", output_to_operand_aliasing={{}: (5, {})} | custom-call | bytes 1 | tf_op jit(solution)/shard_map/pallas_call | solution.py:707
  (14 shorter events, 3.3 us)
Async XLA Ops:
  4.9 10.3 %collective-permute-start.1 = (f32[10,5,16,128]{3,2,1,0:T(8,128)S(1)}, f32[10,5,16,128]{3,2,1,0:T(8,128)S(1)}, u32[]{:S(2)}, u32[]{:S(2)}) collective-permute-start(f32[10,5,16,128]{3,2,1,0:T(8,128)S(1)} %get-tuple-element.34.u0), channel_id=1, source_target_pairs={{1,0},{2,1},{3,2},{4,3},{5,4},{6,5},{7,6},{0,7},{9,8},{10,9},{11,1... | collective-permute-start | bytes 1228808 | tf_op jit(solution)/shard_map/ppermute | solution.py:725
  5.6 10.4 %collective-permute-start = (f32[10,5,16,128]{3,2,1,0:T(8,128)S(1)}, f32[10,5,16,128]{3,2,1,0:T(8,128)S(1)}, u32[]{:S(2)}, u32[]{:S(2)}) collective-permute-start(f32[10,5,16,128]{3,2,1,0:T(8,128)S(1)} %get-tuple-element.35.u3), channel_id=1, source_target_pairs={{7,0},{0,1},{1,2},{2,3},{3,4},{4,5},{5,6},{6,7},{15,8},{8,9},{9,10... | collective-permute-start | bytes 1228808 | tf_op jit(solution)/shard_map/ppermute | solution.py:725
  6.8 12.9 %collective-permute-start.5 = (f32[57,8,128]{2,1,0:T(8,128)S(1)}, f32[57,8,128]{2,1,0:T(8,128)S(1)}, u32[]{:S(2)}, u32[]{:S(2)}) collective-permute-start(f32[57,8,128]{2,1,0:T(8,128)S(1)} %get-tuple-element.46), channel_id=1, source_target_pairs={{24,0},{0,8},{8,16},{16,24},{25,1},{1,9},{9,17},{17,25},{26,2},{2,... | collective-permute-start | bytes 700424 | tf_op jit(solution)/shard_map/ppermute | solution.py:725
  8.1 20.4 %collective-permute-start.6 = (f32[57,8,128]{2,1,0:T(8,128)S(1)}, f32[57,8,128]{2,1,0:T(8,128)S(1)}, u32[]{:S(2)}, u32[]{:S(2)}) collective-permute-start(f32[57,8,128]{2,1,0:T(8,128)S(1)} %get-tuple-element.47), channel_id=1, source_target_pairs={{16,0},{24,8},{0,16},{8,24},{17,1},{25,9},{1,17},{9,25},{18,2},{26... | collective-permute-start | bytes 700424 | tf_op jit(solution)/shard_map/ppermute | solution.py:725
  9.1 31.3 %collective-permute-start.7 = (f32[57,8,128]{2,1,0:T(8,128)S(1)}, f32[57,8,128]{2,1,0:T(8,128)S(1)}, u32[]{:S(2)}, u32[]{:S(2)}) collective-permute-start(f32[57,8,128]{2,1,0:T(8,128)S(1)} %get-tuple-element.48), channel_id=1, source_target_pairs={{8,0},{16,8},{24,16},{0,24},{9,1},{17,9},{25,17},{1,25},{10,2},{18... | collective-permute-start | bytes 700424 | tf_op jit(solution)/shard_map/ppermute | solution.py:725
  14.1 6.9 %copy-start = (f32[5,4,4,4,1,1280]{5,4,3,2,1,0:T(1,128)S(1)}, f32[5,4,4,4,1,1280]{5,4,3,2,1,0:T(1,128)}, u32[]{:S(2)}) copy-start(f32[5,4,4,4,1,1280]{5,4,3,2,1,0:T(1,128)} %param.3) | copy-start | bytes 4915204
  17.2 27.5 %collective-permute-start.2 = (f32[57,8,128]{2,1,0:T(8,128)S(1)}, f32[57,8,128]{2,1,0:T(8,128)S(1)}, u32[]{:S(2)}, u32[]{:S(2)}) collective-permute-start(f32[57,8,128]{2,1,0:T(8,128)S(1)} %get-tuple-element.41), channel_id=1, source_target_pairs={{24,0},{0,8},{8,16},{16,24},{25,1},{1,9},{9,17},{17,25},{26,2},{2,... | collective-permute-start | bytes 700424 | tf_op jit(solution)/shard_map/ppermute | solution.py:725
  18.6 29.9 %collective-permute-start.3 = (f32[57,8,128]{2,1,0:T(8,128)S(1)}, f32[57,8,128]{2,1,0:T(8,128)S(1)}, u32[]{:S(2)}, u32[]{:S(2)}) collective-permute-start(f32[57,8,128]{2,1,0:T(8,128)S(1)} %get-tuple-element.42), channel_id=1, source_target_pairs={{16,0},{24,8},{0,16},{8,24},{17,1},{25,9},{1,17},{9,25},{18,2},{26... | collective-permute-start | bytes 700424 | tf_op jit(solution)/shard_map/ppermute | solution.py:725
  19.6 30.8 %collective-permute-start.4 = (f32[57,8,128]{2,1,0:T(8,128)S(1)}, f32[57,8,128]{2,1,0:T(8,128)S(1)}, u32[]{:S(2)}, u32[]{:S(2)}) collective-permute-start(f32[57,8,128]{2,1,0:T(8,128)S(1)} %get-tuple-element.43), channel_id=1, source_target_pairs={{8,0},{16,8},{24,16},{0,24},{9,1},{17,9},{25,17},{1,25},{10,2},{18... | collective-permute-start | bytes 700424 | tf_op jit(solution)/shard_map/ppermute | solution.py:725
  21.0 19.4 %copy-start.1 = (f32[16]{0:T(128)S(1)}, f32[16]{0:T(128)}, u32[]{:S(2)}) copy-start(f32[16]{0:T(128)} %constant.7.clone.table_ref) | copy-start | bytes 196
  51.8 10.6 %collective-permute-start.9 = (f32[10,5,16,128]{3,2,1,0:T(8,128)S(1)}, f32[10,5,16,128]{3,2,1,0:T(8,128)S(1)}, u32[]{:S(2)}, u32[]{:S(2)}) collective-permute-start(f32[10,5,16,128]{3,2,1,0:T(8,128)S(1)} %get-tuple-element.50.u0), channel_id=1, source_target_pairs={{1,0},{2,1},{3,2},{4,3},{5,4},{6,5},{7,6},{0,7},{9,8},{10,9},{11,1... | collective-permute-start | bytes 1228808 | tf_op jit(solution)/shard_map/ppermute | solution.py:725
  52.3 10.3 %collective-permute-start.8 = (f32[10,5,16,128]{3,2,1,0:T(8,128)S(1)}, f32[10,5,16,128]{3,2,1,0:T(8,128)S(1)}, u32[]{:S(2)}, u32[]{:S(2)}) collective-permute-start(f32[10,5,16,128]{3,2,1,0:T(8,128)S(1)} %get-tuple-element.51.u3), channel_id=1, source_target_pairs={{7,0},{0,1},{1,2},{2,3},{3,4},{4,5},{5,6},{6,7},{15,8},{8,9},{9,10... | collective-permute-start | bytes 1228808 | tf_op jit(solution)/shard_map/ppermute | solution.py:725
  53.6 11.6 %collective-permute-start.13 = (f32[50,8,128]{2,1,0:T(8,128)S(1)}, f32[50,8,128]{2,1,0:T(8,128)S(1)}, u32[]{:S(2)}, u32[]{:S(2)}) collective-permute-start(f32[50,8,128]{2,1,0:T(8,128)S(1)} %get-tuple-element.58), channel_id=1, source_target_pairs={{24,0},{0,8},{8,16},{16,24},{25,1},{1,9},{9,17},{17,25},{26,2},{2,... | collective-permute-start | bytes 614408 | tf_op jit(solution)/shard_map/ppermute | solution.py:725
  53.6 18.2 %collective-permute-start.14 = (f32[50,8,128]{2,1,0:T(8,128)S(1)}, f32[50,8,128]{2,1,0:T(8,128)S(1)}, u32[]{:S(2)}, u32[]{:S(2)}) collective-permute-start(f32[50,8,128]{2,1,0:T(8,128)S(1)} %get-tuple-element.59), channel_id=1, source_target_pairs={{16,0},{24,8},{0,16},{8,24},{17,1},{25,9},{1,17},{9,25},{18,2},{26... | collective-permute-start | bytes 614408 | tf_op jit(solution)/shard_map/ppermute | solution.py:725
  54.7 27.3 %collective-permute-start.15 = (f32[50,8,128]{2,1,0:T(8,128)S(1)}, f32[50,8,128]{2,1,0:T(8,128)S(1)}, u32[]{:S(2)}, u32[]{:S(2)}) collective-permute-start(f32[50,8,128]{2,1,0:T(8,128)S(1)} %get-tuple-element.60), channel_id=1, source_target_pairs={{8,0},{16,8},{24,16},{0,24},{9,1},{17,9},{25,17},{1,25},{10,2},{18... | collective-permute-start | bytes 614408 | tf_op jit(solution)/shard_map/ppermute | solution.py:725
  63.9 21.0 %collective-permute-start.10 = (f32[50,8,128]{2,1,0:T(8,128)S(1)}, f32[50,8,128]{2,1,0:T(8,128)S(1)}, u32[]{:S(2)}, u32[]{:S(2)}) collective-permute-start(f32[50,8,128]{2,1,0:T(8,128)S(1)} %get-tuple-element.54), channel_id=1, source_target_pairs={{24,0},{0,8},{8,16},{16,24},{25,1},{1,9},{9,17},{17,25},{26,2},{2,... | collective-permute-start | bytes 614408 | tf_op jit(solution)/shard_map/ppermute | solution.py:725
  64.0 25.0 %collective-permute-start.11 = (f32[50,8,128]{2,1,0:T(8,128)S(1)}, f32[50,8,128]{2,1,0:T(8,128)S(1)}, u32[]{:S(2)}, u32[]{:S(2)}) collective-permute-start(f32[50,8,128]{2,1,0:T(8,128)S(1)} %get-tuple-element.55), channel_id=1, source_target_pairs={{16,0},{24,8},{0,16},{8,24},{17,1},{25,9},{1,17},{9,25},{18,2},{26... | collective-permute-start | bytes 614408 | tf_op jit(solution)/shard_map/ppermute | solution.py:725
  65.2 25.6 %collective-permute-start.12 = (f32[50,8,128]{2,1,0:T(8,128)S(1)}, f32[50,8,128]{2,1,0:T(8,128)S(1)}, u32[]{:S(2)}, u32[]{:S(2)}) collective-permute-start(f32[50,8,128]{2,1,0:T(8,128)S(1)} %get-tuple-element.56), channel_id=1, source_target_pairs={{8,0},{16,8},{24,16},{0,24},{9,1},{17,9},{25,17},{1,25},{10,2},{18... | collective-permute-start | bytes 614408 | tf_op jit(solution)/shard_map/ppermute | solution.py:725
